TPU v7x, 256 devices: a whole 4x4x8 slice. The times are simulated.
256 devices in a mesh: dp: 4 (over x), row: 4 (over z_lo), col: 16 (over y, z_hi, core).
Axes of the slice: x: 4, y: 4, z: 8 (z_hi: 2, z_lo: 4; z = z_hi * 4 + z_lo), core: 2. Of those that a mesh axis runs over, the one named last changes fastest.
Arguments:
- inputs: bfloat16 [2048, 8192], P(('dp', 'row'), 'col'), may hold values from -64 to 64
- grad_out: bfloat16 [2048, 4, 8192], P(('dp', 'col'), None, 'row')
- row_moment: float32 [8192], P('col'), may hold values from 0.01 to 1.5
- column_moment: float32 [32768], P(('dp', 'row')), may hold values from 0.05 to 0.5
Outputs:
- update: float32 [8192, 32768], P('col', ('dp', 'row'))
- row_state: float32 [8192], P('col')
- column_state: float32 [32768], P(('dp', 'row'))
- row_mean: float32 [], replicated
All inputs are finite; a program needn't handle non-finite values.
Results may differ from a plain program's by a relative error of at most 0.0004.
Values may be sent and summed in bfloat16 or wider, within the bound.
No kernel may reach another device: no remote copies, remote signals or barrier semaphores. Data moves between devices by JAX's collectives and lax.ppermute only.
A program may use at most 128 MiB of HBM per device.

v0:
```python
import jax
import jax.numpy as jnp
from jax import lax
from jax.sharding import PartitionSpec as P

D = 8192
FF = 32768


def per_device(inputs, grad_out, row_moment, column_moment):
    replica_inputs = lax.all_gather(inputs, "row", axis=0, tiled=True)
    replica_grads = lax.all_gather(grad_out, "col", axis=0, tiled=True)
    gradient = lax.psum_scatter(
        jnp.einsum(
            "td,tgf->gdf", replica_inputs, replica_grads, preferred_element_type=jnp.float32
        ),
        "dp",
        scatter_dimension=0,
        tiled=True,
    )[0]
    squares = gradient * gradient + 1e-30
    row_part = jnp.sum(squares, axis=1)
    column_part = jnp.sum(squares, axis=0)
    row_sums = lax.psum(row_part, ("dp", "row"))
    column_sums = lax.psum(column_part, "col")
    row_state = 0.8 * row_moment + 0.2 * row_sums / FF
    column_state = 0.8 * column_moment + 0.2 * column_sums / D
    row_mean = lax.psum(jnp.sum(row_state), "col") / D
    scaled_step = gradient / jnp.sqrt(row_state[:, None] * column_state[None, :] / row_mean)
    clip_total = lax.psum(jnp.sum(scaled_step * scaled_step), ("dp", "row", "col"))
    clip_ratio = jnp.sqrt(clip_total / (D * FF))
    update = scaled_step / jnp.maximum(1.0, clip_ratio)
    return (update, row_state, column_state, row_mean)


def solution(mesh):
    return jax.shard_map(
        per_device,
        mesh=mesh,
        in_specs=(
            P(("dp", "row"), "col"),
            P(("dp", "col"), None, "row"),
            P("col"),
            P(("dp", "row")),
        ),
        out_specs=(P("col", ("dp", "row")), P("col"), P(("dp", "row")), P()),
        check_vma=False,
    )
```

profile of v0, /device:TPU:1, one launch (start us, length us, event | category | flops | bytes accessed | tf_op | source)
XLA Modules:
  0.0 465.1 jit_solution(16100080248466929308)
XLA Ops:
  7.2 0.0 all-gather.2.cloned.1.call-start
  7.2 2.1 copy.8
  9.3 0.0 all-gather.2.cloned.1.call-update
  9.4 0.0 reduce-scatter.2.cloned.1.call-start
  9.4 16.5 %all_gather.7 = bf16[512,512]{1,0:T(8,128)(2,1)S(1)} all-gather(bf16[128,512]{1,0:T(8,128)(2,1)} %param.4), channel_id=1, replica_groups=mesh['dp'=4,'row'=4,'col'=16] {'row'}, dimensions={0}, use_global_device_ids=true | all-gather | bytes 655360 | tf_op jit(solution)/shard_map/all_gather | solution.py:11
  25.9 97.9 %all-gather.2.cloned.1.call-done = bf16[512,4,2048]{2,0,1:T(8,128)(2,1)} async-done(((bf16[32,4,2048]{2,0,1:T(8,128)(2,1)}), bf16[512,4,2048]{2,0,1:T(8,128)(2,1)}) %all-gather.2.cloned.1.call-update) | async-done | bytes 8388624 | tf_op jit(solution)/shard_map/all_gather | solution.py:12
  123.8 11.8 %convolution_bitcast_fusion = f32[4,512,2048]{1,2,0:T(8,128)} fusion(bf16[512,4,2048]{2,0,1:T(8,128)(2,1)} %all-gather.2.cloned.1.call-done, bf16[512,512]{1,0:T(8,128)(2,1)S(1)} %all_gather.7), kind=kOutput, calls=%fused_computation | convolution fusion | flops 4294967296 | bytes 25690112 | tf_op jit(solution)/shard_map/td,tgf->gdf/dot_general | solution.py:14
  135.6 0.0 reduce-scatter.2.cloned.1.call-update
  135.6 0.0 copy-start.3
  135.6 0.0 copy-start.2
  135.6 144.8 %reduce-scatter.2.cloned.1.call-done = f32[1,512,2048]{1,2,0:T(8,128)} async-done(((f32[4,512,2048]{1,2,0:T(8,128)}), f32[1,512,2048]{1,2,0:T(8,128)}) %reduce-scatter.2.cloned.1.call-update) | async-done | bytes 4194320 | tf_op jit(solution)/shard_map/reduce_scatter | solution.py:13
  280.4 2.9 fusion.1
  283.3 34.8 %psum.28 = f32[512]{0:T(512)S(1)} all-reduce(f32[512]{0:T(512)S(1)} %get-tuple-element.9), channel_id=1, replica_groups=mesh['dp'=4,'row'=4,'col'=16] {'dp','row'}, use_global_device_ids=true, to_apply=%region_2.0 | all-reduce | flops 512 | bytes 4096 | tf_op jit(solution)/shard_map/psum | solution.py:24
  318.2 0.0 copy-done.3
  318.2 0.6 fusion.4
  318.8 51.4 %all-reduce = (f32[]{:T(128)}, f32[2048]{0:T(1024)S(1)}) all-reduce(f32[]{:T(128)} %get-tuple-element.12, f32[2048]{0:T(1024)S(1)} %get-tuple-element.8), channel_id=1, replica_groups=mesh['dp'=4,'row'=4,'col'=16] {'col'}, use_global_device_ids=true, to_apply=%region_6.0 | all-reduce | flops 2049 | bytes 16392 | tf_op jit(solution)/shard_map/psum | solution.py:28
  370.9 0.0 copy-done.2
  370.9 0.0 copy-start
  370.9 3.8 multiply_reduce_fusion
  374.7 72.4 %psum.31 = f32[]{:T(128)} all-reduce(f32[]{:T(128)} %multiply_reduce_fusion), channel_id=1, replica_groups=mesh['dp'=4,'row'=4,'col'=16] {'dp','row','col'}, use_global_device_ids=true, to_apply=%region_8.0 | all-reduce | flops 1 | bytes 8 | tf_op jit(solution)/shard_map/psum | solution.py:30
  447.9 3.9 broadcast_divide_fusion
  451.8 0.0 copy-done.1
  451.8 0.0 copy-done
  451.8 5.3 %copy.9 = f32[512,2048]{1,0:T(8,128)} copy(f32[512,2048]{0,1:T(8,128)} %broadcast_divide_fusion) | data formatting | bytes 8388608
  (2 shorter events, 0.0 us)
Async XLA Ops:
  7.2 116.7 %all-gather.2.cloned.1.call-start = ((), (), s32[]{:S(2)}) async-start(), calls=%async_computation.1 | async-start | bytes 8912896 | tf_op jit(solution)/shard_map/all_gather | solution.py:12
  9.4 271.1 %reduce-scatter.2.cloned.1.call-start = ((), (), s32[]{:S(2)}) async-start(), calls=%async_computation.2 | async-start | bytes 20971520 | tf_op jit(solution)/shard_map/reduce_scatter | solution.py:13
  135.6 182.5 %copy-start.3 = (f32[512]{0:T(512)S(1)}, f32[512]{0:T(512)}, u32[]{:S(2)}) copy-start(f32[512]{0:T(512)} %param.6) | copy-start | bytes 6148
  135.6 235.2 %copy-start.2 = (f32[2048]{0:T(1024)S(1)}, f32[2048]{0:T(1024)}, u32[]{:S(2)}) copy-start(f32[2048]{0:T(1024)} %param.7) | copy-start | bytes 24580
  318.8 133.0 %copy-start.1 = (f32[512]{0:T(512)}, f32[512]{0:T(512)S(1)}, u32[]{:S(2)}) copy-start(f32[512]{0:T(512)S(1)} %get-tuple-element.13) | copy-start | bytes 6148
  370.9 80.9 %copy-start = (f32[2048]{0:T(1024)}, f32[2048]{0:T(1024)S(1)}, u32[]{:S(2)}) copy-start(f32[2048]{0:T(1024)S(1)} %multiply_add_fusion) | copy-start | bytes 24580
Sparse Core Ops, SparseCore 0:
  11.3 112.4 all-gather.1
  135.7 144.6 reduce-scatter.1
where the time goes:
time: 466 us; the launch traced here: 465 us
  waiting for transfers between devices  243 us (52%)
  blocking collectives  175 us (38%)
  between operations  16.6 us (4%)
  matrix products  11.8 us (3%)
  other arithmetic  11.3 us (2%)
  local copies, waits for them, and re-layouts  7.49 us (2%)
    reduce_scatter x1, waiting for transfers between devices, per_device(): lax.psum_scatter(jnp.einsum('td,tgf->gdf', replica_inputs, replica_grads,...  145 us
    all_gather x1, waiting for transfers between devices, per_device(): replica_grads = lax.all_gather(grad_out, 'col', axis=0, tiled=True)  97.9 us
    psum x1, blocking collectives, per_device(): lax.psum(jnp.sum(scaled_step * scaled_step), ('dp', 'row', 'col'))  72.4 us
    psum x1, blocking collectives, per_device(): row_mean = lax.psum(jnp.sum(row_state), 'col') / D  51.4 us
    psum x1, blocking collectives, per_device(): row_sums = lax.psum(row_part, ('dp', 'row'))  34.8 us
    all_gather x1, blocking collectives, per_device(): replica_inputs = lax.all_gather(inputs, 'row', axis=0, tiled=True)  16.5 us
    dot_general x1, matrix products, per_device(): jnp.einsum('td,tgf->gdf', replica_inputs, replica_grads, preferred_elemen...  11.8 us
  transfers between devices with their start and end apart: 2, of which 2 were waited for; matrix products, arithmetic and copies ran while one was open for 0% of the time, Pallas kernels for 0%

commit v1 on v0

v1 whole, which is shorter than its diff:
```python
import jax
import jax.numpy as jnp
from jax import lax
from jax.experimental import pallas as pl
from jax.experimental.pallas import tpu as pltpu
from jax.sharding import PartitionSpec as P

D = 8192
FF = 32768
VMEM_LIMIT = 24 * 1024 * 1024
COLS = 512
ORDER = [(s, t) for t in (0, 1, 3, 2) for s in range(4)]


def arrange_kernel(at_ref, x0_ref, x1_ref, x2a_ref, x2b_ref, x3_ref, near_ref, far_ref, x2_ref):
    half = x2a_ref.shape[0]
    x2_ref[0:half, :] = x2a_ref[...]
    x2_ref[half:, :] = x2b_ref[...]
    pieces = (x0_ref, x1_ref, x2_ref, x3_ref)

    def put(out_ref, column, offset, blocks):
        rows = []
        for s, t in blocks:
            start = pl.multiple_of(at_ref[t] + offset, 32)
            rows.append(pieces[s][pl.ds(start, 32), :])
        out_ref[:, column : column + 128] = jnp.concatenate(rows, axis=0).T

    for other in (0, 1):
        near = at_ref[4] + at_ref[6 + other]
        far = at_ref[5] + at_ref[6 + other]
        for k in range(4):
            blocks = ORDER[4 * k : 4 * k + 4]
            put(near_ref, other * 512 + k * 128, near, blocks)
            put(far_ref, other * 512 + k * 128, far, blocks)


def arrange(at, pieces):
    whole = pl.BlockSpec(memory_space=pltpu.VMEM)
    return pl.pallas_call(
        arrange_kernel,
        in_specs=[pl.BlockSpec(memory_space=pltpu.SMEM)] + [whole] * 5,
        out_specs=[whole] * 2,
        out_shape=[jax.ShapeDtypeStruct((512, 1024), jnp.bfloat16)] * 2,
        scratch_shapes=[pltpu.VMEM((512, 512), jnp.bfloat16)],
        compiler_params=PARAMS,
        cost_estimate=pl.CostEstimate(flops=0, bytes_accessed=4 << 20, transcendentals=0),
    )(at, *pieces)


def near_kernel(x_ref, own_ref, other_ref, out_ref):
    out_ref[...] = jnp.dot(
        x_ref[:, 0:512], own_ref[...], preferred_element_type=jnp.float32
    ) + jnp.dot(x_ref[:, 512:1024], other_ref[...], preferred_element_type=jnp.float32)


def across(value):
    part = value[:, 0:128]
    for k in range(1, COLS // 128):
        part = part + value[:, k * 128 : (k + 1) * 128]
    return part


def gather_rows(step, part, acc_ref, row_ref):
    @pl.when(step == 0)
    def _():
        acc_ref[...] = part

    @pl.when(step > 0)
    def _():
        acc_ref[...] += part

    @pl.when(step == pl.num_programs(0) - 1)
    def _():
        row_ref[...] = jnp.sum(acc_ref[...].T, axis=0, keepdims=True)


def far_kernel(
    x_ref, own_ref, own_last_ref, other_ref, other_last_ref, near_ref,
    out_ref, col_ref, row_ref, acc_ref,
):
    value = near_ref[...]
    own = jnp.concatenate([own_ref[...], own_last_ref[...]], axis=0)
    value += jnp.dot(x_ref[:, 0:512], own, preferred_element_type=jnp.float32)
    other = jnp.concatenate([other_ref[...], other_last_ref[...]], axis=0)
    value += jnp.dot(x_ref[:, 512:1024], other, preferred_element_type=jnp.float32)
    out_ref[...] = value
    squares = value * value + 1e-30
    col_ref[...] = jnp.sum(squares, axis=0, keepdims=True)
    gather_rows(pl.program_id(0), across(squares), acc_ref, row_ref)


def fixed(*shape):
    return pl.BlockSpec(shape, lambda j: (0, 0))


def moving(rows):
    return pl.BlockSpec((rows, COLS), lambda j: (0, j))


G_SPEC = moving(512)
PARAMS = pltpu.CompilerParams(vmem_limit_bytes=VMEM_LIMIT)
COST = pl.CostEstimate(flops=2 * 512 * 1024 * 2048, bytes_accessed=9 << 20, transcendentals=0)


def near_product(x, own, other):
    return pl.pallas_call(
        near_kernel,
        grid=(2048 // COLS,),
        in_specs=[fixed(512, 1024), moving(512), moving(512)],
        out_specs=G_SPEC,
        out_shape=jax.ShapeDtypeStruct((512, 2048), jnp.float32),
        compiler_params=PARAMS,
        cost_estimate=COST,
    )(x, own, other)


def far_product(x, own, own_last, other, other_last, near):
    return pl.pallas_call(
        far_kernel,
        grid=(2048 // COLS,),
        in_specs=[fixed(512, 1024), moving(384), moving(128), moving(384), moving(128), G_SPEC],
        out_specs=[G_SPEC, moving(1), fixed(1, 512)],
        out_shape=[
            jax.ShapeDtypeStruct((512, 2048), jnp.float32),
            jax.ShapeDtypeStruct((1, 2048), jnp.float32),
            jax.ShapeDtypeStruct((1, 512), jnp.float32),
        ],
        scratch_shapes=[pltpu.VMEM((512, 128), jnp.float32)],
        compiler_params=PARAMS,
        cost_estimate=COST,
    )(x, own, own_last, other, other_last, near)


def weigh_kernel(g_ref, moment_ref, sums_ref, row_ref, state_ref, out_ref, acc_ref, weighed_ref):
    step = pl.program_id(0)
    state = 0.8 * moment_ref[...] + 0.2 * sums_ref[...] / D
    state_ref[...] = state
    scaled = g_ref[...] * lax.rsqrt(state)
    gather_rows(step, across(scaled * scaled), acc_ref, weighed_ref)

    @pl.when(step == pl.num_programs(0) - 1)
    def _():
        out_ref[0:1, :] = row_ref[...]
        out_ref[1:2, :] = weighed_ref[...]


def weigh(g, column_moment, column_sums, row_part):
    return pl.pallas_call(
        weigh_kernel,
        grid=(2048 // COLS,),
        in_specs=[G_SPEC, moving(1), moving(1), fixed(1, 512)],
        out_specs=[moving(1), fixed(2, 512)],
        out_shape=[
            jax.ShapeDtypeStruct((1, 2048), jnp.float32),
            jax.ShapeDtypeStruct((2, 512), jnp.float32),
        ],
        scratch_shapes=[
            pltpu.VMEM((512, 128), jnp.float32),
            pltpu.VMEM((1, 512), jnp.float32),
        ],
        compiler_params=PARAMS,
        cost_estimate=pl.CostEstimate(
            flops=4 * 512 * 2048, bytes_accessed=4 << 20, transcendentals=0
        ),
    )(g, column_moment, column_sums, row_part)


def totals_kernel(moment_ref, sums_ref, state_ref, total_ref):
    state = 0.8 * moment_ref[...] + 0.2 * sums_ref[0:1, :] / FF
    state_ref[...] = state
    squares = jnp.sum(sums_ref[1:2, :] / state)
    lane = lax.broadcasted_iota(jnp.int32, (1, 128), 1)
    total_ref[...] = jnp.where(lane == 0, squares, jnp.where(lane == 1, jnp.sum(state), 0.0))


def totals_of(row_moment, sums):
    return pl.pallas_call(
        totals_kernel,
        out_shape=[
            jax.ShapeDtypeStruct((1, 512), jnp.float32),
            jax.ShapeDtypeStruct((1, 128), jnp.float32),
        ],
        compiler_params=PARAMS,
        cost_estimate=pl.CostEstimate(flops=2048, bytes_accessed=8192, transcendentals=0),
    )(row_moment, sums)


def clip_kernel(g_ref, row_ref, col_ref, totals_ref, out_ref, mean_ref, rows_ref):
    @pl.when(pl.program_id(0) == 0)
    def _():
        rows_ref[...] = jnp.broadcast_to(lax.rsqrt(row_ref[...]), (128, 512)).T

    lane = lax.broadcasted_iota(jnp.int32, (1, 128), 1)
    totals = totals_ref[...]
    total = jnp.sum(jnp.where(lane == 0, totals, 0.0), axis=1, keepdims=True)
    row_mean = jnp.sum(jnp.where(lane == 1, totals, 0.0), axis=1, keepdims=True) / D
    mean_ref[...] = row_mean
    clip_ratio = jnp.sqrt(row_mean * total / (D * FF))
    factor = jnp.sqrt(row_mean) / jnp.maximum(1.0, clip_ratio)
    columns = lax.rsqrt(col_ref[...]) * factor
    rows = rows_ref[...]
    for k in range(COLS // 128):
        piece = slice(k * 128, (k + 1) * 128)
        out_ref[:, piece] = g_ref[:, piece] * rows * columns[:, piece]


def clip(g, row_state, column_state, totals):
    return pl.pallas_call(
        clip_kernel,
        grid=(2048 // COLS,),
        in_specs=[G_SPEC, fixed(1, 512), moving(1), fixed(1, 128)],
        out_specs=[G_SPEC, fixed(1, 1)],
        out_shape=[
            jax.ShapeDtypeStruct((512, 2048), jnp.float32),
            jax.ShapeDtypeStruct((1, 1), jnp.float32),
        ],
        scratch_shapes=[pltpu.VMEM((512, 128), jnp.float32)],
        compiler_params=PARAMS,
        cost_estimate=pl.CostEstimate(
            flops=2 * 512 * 2048, bytes_accessed=8 << 20, transcendentals=0
        ),
    )(g, row_state, column_state, totals)


def cyclic(size, stride, shift):
    total = size * stride
    return [(j, (j + shift * stride) % total) for j in range(total)]


def flipped(total, mask):
    return [(j, j ^ mask) for j in range(total)]


def swap_cores(value):
    return lax.ppermute(value, "col", flipped(16, 1))


def move_x(value, shift):
    return lax.ppermute(value, "dp", cyclic(4, 1, shift % 4))


def move_y(value, shift):
    return lax.ppermute(value, "col", cyclic(4, 4, shift % 4))


def swap_row(value, mask):
    return lax.ppermute(value, "row", flipped(4, mask))


def swap_z(value):
    return lax.ppermute(value, "col", flipped(16, 2))


def over(value, axis, masks):
    size = 16 if axis == "col" else 4
    for mask in masks:
        value = value + lax.ppermute(value, axis, flipped(size, mask))
    return value


def over_col(value):
    return over(value, "col", (1, 4, 8, 2))


def over_dp_row(value):
    return over(over(value, "dp", (1, 2)), "row", (1, 2))


def per_device(inputs, grad_out, row_moment, column_moment):
    me = lax.axis_index("dp")
    low = lax.axis_index("row")
    col = lax.axis_index("col")
    y, high, core = col // 4, col // 2 % 2, col % 2
    starts = [(low ^ ((y - t) % 4)) * 128 for t in range(4)]
    starts += [high * 64, (1 - high) * 64, core * 32, (1 - core) * 32]
    at = jnp.stack(starts).astype(jnp.int32)
    stage = lax.optimization_barrier

    pair = jnp.concatenate([inputs, swap_row(inputs, 1)])
    x0 = jnp.concatenate([pair, swap_row(pair, 2)])
    by_group = stage(jnp.transpose(grad_out, (1, 0, 2)))
    groups = [
        lax.dynamic_index_in_dim(by_group, (me + s) % 4, 0, keepdims=False) for s in range(4)
    ]
    blocks = [groups[0]] + [move_x(groups[s], s) for s in (1, 2, 3)]
    near, x0 = stage((jnp.concatenate(blocks), x0))

    far = swap_z(near)
    near1, near3 = move_y(near, 1), move_y(near, -1)
    near1, near3, x0 = stage((near1, near3, x0))

    near2a, near2b = move_y(near1[0:64], 1), move_y(near3[64:128], -1)
    x1, x3 = move_x(x0, 1), move_x(x0, -1)
    near2a, near2b, far, x1, x3 = stage((near2a, near2b, far, x1, x3))

    far1, far3 = move_y(far, 1), move_y(far, -1)
    own = jnp.concatenate([near, near1, near3, near2a, near2b])
    other = swap_cores(own)
    x2a, x2b = move_x(x1[0:256], 1), move_x(x3[256:512], -1)
    far1, far3, other, x2a, x2b = stage((far1, far3, other, x2a, x2b))

    far2a, far2b = move_y(far1[0:64], 1), move_y(far3[64:128], -1)
    far_own = jnp.concatenate([far, far1, far3])
    far_other = swap_cores(far_own)
    x_near, x_far = arrange(at, (x0, x1, x2a, x2b, x3))
    gradient = near_product(x_near, own, other)
    far2a, far2b, gradient = stage((far2a, far2b, gradient))

    far_last = jnp.concatenate([far2a, far2b])
    far_other_last = swap_cores(far_last)
    gradient, column_part, row_part = far_product(
        x_far, far_own, far_last, far_other, far_other_last, gradient
    )
    column_state, sums = weigh(
        gradient, column_moment[None], over_col(column_part), row_part
    )
    row_state, totals = totals_of(row_moment[None], over_dp_row(sums))
    update, row_mean = clip(gradient, row_state, column_state, over_col(totals))
    return (update, row_state[0], column_state[0], row_mean[0, 0])


def solution(mesh):
    return jax.shard_map(
        per_device,
        mesh=mesh,
        in_specs=(
            P(("dp", "row"), "col"),
            P(("dp", "col"), None, "row"),
            P("col"),
            P(("dp", "row")),
        ),
        out_specs=(P("col", ("dp", "row")), P("col"), P(("dp", "row")), P()),
        check_vma=False,
    )
```

time: 466 us -> 157 us (0.34)
  blocking collectives: 175 us -> 0 us
  waiting for transfers between devices: 243 us -> 70.8 us
  starting transfers between devices: 0.08 us -> 52.9 us
  Pallas kernels: 0 us -> 15.9 us
  between operations: 16.6 us -> 0.87 us
  matrix products: 11.8 us -> 0 us
  other arithmetic: 11.3 us -> 0.16 us
  local copies, waits for them, and re-layouts: 7.49 us -> 13.3 us
    psum x3 -> x0, blocking collectives: 159 us -> none  [the longest x1 72.4 us: per_device(): lax.psum(jnp.sum(scaled_step * scaled_step), ('dp', 'row', 'col'))]
    reduce_scatter x1 -> x0, waiting for transfers between devices: 145 us -> none  [per_device(): lax.psum_scatter(jnp.einsum('td,tgf->gdf', replica_inputs, replica_grads,...]
    all_gather x1 -> x0, waiting for transfers between devices: 97.9 us -> none  [per_device(): replica_grads = lax.all_gather(grad_out, 'col', axis=0, tiled=True)]
    ppermute x0 -> x33, waiting for transfers between devices: none -> 70.8 us  [the longest x12 26.2 us: over(): value = value + lax.ppermute(value, axis, flipped(size, mask))]
    ppermute x0 -> x33, starting transfers between devices: none -> 52.9 us  [the longest x12 22.3 us: over(): value = value + lax.ppermute(value, axis, flipped(size, mask))]
    all_gather x1 -> x0, blocking collectives: 16.5 us -> none  [per_device(): replica_inputs = lax.all_gather(inputs, 'row', axis=0, tiled=True)]
    pallas_call x0 -> x6, Pallas kernels: none -> 15.9 us  [the longest x1 5.13 us: far_product(): pl.pallas_call(far_kernel, grid=(2048 // COLS,), in_specs=[fixed(512, 102...]
    dot_general x1 -> x0, matrix products: 11.8 us -> none  [per_device(): jnp.einsum('td,tgf->gdf', replica_inputs, replica_grads, preferred_elemen...]
  transfers between devices with their start and end apart: 2 -> 33, of which waited for: 2 -> 25; matrix products, arithmetic and copies ran while one was open for 0% -> 4% of each run, Pallas kernels for 0% -> 3%
where the time goes in v1:
time: 157 us; the launch traced here: 154 us
  waiting for transfers between devices  70.8 us (45%)
  starting transfers between devices  52.9 us (34%)
  Pallas kernels  15.9 us (10%)
  local copies, waits for them, and re-layouts  13.3 us (8%)
    ppermute x12, waiting for transfers between devices, over(): value = value + lax.ppermute(value, axis, flipped(size, mask))  26.2 us
    ppermute x12, starting transfers between devices, over(): value = value + lax.ppermute(value, axis, flipped(size, mask))  22.3 us
    ppermute x7, waiting for transfers between devices, move_x(): return lax.ppermute(value, 'dp', cyclic(4, 1, shift % 4))  13.2 us
    ppermute x8, waiting for transfers between devices, move_y(): return lax.ppermute(value, 'col', cyclic(4, 4, shift % 4))  12.4 us
    ppermute x1, waiting for transfers between devices, swap_z(): return lax.ppermute(value, 'col', flipped(16, 2))  10.2 us
    unnamed x30, local copies, waits for them, and re-layouts  9.87 us
    ppermute x8, starting transfers between devices, move_y(): return lax.ppermute(value, 'col', cyclic(4, 4, shift % 4))  7.3 us
    ppermute x7, starting transfers between devices, move_x(): return lax.ppermute(value, 'dp', cyclic(4, 1, shift % 4))  7.3 us
  transfers between devices with their start and end apart: 33, of which 25 were waited for; matrix products, arithmetic and copies ran while one was open for 4% of the time, Pallas kernels for 3%

profile of v1, /device:TPU:1, one launch (start us, length us, event | category | flops | bytes accessed | tf_op | source)
XLA Modules:
  0.0 153.9 jit_solution(13200282625131586980)
XLA Ops:
  0.6 2.6 %collective-permute-start.3 = (bf16[128,512]{1,0:T(8,128)(2,1)}, bf16[128,512]{1,0:T(8,128)(2,1)S(1)}, u32[]{:S(2)}, u32[]{:S(2)}) collective-permute-start(bf16[128,512]{1,0:T(8,128)(2,1)} %param.4), channel_id=1, source_target_pairs={{0,16},{16,0},{32,48},{48,32},{1,17},{17,1},{33,49},{49,33},{2,18}... | collective-permute-start | bytes 393224 | tf_op jit(solution)/shard_map/ppermute | solution.py:247
  4.6 2.6 %collective-permute-start.2 = (bf16[32,2048]{1,0:T(8,128)(2,1)S(1)}, bf16[32,2048]{1,0:T(8,128)(2,1)S(1)}, u32[]{:S(2)}, u32[]{:S(2)}) collective-permute-start(bf16[32,2048]{1,0:T(8,128)(2,1)S(1)} %get-tuple-element.63), channel_id=1, source_target_pairs={{0,192},{64,0},{128,64},{192,128},{1,193},{65,1},{129,65},{193,129... | collective-permute-start | bytes 393224 | tf_op jit(solution)/shard_map/ppermute | solution.py:239
  8.3 3.1 %collective-permute-start.4 = (bf16[256,512]{1,0:T(8,128)(2,1)S(1)}, bf16[256,512]{1,0:T(8,128)(2,1)S(1)}, u32[]{:S(2)}, u32[]{:S(2)}) collective-permute-start(bf16[256,512]{1,0:T(8,128)(2,1)S(1)} %pad_maximum_fusion.2), channel_id=1, source_target_pairs={{0,32},{16,48},{32,0},{48,16},{1,33},{17,49},{33,1},{49,17},{2,34}... | collective-permute-start | bytes 786440 | tf_op jit(solution)/shard_map/ppermute | solution.py:247
  12.6 3.8 %collective-permute-done = bf16[32,2048]{1,0:T(8,128)(2,1)S(1)} collective-permute-done((bf16[32,2048]{1,0:T(8,128)(2,1)S(1)}, bf16[32,2048]{1,0:T(8,128)(2,1)S(1)}, u32[]{:S(2)}, u32[]{:S(2)}) %collective-permute-start) | collective-permute-done | bytes 131104 | tf_op jit(solution)/shard_map/ppermute | solution.py:239
  16.4 7.2 %collective-permute-done.4 = bf16[256,512]{1,0:T(8,128)(2,1)S(1)} collective-permute-done((bf16[256,512]{1,0:T(8,128)(2,1)S(1)}, bf16[256,512]{1,0:T(8,128)(2,1)S(1)}, u32[]{:S(2)}, u32[]{:S(2)}) %collective-permute-start.4) | collective-permute-done | bytes 262176 | tf_op jit(solution)/shard_map/ppermute | solution.py:247
  23.6 2.8 %collective-permute-start.6 = (bf16[128,2048]{1,0:T(8,128)(2,1)S(1)}, bf16[128,2048]{1,0:T(8,128)(2,1)S(1)}, u32[]{:S(2)}, u32[]{:S(2)}) collective-permute-start(bf16[128,2048]{1,0:T(8,128)(2,1)S(1)} %pad_maximum_fusion), channel_id=1, source_target_pairs={{0,12},{1,13},{2,14},{3,15},{4,0},{5,1},{6,2},{7,3},{8,4},{9,5},{1... | collective-permute-start | bytes 1572872 | tf_op jit(solution)/shard_map/ppermute | solution.py:243
  26.4 5.1 %collective-permute-start.9 = (bf16[128,2048]{1,0:T(8,128)(2,1)S(1)}, bf16[128,2048]{1,0:T(8,128)(2,1)S(1)}, u32[]{:S(2)}, u32[]{:S(2)}) collective-permute-start(bf16[128,2048]{1,0:T(8,128)(2,1)S(1)} %pad_maximum_fusion), channel_id=1, source_target_pairs={{0,2},{1,3},{2,0},{3,1},{4,6},{5,7},{6,4},{7,5},{8,10},{9,11},{10,... | collective-permute-start | bytes 1572872 | tf_op jit(solution)/shard_map/ppermute | solution.py:251
  31.5 5.7 %collective-permute-done.6 = bf16[128,2048]{1,0:T(8,128)(2,1)S(1)} collective-permute-done((bf16[128,2048]{1,0:T(8,128)(2,1)S(1)}, bf16[128,2048]{1,0:T(8,128)(2,1)S(1)}, u32[]{:S(2)}, u32[]{:S(2)}) %collective-permute-start.6) | collective-permute-done | bytes 524320 | tf_op jit(solution)/shard_map/ppermute | solution.py:243
  37.2 3.1 %collective-permute-done.5 = bf16[128,2048]{1,0:T(8,128)(2,1)S(1)} collective-permute-done((bf16[128,2048]{1,0:T(8,128)(2,1)S(1)}, bf16[128,2048]{1,0:T(8,128)(2,1)S(1)}, u32[]{:S(2)}, u32[]{:S(2)}) %collective-permute-start.5) | collective-permute-done | bytes 524320 | tf_op jit(solution)/shard_map/ppermute | solution.py:243
  44.1 10.2 %collective-permute-done.9 = bf16[128,2048]{1,0:T(8,128)(2,1)S(1)} collective-permute-done((bf16[128,2048]{1,0:T(8,128)(2,1)S(1)}, bf16[128,2048]{1,0:T(8,128)(2,1)S(1)}, u32[]{:S(2)}, u32[]{:S(2)}) %collective-permute-start.9) | collective-permute-done | bytes 524320 | tf_op jit(solution)/shard_map/ppermute | solution.py:251
  55.1 3.0 %collective-permute-start.14 = (bf16[512,2048]{1,0:T(8,128)(2,1)S(1)}, bf16[512,2048]{1,0:T(8,128)(2,1)S(1)}, u32[]{:S(2)}, u32[]{:S(2)}) collective-permute-start(bf16[512,2048]{1,0:T(8,128)(2,1)S(1)} %constant_dynamic-update-slice_fusion.own_ref), channel_id=1, source_target_pairs={{0,1},{1,0},{2,3},{3,2},{4,5},{5,4},{6,7},{7,6},{8,9},{9,8},{10,11... | collective-permute-start | bytes 6291464 | tf_op jit(solution)/shard_map/ppermute | solution.py:235
  62.0 4.9 %collective-permute-done.16.x2b_ref = bf16[256,512]{1,0:T(8,128)(2,1)S(1)} collective-permute-done((bf16[256,512]{1,0:T(8,128)(2,1)S(1)}, bf16[256,512]{1,0:T(8,128)(2,1)S(1)}, u32[]{:S(2)}, u32[]{:S(2)}) %collective-permute-start.16) | collective-permute-done | bytes 262176 | tf_op jit(solution)/shard_map/ppermute | solution.py:239
  66.9 2.7 %collective-permute-done.15.x2a_ref = bf16[256,512]{1,0:T(8,128)(2,1)S(1)} collective-permute-done((bf16[256,512]{1,0:T(8,128)(2,1)S(1)}, bf16[256,512]{1,0:T(8,128)(2,1)S(1)}, u32[]{:S(2)}, u32[]{:S(2)}) %collective-permute-start.15) | collective-permute-done | bytes 262176 | tf_op jit(solution)/shard_map/ppermute | solution.py:239
  84.1 3.5 %shard_map.76.near_ref = f32[512,2048]{1,0:T(8,128)S(1)} custom-call(bf16[512,1024]{1,0:T(8,128)(2,1)S(1)} %get-tuple-element.48.x_ref, bf16[512,2048]{1,0:T(8,128)(2,1)S(1)} %constant_dynamic-update-slice_fusion.own_ref, bf16[512,2048]{1,0:T(8,128)(2,1)S(1)} %copy-done.1), custom_call_target="tpu_custom_call" | custom-call | flops 2147483648 | bytes 9437184 | tf_op jit(solution)/shard_map/pallas_call | solution.py:106
  92.8 5.1 %shard_map.77 = (f32[512,2048]{1,0:T(8,128)S(1)}, f32[1,2048]{1,0:T(1,128)S(1)}, f32[1,512]{1,0:T(1,128)S(1)}) custom-call(bf16[512,1024]{1,0:T(8,128)(2,1)S(1)} %get-tuple-element.45.x_ref, bf16[384,2048]{1,0:T(8,128)(2,1)} %constant_dynamic-update-slice_fusion.5.own_ref, bf16[128,2048]{1,0:T(8,128)(2,1)S(1)} %constant_dynamic-update-slice_fusion.8.own_last_ref, ...), custom_call_target="tpu_custom_call" | custom-call | flops 2147483648 | bytes 9437184 | tf_op jit(solution)/shard_map/pallas_call | solution.py:118
  102.5 3.4 %collective-permute-done.23 = f32[1,2048]{1,0:T(1,128)S(1)} collective-permute-done((f32[1,2048]{1,0:T(1,128)S(1)}, f32[1,2048]{1,0:T(1,128)S(1)}, u32[]{:S(2)}, u32[]{:S(2)}) %collective-permute-start.23) | collective-permute-done | bytes 8224 | tf_op jit(solution)/shard_map/ppermute | solution.py:257
  105.9 4.1 %collective-permute-start.24 = (f32[1,2048]{1,0:T(1,128)S(1)}, f32[1,2048]{1,0:T(1,128)S(1)}, u32[]{:S(2)}, u32[]{:S(2)}) collective-permute-start(f32[1,2048]{1,0:T(1,128)S(1)} %add.113), channel_id=1, source_target_pairs={{0,2},{1,3},{2,0},{3,1},{4,6},{5,7},{6,4},{7,5},{8,10},{9,11},{10,... | collective-permute-start | bytes 24584 | tf_op jit(solution)/shard_map/ppermute | solution.py:257
  110.0 2.4 %collective-permute-done.24 = f32[1,2048]{1,0:T(1,128)S(1)} collective-permute-done((f32[1,2048]{1,0:T(1,128)S(1)}, f32[1,2048]{1,0:T(1,128)S(1)}, u32[]{:S(2)}, u32[]{:S(2)}) %collective-permute-start.24) | collective-permute-done | bytes 8224 | tf_op jit(solution)/shard_map/ppermute | solution.py:257
  121.1 2.5 %collective-permute-done.27 = f32[2,512]{1,0:T(2,128)S(1)} collective-permute-done((f32[2,512]{1,0:T(2,128)S(1)}, f32[2,512]{1,0:T(2,128)S(1)}, u32[]{:S(2)}, u32[]{:S(2)}) %collective-permute-start.27) | collective-permute-done | bytes 4128 | tf_op jit(solution)/shard_map/ppermute | solution.py:257
  123.8 3.2 %collective-permute-done.28 = f32[2,512]{1,0:T(2,128)S(1)} collective-permute-done((f32[2,512]{1,0:T(2,128)S(1)}, f32[2,512]{1,0:T(2,128)S(1)}, u32[]{:S(2)}, u32[]{:S(2)}) %collective-permute-start.28) | collective-permute-done | bytes 4128 | tf_op jit(solution)/shard_map/ppermute | solution.py:257
  127.6 8.3 %collective-permute-start.29 = (f32[1,128]{1,0:T(1,128)S(1)}, f32[1,128]{1,0:T(1,128)S(1)}, u32[]{:S(2)}, u32[]{:S(2)}) collective-permute-start(f32[1,128]{1,0:T(1,128)S(1)} %get-tuple-element.59), channel_id=1, source_target_pairs={{0,1},{1,0},{2,3},{3,2},{4,5},{5,4},{6,7},{7,6},{8,9},{9,8},{10,11... | collective-permute-start | bytes 1544 | tf_op jit(solution)/shard_map/ppermute | solution.py:257
  139.7 3.3 %collective-permute-done.31 = f32[1,128]{1,0:T(1,128)S(1)} collective-permute-done((f32[1,128]{1,0:T(1,128)S(1)}, f32[1,128]{1,0:T(1,128)S(1)}, u32[]{:S(2)}, u32[]{:S(2)}) %collective-permute-start.31) | collective-permute-done | bytes 544 | tf_op jit(solution)/shard_map/ppermute | solution.py:257
  143.0 4.0 %collective-permute-start.32 = (f32[1,128]{1,0:T(1,128)S(1)}, f32[1,128]{1,0:T(1,128)S(1)}, u32[]{:S(2)}, u32[]{:S(2)}) collective-permute-start(f32[1,128]{1,0:T(1,128)S(1)} %add.121), channel_id=1, source_target_pairs={{0,2},{1,3},{2,0},{3,1},{4,6},{5,7},{6,4},{7,5},{8,10},{9,11},{10,... | collective-permute-start | bytes 1544 | tf_op jit(solution)/shard_map/ppermute | solution.py:257
  150.7 3.2 %shard_map.80 = (f32[512,2048]{1,0:T(8,128)}, f32[1,1]{1,0:T(1,128)}) custom-call(f32[512,2048]{1,0:T(8,128)S(1)} %get-tuple-element.53.g_ref, f32[1,512]{1,0:T(1,128)S(1)} %copy-done.8, f32[1,2048]{1,0:T(1,128)S(1)} %copy-done.7, f32[1,128]{1,0:T(1,128)S(1)} %add.122.totals_ref), custom_call_target="tpu_custom_call" | custom-call | flops 2097152 | bytes 8388608 | tf_op jit(solution)/shard_map/pallas_call | solution.py:208
  (104 shorter events, 53.4 us)
Async XLA Ops:
  0.6 7.7 %collective-permute-start.3 = (bf16[128,512]{1,0:T(8,128)(2,1)}, bf16[128,512]{1,0:T(8,128)(2,1)S(1)}, u32[]{:S(2)}, u32[]{:S(2)}) collective-permute-start(bf16[128,512]{1,0:T(8,128)(2,1)} %param.4), channel_id=1, source_target_pairs={{0,16},{16,0},{32,48},{48,32},{1,17},{17,1},{33,49},{49,33},{2,18}... | collective-permute-start | bytes 393224 | tf_op jit(solution)/shard_map/ppermute | solution.py:247
  4.6 6.8 %collective-permute-start.2 = (bf16[32,2048]{1,0:T(8,128)(2,1)S(1)}, bf16[32,2048]{1,0:T(8,128)(2,1)S(1)}, u32[]{:S(2)}, u32[]{:S(2)}) collective-permute-start(bf16[32,2048]{1,0:T(8,128)(2,1)S(1)} %get-tuple-element.63), channel_id=1, source_target_pairs={{0,192},{64,0},{128,64},{192,128},{1,193},{65,1},{129,65},{193,129... | collective-permute-start | bytes 393224 | tf_op jit(solution)/shard_map/ppermute | solution.py:239
  7.2 5.4 %collective-permute-start.1 = (bf16[32,2048]{1,0:T(8,128)(2,1)S(1)}, bf16[32,2048]{1,0:T(8,128)(2,1)S(1)}, u32[]{:S(2)}, u32[]{:S(2)}) collective-permute-start(bf16[32,2048]{1,0:T(8,128)(2,1)S(1)} %get-tuple-element.64), channel_id=1, source_target_pairs={{0,128},{64,192},{128,0},{192,64},{1,129},{65,193},{129,1},{193,65... | collective-permute-start | bytes 393224 | tf_op jit(solution)/shard_map/ppermute | solution.py:239
  7.7 8.7 %collective-permute-start = (bf16[32,2048]{1,0:T(8,128)(2,1)S(1)}, bf16[32,2048]{1,0:T(8,128)(2,1)S(1)}, u32[]{:S(2)}, u32[]{:S(2)}) collective-permute-start(bf16[32,2048]{1,0:T(8,128)(2,1)S(1)} %get-tuple-element.65), channel_id=1, source_target_pairs={{0,64},{64,128},{128,192},{192,0},{1,65},{65,129},{129,193},{193,1... | collective-permute-start | bytes 393224 | tf_op jit(solution)/shard_map/ppermute | solution.py:239
  8.3 15.2 %collective-permute-start.4 = (bf16[256,512]{1,0:T(8,128)(2,1)S(1)}, bf16[256,512]{1,0:T(8,128)(2,1)S(1)}, u32[]{:S(2)}, u32[]{:S(2)}) collective-permute-start(bf16[256,512]{1,0:T(8,128)(2,1)S(1)} %pad_maximum_fusion.2), channel_id=1, source_target_pairs={{0,32},{16,48},{32,0},{48,16},{1,33},{17,49},{33,1},{49,17},{2,34}... | collective-permute-start | bytes 786440 | tf_op jit(solution)/shard_map/ppermute | solution.py:247
  23.6 13.6 %collective-permute-start.6 = (bf16[128,2048]{1,0:T(8,128)(2,1)S(1)}, bf16[128,2048]{1,0:T(8,128)(2,1)S(1)}, u32[]{:S(2)}, u32[]{:S(2)}) collective-permute-start(bf16[128,2048]{1,0:T(8,128)(2,1)S(1)} %pad_maximum_fusion), channel_id=1, source_target_pairs={{0,12},{1,13},{2,14},{3,15},{4,0},{5,1},{6,2},{7,3},{8,4},{9,5},{1... | collective-permute-start | bytes 1572872 | tf_op jit(solution)/shard_map/ppermute | solution.py:243
  26.4 13.9 %collective-permute-start.5 = (bf16[128,2048]{1,0:T(8,128)(2,1)S(1)}, bf16[128,2048]{1,0:T(8,128)(2,1)S(1)}, u32[]{:S(2)}, u32[]{:S(2)}) collective-permute-start(bf16[128,2048]{1,0:T(8,128)(2,1)S(1)} %pad_maximum_fusion), channel_id=1, source_target_pairs={{0,4},{1,5},{2,6},{3,7},{4,8},{5,9},{6,10},{7,11},{8,12},{9,13},{1... | collective-permute-start | bytes 1572872 | tf_op jit(solution)/shard_map/ppermute | solution.py:243
  26.4 27.9 %collective-permute-start.9 = (bf16[128,2048]{1,0:T(8,128)(2,1)S(1)}, bf16[128,2048]{1,0:T(8,128)(2,1)S(1)}, u32[]{:S(2)}, u32[]{:S(2)}) collective-permute-start(bf16[128,2048]{1,0:T(8,128)(2,1)S(1)} %pad_maximum_fusion), channel_id=1, source_target_pairs={{0,2},{1,3},{2,0},{3,1},{4,6},{5,7},{6,4},{7,5},{8,10},{9,11},{10,... | collective-permute-start | bytes 1572872 | tf_op jit(solution)/shard_map/ppermute | solution.py:251
  40.3 14.1 %collective-permute-start.11 = (bf16[512,512]{1,0:T(8,128)(2,1)S(1)}, bf16[512,512]{1,0:T(8,128)(2,1)S(1)}, u32[]{:S(2)}, u32[]{:S(2)}) collective-permute-start(bf16[512,512]{1,0:T(8,128)(2,1)S(1)} %pad_maximum_fusion.1.x0_ref), channel_id=1, source_target_pairs={{0,192},{64,0},{128,64},{192,128},{1,193},{65,1},{129,65},{193,129... | collective-permute-start | bytes 1572872 | tf_op jit(solution)/shard_map/ppermute | solution.py:239
  42.4 12.7 %collective-permute-start.10 = (bf16[512,512]{1,0:T(8,128)(2,1)S(1)}, bf16[512,512]{1,0:T(8,128)(2,1)S(1)}, u32[]{:S(2)}, u32[]{:S(2)}) collective-permute-start(bf16[512,512]{1,0:T(8,128)(2,1)S(1)} %pad_maximum_fusion.1.x0_ref), channel_id=1, source_target_pairs={{0,64},{64,128},{128,192},{192,0},{1,65},{65,129},{129,193},{193,1... | collective-permute-start | bytes 1572872 | tf_op jit(solution)/shard_map/ppermute | solution.py:239
  42.5 11.9 %collective-permute-start.8 = (bf16[64,2048]{1,0:T(8,128)(2,1)S(1)}, bf16[64,2048]{1,0:T(8,128)(2,1)S(1)}, u32[]{:S(2)}, u32[]{:S(2)}) collective-permute-start(bf16[64,2048]{1,0:T(8,128)(2,1)S(1)} %slice.19), channel_id=1, source_target_pairs={{0,12},{1,13},{2,14},{3,15},{4,0},{5,1},{6,2},{7,3},{8,4},{9,5},{1... | collective-permute-start | bytes 786440 | tf_op jit(solution)/shard_map/ppermute | solution.py:243
  42.9 11.5 %collective-permute-start.7 = (bf16[64,2048]{1,0:T(8,128)(2,1)S(1)}, bf16[64,2048]{1,0:T(8,128)(2,1)S(1)}, u32[]{:S(2)}, u32[]{:S(2)}) collective-permute-start(bf16[64,2048]{1,0:T(8,128)(2,1)S(1)} %slice.18), channel_id=1, source_target_pairs={{0,4},{1,5},{2,6},{3,7},{4,8},{5,9},{6,10},{7,11},{8,12},{9,13},{1... | collective-permute-start | bytes 786440 | tf_op jit(solution)/shard_map/ppermute | solution.py:243
  55.1 18.2 %collective-permute-start.14 = (bf16[512,2048]{1,0:T(8,128)(2,1)S(1)}, bf16[512,2048]{1,0:T(8,128)(2,1)S(1)}, u32[]{:S(2)}, u32[]{:S(2)}) collective-permute-start(bf16[512,2048]{1,0:T(8,128)(2,1)S(1)} %constant_dynamic-update-slice_fusion.own_ref), channel_id=1, source_target_pairs={{0,1},{1,0},{2,3},{3,2},{4,5},{5,4},{6,7},{7,6},{8,9},{9,8},{10,11... | collective-permute-start | bytes 6291464 | tf_op jit(solution)/shard_map/ppermute | solution.py:235
  58.1 13.5 %collective-permute-start.13 = (bf16[128,2048]{1,0:T(8,128)(2,1)S(1)}, bf16[128,2048]{1,0:T(8,128)(2,1)S(1)}, u32[]{:S(2)}, u32[]{:S(2)}) collective-permute-start(bf16[128,2048]{1,0:T(8,128)(2,1)S(1)} %collective-permute-done.9), channel_id=1, source_target_pairs={{0,12},{1,13},{2,14},{3,15},{4,0},{5,1},{6,2},{7,3},{8,4},{9,5},{1... | collective-permute-start | bytes 1572872 | tf_op jit(solution)/shard_map/ppermute | solution.py:243
  58.9 14.4 %collective-permute-start.12 = (bf16[128,2048]{1,0:T(8,128)(2,1)S(1)}, bf16[128,2048]{1,0:T(8,128)(2,1)S(1)}, u32[]{:S(2)}, u32[]{:S(2)}) collective-permute-start(bf16[128,2048]{1,0:T(8,128)(2,1)S(1)} %collective-permute-done.9), channel_id=1, source_target_pairs={{0,4},{1,5},{2,6},{3,7},{4,8},{5,9},{6,10},{7,11},{8,12},{9,13},{1... | collective-permute-start | bytes 1572872 | tf_op jit(solution)/shard_map/ppermute | solution.py:243
  59.6 7.3 %collective-permute-start.16 = (bf16[256,512]{1,0:T(8,128)(2,1)S(1)}, bf16[256,512]{1,0:T(8,128)(2,1)S(1)}, u32[]{:S(2)}, u32[]{:S(2)}) collective-permute-start(bf16[256,512]{1,0:T(8,128)(2,1)S(1)} %slice.21), channel_id=1, source_target_pairs={{0,192},{64,0},{128,64},{192,128},{1,193},{65,1},{129,65},{193,129... | collective-permute-start | bytes 786440 | tf_op jit(solution)/shard_map/ppermute | solution.py:239
  61.1 8.4 %collective-permute-start.15 = (bf16[256,512]{1,0:T(8,128)(2,1)S(1)}, bf16[256,512]{1,0:T(8,128)(2,1)S(1)}, u32[]{:S(2)}, u32[]{:S(2)}) collective-permute-start(bf16[256,512]{1,0:T(8,128)(2,1)S(1)} %slice.20), channel_id=1, source_target_pairs={{0,64},{64,128},{128,192},{192,0},{1,65},{65,129},{129,193},{193,1... | collective-permute-start | bytes 786440 | tf_op jit(solution)/shard_map/ppermute | solution.py:239
  76.3 16.5 %collective-permute-start.19 = (bf16[384,2048]{1,0:T(8,128)(2,1)}, bf16[384,2048]{1,0:T(8,128)(2,1)}, u32[]{:S(2)}, u32[]{:S(2)}) collective-permute-start(bf16[384,2048]{1,0:T(8,128)(2,1)} %constant_dynamic-update-slice_fusion.5.own_ref), channel_id=1, source_target_pairs={{0,1},{1,0},{2,3},{3,2},{4,5},{5,4},{6,7},{7,6},{8,9},{9,8},{10,11... | collective-permute-start | bytes 4718600 | tf_op jit(solution)/shard_map/ppermute | solution.py:235
  78.9 8.6 %collective-permute-start.18 = (bf16[64,2048]{1,0:T(8,128)(2,1)}, bf16[64,2048]{1,0:T(8,128)(2,1)}, u32[]{:S(2)}, u32[]{:S(2)}) collective-permute-start(bf16[64,2048]{1,0:T(8,128)(2,1)} %slice.23), channel_id=1, source_target_pairs={{0,12},{1,13},{2,14},{3,15},{4,0},{5,1},{6,2},{7,3},{8,4},{9,5},{1... | collective-permute-start | bytes 786440 | tf_op jit(solution)/shard_map/ppermute | solution.py:243
  78.9 9.1 %collective-permute-start.17 = (bf16[64,2048]{1,0:T(8,128)(2,1)}, bf16[64,2048]{1,0:T(8,128)(2,1)}, u32[]{:S(2)}, u32[]{:S(2)}) collective-permute-start(bf16[64,2048]{1,0:T(8,128)(2,1)} %slice.22), channel_id=1, source_target_pairs={{0,4},{1,5},{2,6},{3,7},{4,8},{5,9},{6,10},{7,11},{8,12},{9,13},{1... | collective-permute-start | bytes 786440 | tf_op jit(solution)/shard_map/ppermute | solution.py:243
  101.8 4.1 %collective-permute-start.23 = (f32[1,2048]{1,0:T(1,128)S(1)}, f32[1,2048]{1,0:T(1,128)S(1)}, u32[]{:S(2)}, u32[]{:S(2)}) collective-permute-start(f32[1,2048]{1,0:T(1,128)S(1)} %add.112), channel_id=1, source_target_pairs={{0,8},{1,9},{2,10},{3,11},{4,12},{5,13},{6,14},{7,15},{8,0},{9,1},... | collective-permute-start | bytes 24584 | tf_op jit(solution)/shard_map/ppermute | solution.py:257
  105.9 6.5 %collective-permute-start.24 = (f32[1,2048]{1,0:T(1,128)S(1)}, f32[1,2048]{1,0:T(1,128)S(1)}, u32[]{:S(2)}, u32[]{:S(2)}) collective-permute-start(f32[1,2048]{1,0:T(1,128)S(1)} %add.113), channel_id=1, source_target_pairs={{0,2},{1,3},{2,0},{3,1},{4,6},{5,7},{6,4},{7,5},{8,10},{9,11},{10,... | collective-permute-start | bytes 24584 | tf_op jit(solution)/shard_map/ppermute | solution.py:257
  127.6 9.1 %collective-permute-start.29 = (f32[1,128]{1,0:T(1,128)S(1)}, f32[1,128]{1,0:T(1,128)S(1)}, u32[]{:S(2)}, u32[]{:S(2)}) collective-permute-start(f32[1,128]{1,0:T(1,128)S(1)} %get-tuple-element.59), channel_id=1, source_target_pairs={{0,1},{1,0},{2,3},{3,2},{4,5},{5,4},{6,7},{7,6},{8,9},{9,8},{10,11... | collective-permute-start | bytes 1544 | tf_op jit(solution)/shard_map/ppermute | solution.py:257
  143.0 6.3 %collective-permute-start.32 = (f32[1,128]{1,0:T(1,128)S(1)}, f32[1,128]{1,0:T(1,128)S(1)}, u32[]{:S(2)}, u32[]{:S(2)}) collective-permute-start(f32[1,128]{1,0:T(1,128)S(1)} %add.121), channel_id=1, source_target_pairs={{0,2},{1,3},{2,0},{3,1},{4,6},{5,7},{6,4},{7,5},{8,10},{9,11},{10,... | collective-permute-start | bytes 1544 | tf_op jit(solution)/shard_map/ppermute | solution.py:257
  (20 other events, 94.5 us)

commit v2 on v1

--- a/solution.py
+++ b/solution.py
@@ -7,31 +7,27 @@
 
 D = 8192
 FF = 32768
-VMEM_LIMIT = 24 * 1024 * 1024
+VMEM_LIMIT = 18 * 1024 * 1024
 COLS = 512
-ORDER = [(s, t) for t in (0, 1, 3, 2) for s in range(4)]
-
-
-def arrange_kernel(at_ref, x0_ref, x1_ref, x2a_ref, x2b_ref, x3_ref, near_ref, far_ref, x2_ref):
+PLACES = (0, 1, 3, 2)
+FIRST = [(s, t, far) for t in PLACES for s, far in ((0, 0), (1, 0), (2, 0), (3, 0), (0, 1))]
+SECOND = [(s, t, 1) for t in PLACES for s in (1, 2, 3)]
+
+
+def arrange_kernel(at_ref, x0_ref, x1_ref, x2a_ref, x2b_ref, x3_ref, first_ref, second_ref, x2_ref):
     half = x2a_ref.shape[0]
     x2_ref[0:half, :] = x2a_ref[...]
     x2_ref[half:, :] = x2b_ref[...]
     pieces = (x0_ref, x1_ref, x2_ref, x3_ref)
 
-    def put(out_ref, column, offset, blocks):
-        rows = []
-        for s, t in blocks:
-            start = pl.multiple_of(at_ref[t] + offset, 32)
-            rows.append(pieces[s][pl.ds(start, 32), :])
-        out_ref[:, column : column + 128] = jnp.concatenate(rows, axis=0).T
-
-    for other in (0, 1):
-        near = at_ref[4] + at_ref[6 + other]
-        far = at_ref[5] + at_ref[6 + other]
-        for k in range(4):
-            blocks = ORDER[4 * k : 4 * k + 4]
-            put(near_ref, other * 512 + k * 128, near, blocks)
-            put(far_ref, other * 512 + k * 128, far, blocks)
+    for order, out_ref in ((FIRST, first_ref), (SECOND, second_ref)):
+        blocks = [block + (other,) for other in (0, 1) for block in order]
+        for k in range(len(blocks) // 4):
+            rows = []
+            for s, t, far, other in blocks[4 * k : 4 * k + 4]:
+                start = pl.multiple_of(at_ref[t] + at_ref[4 + far] + at_ref[6 + other], 32)
+                rows.append(pieces[s][pl.ds(start, 32), :])
+            out_ref[:, k * 128 : (k + 1) * 128] = jnp.concatenate(rows, axis=0).T
 
 
 def arrange(at, pieces):
@@ -40,17 +36,20 @@
         arrange_kernel,
         in_specs=[pl.BlockSpec(memory_space=pltpu.SMEM)] + [whole] * 5,
         out_specs=[whole] * 2,
-        out_shape=[jax.ShapeDtypeStruct((512, 1024), jnp.bfloat16)] * 2,
+        out_shape=[
+            jax.ShapeDtypeStruct((512, 1280), jnp.bfloat16),
+            jax.ShapeDtypeStruct((512, 768), jnp.bfloat16),
+        ],
         scratch_shapes=[pltpu.VMEM((512, 512), jnp.bfloat16)],
         compiler_params=PARAMS,
         cost_estimate=pl.CostEstimate(flops=0, bytes_accessed=4 << 20, transcendentals=0),
     )(at, *pieces)
 
 
-def near_kernel(x_ref, own_ref, other_ref, out_ref):
+def first_kernel(x_ref, own_ref, other_ref, out_ref):
     out_ref[...] = jnp.dot(
-        x_ref[:, 0:512], own_ref[...], preferred_element_type=jnp.float32
-    ) + jnp.dot(x_ref[:, 512:1024], other_ref[...], preferred_element_type=jnp.float32)
+        x_ref[:, 0:640], own_ref[...], preferred_element_type=jnp.float32
+    ) + jnp.dot(x_ref[:, 640:1280], other_ref[...], preferred_element_type=jnp.float32)
 
 
 def across(value):
@@ -74,15 +73,12 @@
         row_ref[...] = jnp.sum(acc_ref[...].T, axis=0, keepdims=True)
 
 
-def far_kernel(
-    x_ref, own_ref, own_last_ref, other_ref, other_last_ref, near_ref,
-    out_ref, col_ref, row_ref, acc_ref,
+def second_kernel(
+    x_ref, own_ref, other_ref, first_ref, out_ref, col_ref, row_ref, acc_ref
 ):
-    value = near_ref[...]
-    own = jnp.concatenate([own_ref[...], own_last_ref[...]], axis=0)
-    value += jnp.dot(x_ref[:, 0:512], own, preferred_element_type=jnp.float32)
-    other = jnp.concatenate([other_ref[...], other_last_ref[...]], axis=0)
-    value += jnp.dot(x_ref[:, 512:1024], other, preferred_element_type=jnp.float32)
+    value = first_ref[...]
+    value += jnp.dot(x_ref[:, 0:384], own_ref[...], preferred_element_type=jnp.float32)
+    value += jnp.dot(x_ref[:, 384:768], other_ref[...], preferred_element_type=jnp.float32)
     out_ref[...] = value
     squares = value * value + 1e-30
     col_ref[...] = jnp.sum(squares, axis=0, keepdims=True)
@@ -102,11 +98,11 @@
 COST = pl.CostEstimate(flops=2 * 512 * 1024 * 2048, bytes_accessed=9 << 20, transcendentals=0)
 
 
-def near_product(x, own, other):
-    return pl.pallas_call(
-        near_kernel,
+def first_product(x, own, other):
+    return pl.pallas_call(
+        first_kernel,
         grid=(2048 // COLS,),
-        in_specs=[fixed(512, 1024), moving(512), moving(512)],
+        in_specs=[fixed(512, 1280), moving(640), moving(640)],
         out_specs=G_SPEC,
         out_shape=jax.ShapeDtypeStruct((512, 2048), jnp.float32),
         compiler_params=PARAMS,
@@ -114,11 +110,11 @@
     )(x, own, other)
 
 
-def far_product(x, own, own_last, other, other_last, near):
-    return pl.pallas_call(
-        far_kernel,
+def second_product(x, own, other, first):
+    return pl.pallas_call(
+        second_kernel,
         grid=(2048 // COLS,),
-        in_specs=[fixed(512, 1024), moving(384), moving(128), moving(384), moving(128), G_SPEC],
+        in_specs=[fixed(512, 768), moving(384), moving(384), G_SPEC],
         out_specs=[G_SPEC, moving(1), fixed(1, 512)],
         out_shape=[
             jax.ShapeDtypeStruct((512, 2048), jnp.float32),
@@ -128,7 +124,7 @@
         scratch_shapes=[pltpu.VMEM((512, 128), jnp.float32)],
         compiler_params=PARAMS,
         cost_estimate=COST,
-    )(x, own, own_last, other, other_last, near)
+    )(x, own, other, first)
 
 
 def weigh_kernel(g_ref, moment_ref, sums_ref, row_ref, state_ref, out_ref, acc_ref, weighed_ref):
@@ -251,19 +247,20 @@
     return lax.ppermute(value, "col", flipped(16, 2))
 
 
-def over(value, axis, masks):
+def over(value, axis, stride):
     size = 16 if axis == "col" else 4
-    for mask in masks:
-        value = value + lax.ppermute(value, axis, flipped(size, mask))
-    return value
+    a, b, c = [
+        lax.ppermute(value, axis, flipped(size, mask * stride)) for mask in (2, 1, 3)
+    ]
+    return (value + b) + (a + c)
 
 
 def over_col(value):
-    return over(value, "col", (1, 4, 8, 2))
+    return over(over(value, "col", 1), "col", 4)
 
 
 def over_dp_row(value):
-    return over(over(value, "dp", (1, 2)), "row", (1, 2))
+    return over(over(value, "dp", 1), "row", 1)
 
 
 def per_device(inputs, grad_out, row_moment, column_moment):
@@ -277,39 +274,39 @@
     stage = lax.optimization_barrier
 
     pair = jnp.concatenate([inputs, swap_row(inputs, 1)])
-    x0 = jnp.concatenate([pair, swap_row(pair, 2)])
-    by_group = stage(jnp.transpose(grad_out, (1, 0, 2)))
+    by_group, pair = stage((jnp.transpose(grad_out, (1, 0, 2)), pair))
     groups = [
         lax.dynamic_index_in_dim(by_group, (me + s) % 4, 0, keepdims=False) for s in range(4)
     ]
-    blocks = [groups[0]] + [move_x(groups[s], s) for s in (1, 2, 3)]
-    near, x0 = stage((jnp.concatenate(blocks), x0))
-
-    far = swap_z(near)
-    near1, near3 = move_y(near, 1), move_y(near, -1)
-    near1, near3, x0 = stage((near1, near3, x0))
-
-    near2a, near2b = move_y(near1[0:64], 1), move_y(near3[64:128], -1)
+    far0 = swap_z(groups[0])
+    blocks = [move_x(groups[s], s) for s in (1, 2, 3)]
+    x0 = jnp.concatenate([pair, swap_row(pair, 2)])
+    first = jnp.concatenate([groups[0]] + blocks + [far0])
+    first, rest, x0 = stage((first, jnp.concatenate(blocks), x0))
+
+    far = swap_z(rest)
+    first1, first3 = move_y(first, 1), move_y(first, -1)
     x1, x3 = move_x(x0, 1), move_x(x0, -1)
-    near2a, near2b, far, x1, x3 = stage((near2a, near2b, far, x1, x3))
+    first1, first3, x1, x3 = stage((first1, first3, x1, x3))
+
+    first2a, first2b = move_y(first1[0:80], 1), move_y(first3[80:160], -1)
+    x2a, x2b = move_x(x1[0:256], 1), move_x(x3[256:512], -1)
+    first2a, first2b, far, x2a, x2b = stage((first2a, first2b, far, x2a, x2b))
 
     far1, far3 = move_y(far, 1), move_y(far, -1)
-    own = jnp.concatenate([near, near1, near3, near2a, near2b])
+    own = jnp.concatenate([first, first1, first3, first2a, first2b])
     other = swap_cores(own)
-    x2a, x2b = move_x(x1[0:256], 1), move_x(x3[256:512], -1)
-    far1, far3, other, x2a, x2b = stage((far1, far3, other, x2a, x2b))
-
-    far2a, far2b = move_y(far1[0:64], 1), move_y(far3[64:128], -1)
-    far_own = jnp.concatenate([far, far1, far3])
+    x_first, x_second = arrange(at, (x0, x1, x2a, x2b, x3))
+    far1, far3, other, x_first, x_second = stage((far1, far3, other, x_first, x_second))
+
+    far2a, far2b = move_y(far1[0:48], 1), move_y(far3[48:96], -1)
+    gradient = first_product(x_first, own, other)
+    far2a, far2b, gradient = stage((far2a, far2b, gradient))
+
+    far_own = jnp.concatenate([far, far1, far3, far2a, far2b])
     far_other = swap_cores(far_own)
-    x_near, x_far = arrange(at, (x0, x1, x2a, x2b, x3))
-    gradient = near_product(x_near, own, other)
-    far2a, far2b, gradient = stage((far2a, far2b, gradient))
-
-    far_last = jnp.concatenate([far2a, far2b])
-    far_other_last = swap_cores(far_last)
-    gradient, column_part, row_part = far_product(
-        x_far, far_own, far_last, far_other, far_other_last, gradient
+    gradient, column_part, row_part = second_product(
+        x_second, far_own, far_other, gradient
     )
     column_state, sums = weigh(
         gradient, column_moment[None], over_col(column_part), row_part

time: 157 us -> 162 us (1.032); the launches traced: 154 us -> 162 us
  starting transfers between devices: 52.9 us -> 71 us
  waiting for transfers between devices: 70.8 us -> 60 us
    ppermute x12 -> x18, starting transfers between devices: 22.3 us -> 32.6 us  [over(): lax.ppermute(value, axis, flipped(size, mask * stride))]
    ppermute x2, waiting for transfers between devices: 7.18 us -> 17.2 us  [swap_row(): return lax.ppermute(value, 'row', flipped(4, mask))]
    ppermute x8, waiting for transfers between devices: 12.4 us -> 4.87 us  [move_y(): return lax.ppermute(value, 'col', cyclic(4, 4, shift % 4))]
    ppermute x12 -> x18, waiting for transfers between devices: 26.2 us -> 19.7 us  [over(): lax.ppermute(value, axis, flipped(size, mask * stride))]
    ppermute x1 -> x2, waiting for transfers between devices: 10.2 us -> 4.97 us  [swap_z(): return lax.ppermute(value, 'col', flipped(16, 2))]
    ppermute x8, starting transfers between devices: 7.3 us -> 11.2 us  [move_y(): return lax.ppermute(value, 'col', cyclic(4, 4, shift % 4))]
    ppermute x7, starting transfers between devices: 7.3 us -> 11.1 us  [move_x(): return lax.ppermute(value, 'dp', cyclic(4, 1, shift % 4))]
    ppermute x1 -> x2, starting transfers between devices: 5.09 us -> 8.16 us  [swap_z(): return lax.ppermute(value, 'col', flipped(16, 2))]
  transfers between devices with their start and end apart: 33 -> 39, of which waited for: 25 -> 20; matrix products, arithmetic and copies ran while one was open for 4% -> 4% of each run, Pallas kernels for 3% -> 4%
where the time goes in v2:
time: 162 us
  starting transfers between devices  71 us (44%)
  waiting for transfers between devices  60 us (37%)
  Pallas kernels  16.7 us (10%)
  local copies, waits for them, and re-layouts  11.8 us (7%)
    ppermute x18, starting transfers between devices, over(): lax.ppermute(value, axis, flipped(size, mask * stride))  32.6 us
    ppermute x18, waiting for transfers between devices, over(): lax.ppermute(value, axis, flipped(size, mask * stride))  19.7 us
    ppermute x2, waiting for transfers between devices, swap_row(): return lax.ppermute(value, 'row', flipped(4, mask))  17.2 us
    ppermute x8, starting transfers between devices, move_y(): return lax.ppermute(value, 'col', cyclic(4, 4, shift % 4))  11.2 us
    ppermute x7, starting transfers between devices, move_x(): return lax.ppermute(value, 'dp', cyclic(4, 1, shift % 4))  11.1 us
    ppermute x7, waiting for transfers between devices, move_x(): return lax.ppermute(value, 'dp', cyclic(4, 1, shift % 4))  10.2 us
    unnamed x33, local copies, waits for them, and re-layouts  9.66 us
    ppermute x2, starting transfers between devices, swap_z(): return lax.ppermute(value, 'col', flipped(16, 2))  8.16 us
  transfers between devices with their start and end apart: 39, of which 20 were waited for; matrix products, arithmetic and copies ran while one was open for 4% of the time, Pallas kernels for 4%

profile of v2, /device:TPU:1, one launch (start us, length us, event | category | flops | bytes accessed | tf_op | source)
XLA Modules:
  0.0 161.5 jit_solution(12591775826267232020)
XLA Ops:
  0.6 2.6 %collective-permute-start = (bf16[128,512]{1,0:T(8,128)(2,1)}, bf16[128,512]{1,0:T(8,128)(2,1)S(1)}, u32[]{:S(2)}, u32[]{:S(2)}) collective-permute-start(bf16[128,512]{1,0:T(8,128)(2,1)} %param.4), channel_id=1, source_target_pairs={{0,16},{16,0},{32,48},{48,32},{1,17},{17,1},{33,49},{49,33},{2,18}... | collective-permute-start | bytes 393224 | tf_op jit(solution)/shard_map/ppermute | solution.py:243
  8.8 2.5 %collective-permute-start.2 = (bf16[32,2048]{1,0:T(8,128)(2,1)S(1)}, bf16[32,2048]{1,0:T(8,128)(2,1)S(1)}, u32[]{:S(2)}, u32[]{:S(2)}) collective-permute-start(bf16[32,2048]{1,0:T(8,128)(2,1)S(1)} %get-tuple-element.73), channel_id=1, source_target_pairs={{0,128},{64,192},{128,0},{192,64},{1,129},{65,193},{129,1},{193,65... | collective-permute-start | bytes 393224 | tf_op jit(solution)/shard_map/ppermute | solution.py:235
  12.4 6.6 %collective-permute-start.4 = (bf16[32,2048]{1,0:T(8,128)(2,1)S(1)}, bf16[32,2048]{1,0:T(8,128)(2,1)S(1)}, u32[]{:S(2)}, u32[]{:S(2)}) collective-permute-start(bf16[32,2048]{1,0:T(8,128)(2,1)S(1)} %get-tuple-element.71), channel_id=1, source_target_pairs={{0,2},{1,3},{2,0},{3,1},{4,6},{5,7},{6,4},{7,5},{8,10},{9,11},{10,... | collective-permute-start | bytes 393224 | tf_op jit(solution)/shard_map/ppermute | solution.py:247
  21.5 16.0 %collective-permute-done.5 = bf16[256,512]{1,0:T(8,128)(2,1)S(1)} collective-permute-done((bf16[256,512]{1,0:T(8,128)(2,1)S(1)}, bf16[256,512]{1,0:T(8,128)(2,1)S(1)}, u32[]{:S(2)}, u32[]{:S(2)}) %collective-permute-start.5) | collective-permute-done | bytes 262176 | tf_op jit(solution)/shard_map/ppermute | solution.py:243
  44.7 9.6 %collective-permute-done.8.x1_ref = bf16[512,512]{1,0:T(8,128)(2,1)S(1)} collective-permute-done((bf16[512,512]{1,0:T(8,128)(2,1)S(1)}, bf16[512,512]{1,0:T(8,128)(2,1)S(1)}, u32[]{:S(2)}, u32[]{:S(2)}) %collective-permute-start.8) | collective-permute-done | bytes 524320 | tf_op jit(solution)/shard_map/ppermute | solution.py:235
  58.2 2.4 %collective-permute-start.14 = (bf16[256,512]{1,0:T(8,128)(2,1)S(1)}, bf16[256,512]{1,0:T(8,128)(2,1)S(1)}, u32[]{:S(2)}, u32[]{:S(2)}) collective-permute-start(bf16[256,512]{1,0:T(8,128)(2,1)S(1)} %slice.21), channel_id=1, source_target_pairs={{0,192},{64,0},{128,64},{192,128},{1,193},{65,1},{129,65},{193,129... | collective-permute-start | bytes 786440 | tf_op jit(solution)/shard_map/ppermute | solution.py:235
  60.7 3.8 %collective-permute-done.12 = bf16[96,2048]{1,0:T(8,128)(2,1)} collective-permute-done((bf16[96,2048]{1,0:T(8,128)(2,1)S(1)}, bf16[96,2048]{1,0:T(8,128)(2,1)}, u32[]{:S(2)}, u32[]{:S(2)}) %collective-permute-start.12) | collective-permute-done | bytes 393248 | tf_op jit(solution)/shard_map/ppermute | solution.py:247
  65.9 2.6 %collective-permute-start.17 = (bf16[640,2048]{1,0:T(8,128)(2,1)S(1)}, bf16[640,2048]{1,0:T(8,128)(2,1)}, u32[]{:S(2)}, u32[]{:S(2)}) collective-permute-start(bf16[640,2048]{1,0:T(8,128)(2,1)S(1)} %constant_dynamic-update-slice_fusion.5.own_ref), channel_id=1, source_target_pairs={{0,1},{1,0},{2,3},{3,2},{4,5},{5,4},{6,7},{7,6},{8,9},{9,8},{10,11... | collective-permute-start | bytes 7864328 | tf_op jit(solution)/shard_map/ppermute | solution.py:231
  68.5 2.7 %collective-permute-start.16 = (bf16[96,2048]{1,0:T(8,128)(2,1)}, bf16[96,2048]{1,0:T(8,128)(2,1)}, u32[]{:S(2)}, u32[]{:S(2)}) collective-permute-start(bf16[96,2048]{1,0:T(8,128)(2,1)} %collective-permute-done.12), channel_id=1, source_target_pairs={{0,12},{1,13},{2,14},{3,15},{4,0},{5,1},{6,2},{7,3},{8,4},{9,5},{1... | collective-permute-start | bytes 1179656 | tf_op jit(solution)/shard_map/ppermute | solution.py:239
  76.5 4.3 %collective-permute-done.15 = bf16[96,2048]{1,0:T(8,128)(2,1)} collective-permute-done((bf16[96,2048]{1,0:T(8,128)(2,1)}, bf16[96,2048]{1,0:T(8,128)(2,1)}, u32[]{:S(2)}, u32[]{:S(2)}) %collective-permute-start.15) | collective-permute-done | bytes 393248 | tf_op jit(solution)/shard_map/ppermute | solution.py:239
  82.8 2.7 %collective-permute-start.19 = (bf16[48,2048]{1,0:T(8,128)(2,1)S(1)}, bf16[48,2048]{1,0:T(8,128)(2,1)S(1)}, u32[]{:S(2)}, u32[]{:S(2)}) collective-permute-start(bf16[48,2048]{1,0:T(8,128)(2,1)S(1)} %slice.23), channel_id=1, source_target_pairs={{0,12},{1,13},{2,14},{3,15},{4,0},{5,1},{6,2},{7,3},{8,4},{9,5},{1... | collective-permute-start | bytes 589832 | tf_op jit(solution)/shard_map/ppermute | solution.py:239
  87.6 5.5 %shard_map.76.first_ref = f32[512,2048]{1,0:T(8,128)S(1)} custom-call(bf16[512,1280]{1,0:T(8,128)(2,1)S(1)} %get-tuple-element.56.x_ref, bf16[640,2048]{1,0:T(8,128)(2,1)S(1)} %constant_dynamic-update-slice_fusion.5.own_ref, bf16[640,2048]{1,0:T(8,128)(2,1)} %collective-permute-done.17.other_ref), custom_call_target="tpu_custom_call" | custom-call | flops 2147483648 | bytes 9437184 | tf_op jit(solution)/shard_map/pallas_call | solution.py:102
  94.5 3.0 %collective-permute-done.20.other_ref = bf16[384,2048]{1,0:T(8,128)(2,1)S(1)} collective-permute-done((bf16[384,2048]{1,0:T(8,128)(2,1)S(1)}, bf16[384,2048]{1,0:T(8,128)(2,1)S(1)}, u32[]{:S(2)}, u32[]{:S(2)}) %collective-permute-start.20) | collective-permute-done | bytes 1572896 | tf_op jit(solution)/shard_map/ppermute | solution.py:231
  97.6 4.1 %shard_map.77 = (f32[512,2048]{1,0:T(8,128)S(1)}, f32[1,2048]{1,0:T(1,128)S(1)}, f32[1,512]{1,0:T(1,128)S(1)}) custom-call(bf16[512,768]{1,0:T(8,128)(2,1)S(1)} %get-tuple-element.53.x_ref, bf16[384,2048]{1,0:T(8,128)(2,1)S(1)} %constant_dynamic-update-slice_fusion.10.own_ref, bf16[384,2048]{1,0:T(8,128)(2,1)S(1)} %collective-permute-done.20.other_ref, ...), custom_call_target="tpu_custom_call" | custom-call | flops 2147483648 | bytes 9437184 | tf_op jit(solution)/shard_map/pallas_call | solution.py:114
  103.1 4.7 %collective-permute-start.23 = (f32[1,2048]{1,0:T(1,128)S(1)}, f32[1,2048]{1,0:T(1,128)S(1)}, u32[]{:S(2)}, u32[]{:S(2)}) collective-permute-start(f32[1,2048]{1,0:T(1,128)S(1)} %get-tuple-element.62), channel_id=1, source_target_pairs={{0,3},{1,2},{2,1},{3,0},{4,7},{5,6},{6,5},{7,4},{8,11},{9,10},{10,... | collective-permute-start | bytes 24584 | tf_op jit(solution)/shard_map/ppermute | solution.py:253
  110.3 2.6 %collective-permute-start.25 = (f32[1,2048]{1,0:T(1,128)S(1)}, f32[1,2048]{1,0:T(1,128)S(1)}, u32[]{:S(2)}, u32[]{:S(2)}) collective-permute-start(f32[1,2048]{1,0:T(1,128)S(1)} %add_add_fusion.1), channel_id=1, source_target_pairs={{0,8},{1,9},{2,10},{3,11},{4,12},{5,13},{6,14},{7,15},{8,0},{9,1},... | collective-permute-start | bytes 24584 | tf_op jit(solution)/shard_map/ppermute | solution.py:253
  119.7 3.3 %collective-permute-start.28 = (f32[2,512]{1,0:T(2,128)S(1)}, f32[2,512]{1,0:T(2,128)S(1)}, u32[]{:S(2)}, u32[]{:S(2)}) collective-permute-start(f32[2,512]{1,0:T(2,128)S(1)} %get-tuple-element.64), channel_id=1, source_target_pairs={{0,128},{64,192},{128,0},{192,64},{1,129},{65,193},{129,1},{193,65... | collective-permute-start | bytes 12296 | tf_op jit(solution)/shard_map/ppermute | solution.py:253
  124.1 2.9 %collective-permute-done.29 = f32[2,512]{1,0:T(2,128)S(1)} collective-permute-done((f32[2,512]{1,0:T(2,128)S(1)}, f32[2,512]{1,0:T(2,128)S(1)}, u32[]{:S(2)}, u32[]{:S(2)}) %collective-permute-start.29) | collective-permute-done | bytes 4128 | tf_op jit(solution)/shard_map/ppermute | solution.py:253
  130.6 2.8 %collective-permute-done.32 = f32[2,512]{1,0:T(2,128)S(1)} collective-permute-done((f32[2,512]{1,0:T(2,128)S(1)}, f32[2,512]{1,0:T(2,128)S(1)}, u32[]{:S(2)}, u32[]{:S(2)}) %collective-permute-start.32) | collective-permute-done | bytes 4128 | tf_op jit(solution)/shard_map/ppermute | solution.py:253
  134.0 5.3 %collective-permute-start.33 = (f32[1,128]{1,0:T(1,128)S(1)}, f32[1,128]{1,0:T(1,128)S(1)}, u32[]{:S(2)}, u32[]{:S(2)}) collective-permute-start(f32[1,128]{1,0:T(1,128)S(1)} %get-tuple-element.67), channel_id=1, source_target_pairs={{0,1},{1,0},{2,3},{3,2},{4,5},{5,4},{6,7},{7,6},{8,9},{9,8},{10,11... | collective-permute-start | bytes 1544 | tf_op jit(solution)/shard_map/ppermute | solution.py:253
  139.3 4.7 %collective-permute-start.34 = (f32[1,128]{1,0:T(1,128)S(1)}, f32[1,128]{1,0:T(1,128)S(1)}, u32[]{:S(2)}, u32[]{:S(2)}) collective-permute-start(f32[1,128]{1,0:T(1,128)S(1)} %get-tuple-element.67), channel_id=1, source_target_pairs={{0,2},{1,3},{2,0},{3,1},{4,6},{5,7},{6,4},{7,5},{8,10},{9,11},{10,... | collective-permute-start | bytes 1544 | tf_op jit(solution)/shard_map/ppermute | solution.py:253
  145.6 5.3 %collective-permute-done.35 = f32[1,128]{1,0:T(1,128)S(1)} collective-permute-done((f32[1,128]{1,0:T(1,128)S(1)}, f32[1,128]{1,0:T(1,128)S(1)}, u32[]{:S(2)}, u32[]{:S(2)}) %collective-permute-start.35) | collective-permute-done | bytes 544 | tf_op jit(solution)/shard_map/ppermute | solution.py:253
  151.0 2.4 %collective-permute-start.37 = (f32[1,128]{1,0:T(1,128)S(1)}, f32[1,128]{1,0:T(1,128)S(1)}, u32[]{:S(2)}, u32[]{:S(2)}) collective-permute-start(f32[1,128]{1,0:T(1,128)S(1)} %add_add_fusion.5), channel_id=1, source_target_pairs={{0,8},{1,9},{2,10},{3,11},{4,12},{5,13},{6,14},{7,15},{8,0},{9,1},... | collective-permute-start | bytes 1544 | tf_op jit(solution)/shard_map/ppermute | solution.py:253
  158.3 3.2 %shard_map.80 = (f32[512,2048]{1,0:T(8,128)}, f32[1,1]{1,0:T(1,128)}) custom-call(f32[512,2048]{1,0:T(8,128)S(1)} %get-tuple-element.61.g_ref, f32[1,512]{1,0:T(1,128)S(1)} %copy-done.8, f32[1,2048]{1,0:T(1,128)S(1)} %copy-done.7, f32[1,128]{1,0:T(1,128)S(1)} %add_add_fusion.4.totals_ref), custom_call_target="tpu_custom_call" | custom-call | flops 2097152 | bytes 8388608 | tf_op jit(solution)/shard_map/pallas_call | solution.py:204
  (113 shorter events, 54.9 us)
Async XLA Ops:
  6.7 13.5 %collective-permute-start.1 = (bf16[32,2048]{1,0:T(8,128)(2,1)S(1)}, bf16[32,2048]{1,0:T(8,128)(2,1)S(1)}, u32[]{:S(2)}, u32[]{:S(2)}) collective-permute-start(bf16[32,2048]{1,0:T(8,128)(2,1)S(1)} %get-tuple-element.74), channel_id=1, source_target_pairs={{0,64},{64,128},{128,192},{192,0},{1,65},{65,129},{129,193},{193,1... | collective-permute-start | bytes 393224 | tf_op jit(solution)/shard_map/ppermute | solution.py:235
  8.8 11.5 %collective-permute-start.2 = (bf16[32,2048]{1,0:T(8,128)(2,1)S(1)}, bf16[32,2048]{1,0:T(8,128)(2,1)S(1)}, u32[]{:S(2)}, u32[]{:S(2)}) collective-permute-start(bf16[32,2048]{1,0:T(8,128)(2,1)S(1)} %get-tuple-element.73), channel_id=1, source_target_pairs={{0,128},{64,192},{128,0},{192,64},{1,129},{65,193},{129,1},{193,65... | collective-permute-start | bytes 393224 | tf_op jit(solution)/shard_map/ppermute | solution.py:235
  11.2 9.0 %collective-permute-start.3 = (bf16[32,2048]{1,0:T(8,128)(2,1)S(1)}, bf16[32,2048]{1,0:T(8,128)(2,1)S(1)}, u32[]{:S(2)}, u32[]{:S(2)}) collective-permute-start(bf16[32,2048]{1,0:T(8,128)(2,1)S(1)} %get-tuple-element.72), channel_id=1, source_target_pairs={{0,192},{64,0},{128,64},{192,128},{1,193},{65,1},{129,65},{193,129... | collective-permute-start | bytes 393224 | tf_op jit(solution)/shard_map/ppermute | solution.py:235
  12.4 9.1 %collective-permute-start.4 = (bf16[32,2048]{1,0:T(8,128)(2,1)S(1)}, bf16[32,2048]{1,0:T(8,128)(2,1)S(1)}, u32[]{:S(2)}, u32[]{:S(2)}) collective-permute-start(bf16[32,2048]{1,0:T(8,128)(2,1)S(1)} %get-tuple-element.71), channel_id=1, source_target_pairs={{0,2},{1,3},{2,0},{3,1},{4,6},{5,7},{6,4},{7,5},{8,10},{9,11},{10,... | collective-permute-start | bytes 393224 | tf_op jit(solution)/shard_map/ppermute | solution.py:247
  19.0 18.5 %collective-permute-start.5 = (bf16[256,512]{1,0:T(8,128)(2,1)S(1)}, bf16[256,512]{1,0:T(8,128)(2,1)S(1)}, u32[]{:S(2)}, u32[]{:S(2)}) collective-permute-start(bf16[256,512]{1,0:T(8,128)(2,1)S(1)} %pad_maximum_fusion.2), channel_id=1, source_target_pairs={{0,32},{16,48},{32,0},{48,16},{1,33},{17,49},{33,1},{49,17},{2,34}... | collective-permute-start | bytes 786440 | tf_op jit(solution)/shard_map/ppermute | solution.py:243
  37.5 17.3 %collective-permute-start.6 = (bf16[160,2048]{1,0:T(8,128)(2,1)S(1)}, bf16[160,2048]{1,0:T(8,128)(2,1)S(1)}, u32[]{:S(2)}, u32[]{:S(2)}) collective-permute-start(bf16[160,2048]{1,0:T(8,128)(2,1)S(1)} %constant_dynamic-update-slice_fusion), channel_id=1, source_target_pairs={{0,4},{1,5},{2,6},{3,7},{4,8},{5,9},{6,10},{7,11},{8,12},{9,13},{1... | collective-permute-start | bytes 1966088 | tf_op jit(solution)/shard_map/ppermute | solution.py:239
  38.9 16.0 %collective-permute-start.7 = (bf16[160,2048]{1,0:T(8,128)(2,1)S(1)}, bf16[160,2048]{1,0:T(8,128)(2,1)S(1)}, u32[]{:S(2)}, u32[]{:S(2)}) collective-permute-start(bf16[160,2048]{1,0:T(8,128)(2,1)S(1)} %constant_dynamic-update-slice_fusion), channel_id=1, source_target_pairs={{0,12},{1,13},{2,14},{3,15},{4,0},{5,1},{6,2},{7,3},{8,4},{9,5},{1... | collective-permute-start | bytes 1966088 | tf_op jit(solution)/shard_map/ppermute | solution.py:239
  40.4 13.8 %collective-permute-start.8 = (bf16[512,512]{1,0:T(8,128)(2,1)S(1)}, bf16[512,512]{1,0:T(8,128)(2,1)S(1)}, u32[]{:S(2)}, u32[]{:S(2)}) collective-permute-start(bf16[512,512]{1,0:T(8,128)(2,1)S(1)} %pad_maximum_fusion.x0_ref), channel_id=1, source_target_pairs={{0,64},{64,128},{128,192},{192,0},{1,65},{65,129},{129,193},{193,1... | collective-permute-start | bytes 1572872 | tf_op jit(solution)/shard_map/ppermute | solution.py:235
  40.8 13.5 %collective-permute-start.9 = (bf16[512,512]{1,0:T(8,128)(2,1)S(1)}, bf16[512,512]{1,0:T(8,128)(2,1)S(1)}, u32[]{:S(2)}, u32[]{:S(2)}) collective-permute-start(bf16[512,512]{1,0:T(8,128)(2,1)S(1)} %pad_maximum_fusion.x0_ref), channel_id=1, source_target_pairs={{0,192},{64,0},{128,64},{192,128},{1,193},{65,1},{129,65},{193,129... | collective-permute-start | bytes 1572872 | tf_op jit(solution)/shard_map/ppermute | solution.py:235
  43.1 21.4 %collective-permute-start.12 = (bf16[96,2048]{1,0:T(8,128)(2,1)S(1)}, bf16[96,2048]{1,0:T(8,128)(2,1)}, u32[]{:S(2)}, u32[]{:S(2)}) collective-permute-start(bf16[96,2048]{1,0:T(8,128)(2,1)S(1)} %pad_maximum_fusion.1), channel_id=1, source_target_pairs={{0,2},{1,3},{2,0},{3,1},{4,6},{5,7},{6,4},{7,5},{8,10},{9,11},{10,... | collective-permute-start | bytes 1179656 | tf_op jit(solution)/shard_map/ppermute | solution.py:247
  54.9 10.2 %collective-permute-start.10 = (bf16[80,2048]{1,0:T(8,128)(2,1)S(1)}, bf16[80,2048]{1,0:T(8,128)(2,1)S(1)}, u32[]{:S(2)}, u32[]{:S(2)}) collective-permute-start(bf16[80,2048]{1,0:T(8,128)(2,1)S(1)} %slice.18), channel_id=1, source_target_pairs={{0,4},{1,5},{2,6},{3,7},{4,8},{5,9},{6,10},{7,11},{8,12},{9,13},{1... | collective-permute-start | bytes 983048 | tf_op jit(solution)/shard_map/ppermute | solution.py:239
  55.9 9.2 %collective-permute-start.11 = (bf16[80,2048]{1,0:T(8,128)(2,1)S(1)}, bf16[80,2048]{1,0:T(8,128)(2,1)S(1)}, u32[]{:S(2)}, u32[]{:S(2)}) collective-permute-start(bf16[80,2048]{1,0:T(8,128)(2,1)S(1)} %slice.19), channel_id=1, source_target_pairs={{0,12},{1,13},{2,14},{3,15},{4,0},{5,1},{6,2},{7,3},{8,4},{9,5},{1... | collective-permute-start | bytes 983048 | tf_op jit(solution)/shard_map/ppermute | solution.py:239
  57.8 7.4 %collective-permute-start.13 = (bf16[256,512]{1,0:T(8,128)(2,1)S(1)}, bf16[256,512]{1,0:T(8,128)(2,1)S(1)}, u32[]{:S(2)}, u32[]{:S(2)}) collective-permute-start(bf16[256,512]{1,0:T(8,128)(2,1)S(1)} %slice.20), channel_id=1, source_target_pairs={{0,64},{64,128},{128,192},{192,0},{1,65},{65,129},{129,193},{193,1... | collective-permute-start | bytes 786440 | tf_op jit(solution)/shard_map/ppermute | solution.py:235
  58.2 7.0 %collective-permute-start.14 = (bf16[256,512]{1,0:T(8,128)(2,1)S(1)}, bf16[256,512]{1,0:T(8,128)(2,1)S(1)}, u32[]{:S(2)}, u32[]{:S(2)}) collective-permute-start(bf16[256,512]{1,0:T(8,128)(2,1)S(1)} %slice.21), channel_id=1, source_target_pairs={{0,192},{64,0},{128,64},{192,128},{1,193},{65,1},{129,65},{193,129... | collective-permute-start | bytes 786440 | tf_op jit(solution)/shard_map/ppermute | solution.py:235
  65.9 14.9 %collective-permute-start.17 = (bf16[640,2048]{1,0:T(8,128)(2,1)S(1)}, bf16[640,2048]{1,0:T(8,128)(2,1)}, u32[]{:S(2)}, u32[]{:S(2)}) collective-permute-start(bf16[640,2048]{1,0:T(8,128)(2,1)S(1)} %constant_dynamic-update-slice_fusion.5.own_ref), channel_id=1, source_target_pairs={{0,1},{1,0},{2,3},{3,2},{4,5},{5,4},{6,7},{7,6},{8,9},{9,8},{10,11... | collective-permute-start | bytes 7864328 | tf_op jit(solution)/shard_map/ppermute | solution.py:231
  68.5 12.3 %collective-permute-start.15 = (bf16[96,2048]{1,0:T(8,128)(2,1)}, bf16[96,2048]{1,0:T(8,128)(2,1)}, u32[]{:S(2)}, u32[]{:S(2)}) collective-permute-start(bf16[96,2048]{1,0:T(8,128)(2,1)} %collective-permute-done.12), channel_id=1, source_target_pairs={{0,4},{1,5},{2,6},{3,7},{4,8},{5,9},{6,10},{7,11},{8,12},{9,13},{1... | collective-permute-start | bytes 1179656 | tf_op jit(solution)/shard_map/ppermute | solution.py:239
  68.5 12.3 %collective-permute-start.16 = (bf16[96,2048]{1,0:T(8,128)(2,1)}, bf16[96,2048]{1,0:T(8,128)(2,1)}, u32[]{:S(2)}, u32[]{:S(2)}) collective-permute-start(bf16[96,2048]{1,0:T(8,128)(2,1)} %collective-permute-done.12), channel_id=1, source_target_pairs={{0,12},{1,13},{2,14},{3,15},{4,0},{5,1},{6,2},{7,3},{8,4},{9,5},{1... | collective-permute-start | bytes 1179656 | tf_op jit(solution)/shard_map/ppermute | solution.py:239
  81.7 11.3 %collective-permute-start.18 = (bf16[48,2048]{1,0:T(8,128)(2,1)S(1)}, bf16[48,2048]{1,0:T(8,128)(2,1)S(1)}, u32[]{:S(2)}, u32[]{:S(2)}) collective-permute-start(bf16[48,2048]{1,0:T(8,128)(2,1)S(1)} %slice.22), channel_id=1, source_target_pairs={{0,4},{1,5},{2,6},{3,7},{4,8},{5,9},{6,10},{7,11},{8,12},{9,13},{1... | collective-permute-start | bytes 589832 | tf_op jit(solution)/shard_map/ppermute | solution.py:239
  82.8 10.3 %collective-permute-start.19 = (bf16[48,2048]{1,0:T(8,128)(2,1)S(1)}, bf16[48,2048]{1,0:T(8,128)(2,1)S(1)}, u32[]{:S(2)}, u32[]{:S(2)}) collective-permute-start(bf16[48,2048]{1,0:T(8,128)(2,1)S(1)} %slice.23), channel_id=1, source_target_pairs={{0,12},{1,13},{2,14},{3,15},{4,0},{5,1},{6,2},{7,3},{8,4},{9,5},{1... | collective-permute-start | bytes 589832 | tf_op jit(solution)/shard_map/ppermute | solution.py:239
  102.1 6.4 %collective-permute-start.22 = (f32[1,2048]{1,0:T(1,128)S(1)}, f32[1,2048]{1,0:T(1,128)S(1)}, u32[]{:S(2)}, u32[]{:S(2)}) collective-permute-start(f32[1,2048]{1,0:T(1,128)S(1)} %get-tuple-element.62), channel_id=1, source_target_pairs={{0,2},{1,3},{2,0},{3,1},{4,6},{5,7},{6,4},{7,5},{8,10},{9,11},{10,... | collective-permute-start | bytes 24584 | tf_op jit(solution)/shard_map/ppermute | solution.py:253
  103.1 7.0 %collective-permute-start.23 = (f32[1,2048]{1,0:T(1,128)S(1)}, f32[1,2048]{1,0:T(1,128)S(1)}, u32[]{:S(2)}, u32[]{:S(2)}) collective-permute-start(f32[1,2048]{1,0:T(1,128)S(1)} %get-tuple-element.62), channel_id=1, source_target_pairs={{0,3},{1,2},{2,1},{3,0},{4,7},{5,6},{6,5},{7,4},{8,11},{9,10},{10,... | collective-permute-start | bytes 24584 | tf_op jit(solution)/shard_map/ppermute | solution.py:253
  134.0 10.8 %collective-permute-start.33 = (f32[1,128]{1,0:T(1,128)S(1)}, f32[1,128]{1,0:T(1,128)S(1)}, u32[]{:S(2)}, u32[]{:S(2)}) collective-permute-start(f32[1,128]{1,0:T(1,128)S(1)} %get-tuple-element.67), channel_id=1, source_target_pairs={{0,1},{1,0},{2,3},{3,2},{4,5},{5,4},{6,7},{7,6},{8,9},{9,8},{10,11... | collective-permute-start | bytes 1544 | tf_op jit(solution)/shard_map/ppermute | solution.py:253
  139.3 6.3 %collective-permute-start.34 = (f32[1,128]{1,0:T(1,128)S(1)}, f32[1,128]{1,0:T(1,128)S(1)}, u32[]{:S(2)}, u32[]{:S(2)}) collective-permute-start(f32[1,128]{1,0:T(1,128)S(1)} %get-tuple-element.67), channel_id=1, source_target_pairs={{0,2},{1,3},{2,0},{3,1},{4,6},{5,7},{6,4},{7,5},{8,10},{9,11},{10,... | collective-permute-start | bytes 1544 | tf_op jit(solution)/shard_map/ppermute | solution.py:253
  144.1 6.9 %collective-permute-start.35 = (f32[1,128]{1,0:T(1,128)S(1)}, f32[1,128]{1,0:T(1,128)S(1)}, u32[]{:S(2)}, u32[]{:S(2)}) collective-permute-start(f32[1,128]{1,0:T(1,128)S(1)} %get-tuple-element.67), channel_id=1, source_target_pairs={{0,3},{1,2},{2,1},{3,0},{4,7},{5,6},{6,5},{7,4},{8,11},{9,10},{10,... | collective-permute-start | bytes 1544 | tf_op jit(solution)/shard_map/ppermute | solution.py:253
  (25 other events, 145.1 us)

commit v3 on v2

--- a/solution.py
+++ b/solution.py
@@ -93,6 +93,10 @@
     return pl.BlockSpec((rows, COLS), lambda j: (0, j))
 
 
+def in_hbm(value):
+    return pltpu.with_memory_space_constraint(value, pltpu.HBM)
+
+
 G_SPEC = moving(512)
 PARAMS = pltpu.CompilerParams(vmem_limit_bytes=VMEM_LIMIT)
 COST = pl.CostEstimate(flops=2 * 512 * 1024 * 2048, bytes_accessed=9 << 20, transcendentals=0)
@@ -117,7 +121,7 @@
         in_specs=[fixed(512, 768), moving(384), moving(384), G_SPEC],
         out_specs=[G_SPEC, moving(1), fixed(1, 512)],
         out_shape=[
-            jax.ShapeDtypeStruct((512, 2048), jnp.float32),
+            pltpu.HBM((512, 2048), jnp.float32),
             jax.ShapeDtypeStruct((1, 2048), jnp.float32),
             jax.ShapeDtypeStruct((1, 512), jnp.float32),
         ],
@@ -127,28 +131,29 @@
     )(x, own, other, first)
 
 
-def weigh_kernel(g_ref, moment_ref, sums_ref, row_ref, state_ref, out_ref, acc_ref, weighed_ref):
+def weigh_kernel(g_ref, moment_ref, parts_ref, row_ref, state_ref, out_ref, acc_ref, weighed_ref):
     step = pl.program_id(0)
-    state = 0.8 * moment_ref[...] + 0.2 * sums_ref[...] / D
+    sums = jnp.sum(parts_ref[...], axis=0, keepdims=True)
+    state = 0.8 * moment_ref[...] + 0.2 * sums / D
     state_ref[...] = state
     scaled = g_ref[...] * lax.rsqrt(state)
     gather_rows(step, across(scaled * scaled), acc_ref, weighed_ref)
 
     @pl.when(step == pl.num_programs(0) - 1)
     def _():
-        out_ref[0:1, :] = row_ref[...]
-        out_ref[1:2, :] = weighed_ref[...]
-
-
-def weigh(g, column_moment, column_sums, row_part):
+        out_ref[:, 0:512] = row_ref[...]
+        out_ref[:, 512:1024] = weighed_ref[...]
+
+
+def weigh(g, column_moment, column_parts, row_part):
     return pl.pallas_call(
         weigh_kernel,
         grid=(2048 // COLS,),
-        in_specs=[G_SPEC, moving(1), moving(1), fixed(1, 512)],
-        out_specs=[moving(1), fixed(2, 512)],
+        in_specs=[G_SPEC, moving(1), moving(16), fixed(1, 512)],
+        out_specs=[moving(1), fixed(1, 1024)],
         out_shape=[
             jax.ShapeDtypeStruct((1, 2048), jnp.float32),
-            jax.ShapeDtypeStruct((2, 512), jnp.float32),
+            jax.ShapeDtypeStruct((1, 1024), jnp.float32),
         ],
         scratch_shapes=[
             pltpu.VMEM((512, 128), jnp.float32),
@@ -158,18 +163,19 @@
         cost_estimate=pl.CostEstimate(
             flops=4 * 512 * 2048, bytes_accessed=4 << 20, transcendentals=0
         ),
-    )(g, column_moment, column_sums, row_part)
-
-
-def totals_kernel(moment_ref, sums_ref, state_ref, total_ref):
-    state = 0.8 * moment_ref[...] + 0.2 * sums_ref[0:1, :] / FF
+    )(in_hbm(g), column_moment, column_parts, row_part)
+
+
+def totals_kernel(moment_ref, parts_ref, state_ref, total_ref):
+    sums = jnp.sum(parts_ref[...], axis=0, keepdims=True)
+    state = 0.8 * moment_ref[...] + 0.2 * sums[:, 0:512] / FF
     state_ref[...] = state
-    squares = jnp.sum(sums_ref[1:2, :] / state)
+    squares = jnp.sum(sums[:, 512:1024] / state)
     lane = lax.broadcasted_iota(jnp.int32, (1, 128), 1)
     total_ref[...] = jnp.where(lane == 0, squares, jnp.where(lane == 1, jnp.sum(state), 0.0))
 
 
-def totals_of(row_moment, sums):
+def totals_of(row_moment, parts):
     return pl.pallas_call(
         totals_kernel,
         out_shape=[
@@ -177,8 +183,8 @@
             jax.ShapeDtypeStruct((1, 128), jnp.float32),
         ],
         compiler_params=PARAMS,
-        cost_estimate=pl.CostEstimate(flops=2048, bytes_accessed=8192, transcendentals=0),
-    )(row_moment, sums)
+        cost_estimate=pl.CostEstimate(flops=16384, bytes_accessed=70000, transcendentals=0),
+    )(row_moment, parts)
 
 
 def clip_kernel(g_ref, row_ref, col_ref, totals_ref, out_ref, mean_ref, rows_ref):
@@ -187,7 +193,7 @@
         rows_ref[...] = jnp.broadcast_to(lax.rsqrt(row_ref[...]), (128, 512)).T
 
     lane = lax.broadcasted_iota(jnp.int32, (1, 128), 1)
-    totals = totals_ref[...]
+    totals = jnp.sum(totals_ref[...], axis=0, keepdims=True)
     total = jnp.sum(jnp.where(lane == 0, totals, 0.0), axis=1, keepdims=True)
     row_mean = jnp.sum(jnp.where(lane == 1, totals, 0.0), axis=1, keepdims=True) / D
     mean_ref[...] = row_mean
@@ -204,7 +210,7 @@
     return pl.pallas_call(
         clip_kernel,
         grid=(2048 // COLS,),
-        in_specs=[G_SPEC, fixed(1, 512), moving(1), fixed(1, 128)],
+        in_specs=[G_SPEC, fixed(1, 512), moving(1), fixed(16, 128)],
         out_specs=[G_SPEC, fixed(1, 1)],
         out_shape=[
             jax.ShapeDtypeStruct((512, 2048), jnp.float32),
@@ -215,7 +221,7 @@
         cost_estimate=pl.CostEstimate(
             flops=2 * 512 * 2048, bytes_accessed=8 << 20, transcendentals=0
         ),
-    )(g, row_state, column_state, totals)
+    )(in_hbm(g), row_state, column_state, totals)
 
 
 def cyclic(size, stride, shift):
@@ -247,20 +253,9 @@
     return lax.ppermute(value, "col", flipped(16, 2))
 
 
-def over(value, axis, stride):
-    size = 16 if axis == "col" else 4
-    a, b, c = [
-        lax.ppermute(value, axis, flipped(size, mask * stride)) for mask in (2, 1, 3)
-    ]
-    return (value + b) + (a + c)
-
-
-def over_col(value):
-    return over(over(value, "col", 1), "col", 4)
-
-
-def over_dp_row(value):
-    return over(over(value, "dp", 1), "row", 1)
+def copies(value, axis):
+    rows = jnp.broadcast_to(value, (16,) + value.shape)
+    return lax.all_to_all(rows, axis, 0, 0).reshape(16, value.shape[1])
 
 
 def per_device(inputs, grad_out, row_moment, column_moment):
@@ -274,32 +269,32 @@
     stage = lax.optimization_barrier
 
     pair = jnp.concatenate([inputs, swap_row(inputs, 1)])
-    by_group, pair = stage((jnp.transpose(grad_out, (1, 0, 2)), pair))
+    by_group = stage(jnp.transpose(grad_out, (1, 0, 2)))
     groups = [
         lax.dynamic_index_in_dim(by_group, (me + s) % 4, 0, keepdims=False) for s in range(4)
     ]
     far0 = swap_z(groups[0])
     blocks = [move_x(groups[s], s) for s in (1, 2, 3)]
-    x0 = jnp.concatenate([pair, swap_row(pair, 2)])
     first = jnp.concatenate([groups[0]] + blocks + [far0])
-    first, rest, x0 = stage((first, jnp.concatenate(blocks), x0))
+    first, rest, pair = stage((first, jnp.concatenate(blocks), pair))
 
     far = swap_z(rest)
     first1, first3 = move_y(first, 1), move_y(first, -1)
+    x0 = jnp.concatenate([pair, swap_row(pair, 2)])
+    first1, first3, x0 = stage((first1, first3, x0))
+
+    first2a, first2b = move_y(first1[0:80], 1), move_y(first3[80:160], -1)
     x1, x3 = move_x(x0, 1), move_x(x0, -1)
-    first1, first3, x1, x3 = stage((first1, first3, x1, x3))
-
-    first2a, first2b = move_y(first1[0:80], 1), move_y(first3[80:160], -1)
-    x2a, x2b = move_x(x1[0:256], 1), move_x(x3[256:512], -1)
-    first2a, first2b, far, x2a, x2b = stage((first2a, first2b, far, x2a, x2b))
+    first2a, first2b, far, x1, x3 = stage((first2a, first2b, far, x1, x3))
 
     far1, far3 = move_y(far, 1), move_y(far, -1)
     own = jnp.concatenate([first, first1, first3, first2a, first2b])
     other = swap_cores(own)
+    x2a, x2b = move_x(x1[0:256], 1), move_x(x3[256:512], -1)
+    far1, far3, other, x2a, x2b = stage((far1, far3, other, x2a, x2b))
+
+    far2a, far2b = move_y(far1[0:48], 1), move_y(far3[48:96], -1)
     x_first, x_second = arrange(at, (x0, x1, x2a, x2b, x3))
-    far1, far3, other, x_first, x_second = stage((far1, far3, other, x_first, x_second))
-
-    far2a, far2b = move_y(far1[0:48], 1), move_y(far3[48:96], -1)
     gradient = first_product(x_first, own, other)
     far2a, far2b, gradient = stage((far2a, far2b, gradient))
 
@@ -309,10 +304,10 @@
         x_second, far_own, far_other, gradient
     )
     column_state, sums = weigh(
-        gradient, column_moment[None], over_col(column_part), row_part
+        gradient, column_moment[None], copies(column_part, "col"), row_part
     )
-    row_state, totals = totals_of(row_moment[None], over_dp_row(sums))
-    update, row_mean = clip(gradient, row_state, column_state, over_col(totals))
+    row_state, totals = totals_of(row_moment[None], copies(sums, ("dp", "row")))
+    update, row_mean = clip(gradient, row_state, column_state, copies(totals, "col"))
     return (update, row_state[0], column_state[0], row_mean[0, 0])
 
 

time: 162 us -> 156 us (0.963)
  blocking collectives: 0 us -> 41.6 us
  starting transfers between devices: 71 us -> 35.2 us
  waiting for transfers between devices: 60 us -> 45.3 us
  Pallas kernels: 16.7 us -> 22.2 us
  local copies, waits for them, and re-layouts: 11.8 us -> 9.86 us
    all_to_all x0 -> x3, blocking collectives: none -> 41.6 us  [copies(): return lax.all_to_all(rows, axis, 0, 0).reshape(16, value.shape[1])]
    ppermute x18 -> x0, starting transfers between devices: 32.6 us -> none  [over(): lax.ppermute(value, axis, flipped(size, mask * stride))]
    ppermute x18 -> x0, waiting for transfers between devices: 19.7 us -> none  [over(): lax.ppermute(value, axis, flipped(size, mask * stride))]
    ppermute x2, waiting for transfers between devices: 4.97 us -> 15.5 us  [swap_z(): return lax.ppermute(value, 'col', flipped(16, 2))]
    ppermute x7, waiting for transfers between devices: 10.2 us -> 4.14 us  [move_x(): return lax.ppermute(value, 'dp', cyclic(4, 1, shift % 4))]
    ppermute x2, waiting for transfers between devices: 17.2 us -> 22.5 us  [swap_row(): return lax.ppermute(value, 'row', flipped(4, mask))]
    ppermute x8, waiting for transfers between devices: 4.87 us -> 0.07 us  [move_y(): return lax.ppermute(value, 'col', cyclic(4, 4, shift % 4))]
    unnamed x33, local copies, waits for them, and re-layouts: 9.66 us -> 6.21 us
  transfers between devices with their start and end apart: 39 -> 21, of which waited for: 20 -> 6; matrix products, arithmetic and copies ran while one was open for 4% -> 4% of each run, Pallas kernels for 4% -> 5%
where the time goes in v3:
time: 156 us; the launch traced here: 155 us
  waiting for transfers between devices  45.3 us (29%)
  blocking collectives  41.6 us (27%)
  starting transfers between devices  35.2 us (23%)
  Pallas kernels  22.2 us (14%)
  local copies, waits for them, and re-layouts  9.86 us (6%)
    all_to_all x3, blocking collectives, copies(): return lax.all_to_all(rows, axis, 0, 0).reshape(16, value.shape[1])  41.6 us
    ppermute x2, waiting for transfers between devices, swap_row(): return lax.ppermute(value, 'row', flipped(4, mask))  22.5 us
    ppermute x2, waiting for transfers between devices, swap_z(): return lax.ppermute(value, 'col', flipped(16, 2))  15.5 us
    ppermute x8, starting transfers between devices, move_y(): return lax.ppermute(value, 'col', cyclic(4, 4, shift % 4))  11.2 us
    ppermute x7, starting transfers between devices, move_x(): return lax.ppermute(value, 'dp', cyclic(4, 1, shift % 4))  11.2 us
    ppermute x2, starting transfers between devices, swap_z(): return lax.ppermute(value, 'col', flipped(16, 2))  7.09 us
    unnamed x33, local copies, waits for them, and re-layouts  6.21 us
    pallas_call x1, Pallas kernels, first_product(): pl.pallas_call(first_kernel, grid=(2048 // COLS,), in_specs=[fixed(512, 1...  5.46 us
  transfers between devices with their start and end apart: 21, of which 6 were waited for; matrix products, arithmetic and copies ran while one was open for 4% of the time, Pallas kernels for 5%

profile of v3, /device:TPU:1, one launch (start us, length us, event | category | flops | bytes accessed | tf_op | source)
XLA Modules:
  0.0 155.3 jit_solution(7625226067284208800)
XLA Ops:
  2.1 2.1 %collective-permute-start = (bf16[32,2048]{1,0:T(8,128)(2,1)S(1)}, bf16[32,2048]{1,0:T(8,128)(2,1)S(1)}, u32[]{:S(2)}, u32[]{:S(2)}) collective-permute-start(bf16[32,2048]{1,0:T(8,128)(2,1)S(1)} %get-tuple-element.68), channel_id=1, source_target_pairs={{0,64},{64,128},{128,192},{192,0},{1,65},{65,129},{129,193},{193,1... | collective-permute-start | bytes 393224 | tf_op jit(solution)/shard_map/ppermute | solution.py:241
  4.2 2.5 %collective-permute-start.1 = (bf16[32,2048]{1,0:T(8,128)(2,1)S(1)}, bf16[32,2048]{1,0:T(8,128)(2,1)S(1)}, u32[]{:S(2)}, u32[]{:S(2)}) collective-permute-start(bf16[32,2048]{1,0:T(8,128)(2,1)S(1)} %get-tuple-element.67), channel_id=1, source_target_pairs={{0,128},{64,192},{128,0},{192,64},{1,129},{65,193},{129,1},{193,65... | collective-permute-start | bytes 393224 | tf_op jit(solution)/shard_map/ppermute | solution.py:241
  7.9 7.0 %collective-permute-start.3 = (bf16[32,2048]{1,0:T(8,128)(2,1)S(1)}, bf16[32,2048]{1,0:T(8,128)(2,1)S(1)}, u32[]{:S(2)}, u32[]{:S(2)}) collective-permute-start(bf16[32,2048]{1,0:T(8,128)(2,1)S(1)} %get-tuple-element.65), channel_id=1, source_target_pairs={{0,2},{1,3},{2,0},{3,1},{4,6},{5,7},{6,4},{7,5},{8,10},{9,11},{10,... | collective-permute-start | bytes 393224 | tf_op jit(solution)/shard_map/ppermute | solution.py:253
  15.7 8.2 %collective-permute-done.4 = bf16[128,512]{1,0:T(8,128)(2,1)S(1)} collective-permute-done((bf16[128,512]{1,0:T(8,128)(2,1)}, bf16[128,512]{1,0:T(8,128)(2,1)S(1)}, u32[]{:S(2)}, u32[]{:S(2)}) %collective-permute-start.4) | collective-permute-done | bytes 131104 | tf_op jit(solution)/shard_map/ppermute | solution.py:249
  25.3 1.5 collective-permute-start.6
  26.8 14.4 %collective-permute-done.7 = bf16[256,512]{1,0:T(8,128)(2,1)S(1)} collective-permute-done((bf16[256,512]{1,0:T(8,128)(2,1)S(1)}, bf16[256,512]{1,0:T(8,128)(2,1)S(1)}, u32[]{:S(2)}, u32[]{:S(2)}) %collective-permute-start.7) | collective-permute-done | bytes 262176 | tf_op jit(solution)/shard_map/ppermute | solution.py:249
  41.6 2.4 %collective-permute-start.12 = (bf16[512,512]{1,0:T(8,128)(2,1)S(1)}, bf16[512,512]{1,0:T(8,128)(2,1)S(1)}, u32[]{:S(2)}, u32[]{:S(2)}) collective-permute-start(bf16[512,512]{1,0:T(8,128)(2,1)S(1)} %pad_maximum_fusion.x0_ref), channel_id=1, source_target_pairs={{0,192},{64,0},{128,64},{192,128},{1,193},{65,1},{129,65},{193,129... | collective-permute-start | bytes 1572872 | tf_op jit(solution)/shard_map/ppermute | solution.py:241
  44.3 2.7 %collective-permute-start.9 = (bf16[80,2048]{1,0:T(8,128)(2,1)S(1)}, bf16[80,2048]{1,0:T(8,128)(2,1)S(1)}, u32[]{:S(2)}, u32[]{:S(2)}) collective-permute-start(bf16[80,2048]{1,0:T(8,128)(2,1)S(1)} %slice.19), channel_id=1, source_target_pairs={{0,12},{1,13},{2,14},{3,15},{4,0},{5,1},{6,2},{7,3},{8,4},{9,5},{1... | collective-permute-start | bytes 983048 | tf_op jit(solution)/shard_map/ppermute | solution.py:245
  47.1 15.5 %collective-permute-done.10 = bf16[96,2048]{1,0:T(8,128)(2,1)} collective-permute-done((bf16[96,2048]{1,0:T(8,128)(2,1)S(1)}, bf16[96,2048]{1,0:T(8,128)(2,1)}, u32[]{:S(2)}, u32[]{:S(2)}) %collective-permute-start.10) | collective-permute-done | bytes 393248 | tf_op jit(solution)/shard_map/ppermute | solution.py:253
  62.7 2.9 %collective-permute-start.15 = (bf16[640,2048]{1,0:T(8,128)(2,1)S(1)}, bf16[640,2048]{1,0:T(8,128)(2,1)}, u32[]{:S(2)}, u32[]{:S(2)}) collective-permute-start(bf16[640,2048]{1,0:T(8,128)(2,1)S(1)} %constant_dynamic-update-slice_fusion.5.own_ref), channel_id=1, source_target_pairs={{0,1},{1,0},{2,3},{3,2},{4,5},{5,4},{6,7},{7,6},{8,9},{9,8},{10,11... | collective-permute-start | bytes 7864328 | tf_op jit(solution)/shard_map/ppermute | solution.py:237
  66.1 2.2 %collective-permute-start.14 = (bf16[96,2048]{1,0:T(8,128)(2,1)}, bf16[96,2048]{1,0:T(8,128)(2,1)}, u32[]{:S(2)}, u32[]{:S(2)}) collective-permute-start(bf16[96,2048]{1,0:T(8,128)(2,1)} %collective-permute-done.10), channel_id=1, source_target_pairs={{0,12},{1,13},{2,14},{3,15},{4,0},{5,1},{6,2},{7,3},{8,4},{9,5},{1... | collective-permute-start | bytes 1179656 | tf_op jit(solution)/shard_map/ppermute | solution.py:245
  69.8 2.7 %collective-permute-start.17 = (bf16[256,512]{1,0:T(8,128)(2,1)}, bf16[256,512]{1,0:T(8,128)(2,1)}, u32[]{:S(2)}, u32[]{:S(2)}) collective-permute-start(bf16[256,512]{1,0:T(8,128)(2,1)} %slice.21), channel_id=1, source_target_pairs={{0,192},{64,0},{128,64},{192,128},{1,193},{65,1},{129,65},{193,129... | collective-permute-start | bytes 786440 | tf_op jit(solution)/shard_map/ppermute | solution.py:241
  73.6 4.1 %collective-permute-done.16.x2a_ref = bf16[256,512]{1,0:T(8,128)(2,1)S(1)} collective-permute-done((bf16[256,512]{1,0:T(8,128)(2,1)}, bf16[256,512]{1,0:T(8,128)(2,1)S(1)}, u32[]{:S(2)}, u32[]{:S(2)}) %collective-permute-start.16) | collective-permute-done | bytes 262176 | tf_op jit(solution)/shard_map/ppermute | solution.py:241
  79.8 2.7 %collective-permute-start.19 = (bf16[48,2048]{1,0:T(8,128)(2,1)S(1)}, bf16[48,2048]{1,0:T(8,128)(2,1)S(1)}, u32[]{:S(2)}, u32[]{:S(2)}) collective-permute-start(bf16[48,2048]{1,0:T(8,128)(2,1)S(1)} %slice.23), channel_id=1, source_target_pairs={{0,12},{1,13},{2,14},{3,15},{4,0},{5,1},{6,2},{7,3},{8,4},{9,5},{1... | collective-permute-start | bytes 589832 | tf_op jit(solution)/shard_map/ppermute | solution.py:245
  84.6 1.6 %shard_map.75 = (bf16[512,1280]{1,0:T(8,128)(2,1)S(1)}, bf16[512,768]{1,0:T(8,128)(2,1)S(1)}) custom-call(s32[8]{0:T(128)S(1)} %stack.35.at_ref, bf16[512,512]{1,0:T(8,128)(2,1)S(1)} %pad_maximum_fusion.x0_ref, bf16[512,512]{1,0:T(8,128)(2,1)S(1)} %copy-done.1, bf16[256,512]{1,0:T(8,128)(2,1)S(1)} %collective-permute-done.16.x2a_ref, ...), custom_call_target="tpu_custom_call" | custom-call | bytes 4194304 | tf_op jit(solution)/shard_map/pallas_call | solution.py:35
  86.2 5.5 %shard_map.76.first_ref = f32[512,2048]{1,0:T(8,128)S(1)} custom-call(bf16[512,1280]{1,0:T(8,128)(2,1)S(1)} %get-tuple-element.50.x_ref, bf16[640,2048]{1,0:T(8,128)(2,1)S(1)} %constant_dynamic-update-slice_fusion.5.own_ref, bf16[640,2048]{1,0:T(8,128)(2,1)} %collective-permute-done.15.other_ref), custom_call_target="tpu_custom_call" | custom-call | flops 2147483648 | bytes 9437184 | tf_op jit(solution)/shard_map/pallas_call | solution.py:106
  91.7 2.1 %collective-permute-start.20 = (bf16[384,2048]{1,0:T(8,128)(2,1)S(1)}, bf16[384,2048]{1,0:T(8,128)(2,1)S(1)}, u32[]{:S(2)}, u32[]{:S(2)}) collective-permute-start(bf16[384,2048]{1,0:T(8,128)(2,1)S(1)} %constant_dynamic-update-slice_fusion.10.own_ref), channel_id=1, source_target_pairs={{0,1},{1,0},{2,3},{3,2},{4,5},{5,4},{6,7},{7,6},{8,9},{9,8},{10,11... | collective-permute-start | bytes 4718600 | tf_op jit(solution)/shard_map/ppermute | solution.py:237
  93.8 3.0 %collective-permute-done.20.other_ref = bf16[384,2048]{1,0:T(8,128)(2,1)S(1)} collective-permute-done((bf16[384,2048]{1,0:T(8,128)(2,1)S(1)}, bf16[384,2048]{1,0:T(8,128)(2,1)S(1)}, u32[]{:S(2)}, u32[]{:S(2)}) %collective-permute-start.20) | collective-permute-done | bytes 1572896 | tf_op jit(solution)/shard_map/ppermute | solution.py:237
  96.9 5.0 %shard_map.77 = (f32[512,2048]{1,0:T(8,128)}, f32[1,2048]{1,0:T(1,128)S(1)}, f32[1,512]{1,0:T(1,128)S(1)}) custom-call(bf16[512,768]{1,0:T(8,128)(2,1)S(1)} %get-tuple-element.47.x_ref, bf16[384,2048]{1,0:T(8,128)(2,1)S(1)} %constant_dynamic-update-slice_fusion.10.own_ref, bf16[384,2048]{1,0:T(8,128)(2,1)S(1)} %collective-permute-done.20.other_ref, ...), custom_call_target="tpu_custom_call" | custom-call | flops 2147483648 | bytes 9437184 | tf_op jit(solution)/shard_map/pallas_call | solution.py:118
  102.0 15.1 %all_to_all.15 = f32[16,1,2048]{2,1,0:T(1,128)S(1)} all-to-all(f32[16,1,2048]{2,1,0:T(1,128)S(1)} %broadcast_in_dim.17), channel_id=1, replica_groups=mesh['dp'=4,'row'=4,'col'=16] {'col'}, dimensions={0} | all-to-all | bytes 262144 | tf_op jit(solution)/shard_map/all_to_all | solution.py:258
  117.2 4.3 %shard_map.78 = (f32[1,2048]{1,0:T(1,128)}, f32[1,1024]{1,0:T(1,128)S(1)}) custom-call(f32[512,2048]{1,0:T(8,128)} %get-tuple-element.55.g_ref, f32[1,2048]{1,0:T(1,128)S(1)} %bitcast.38, f32[16,2048]{1,0:T(8,128)S(1)} %bitcast.35, f32[1,512]{1,0:T(1,128)S(1)} %get-tuple-element.57.row_ref), custom_call_target="tpu_custom_call" | custom-call | flops 4194304 | bytes 4194304 | tf_op jit(solution)/shard_map/pallas_call | solution.py:149
  121.5 12.6 %all_to_all.16 = f32[16,1,1024]{2,1,0:T(1,128)S(1)} all-to-all(f32[16,1,1024]{2,1,0:T(1,128)S(1)} %broadcast_in_dim.18), channel_id=1, replica_groups=mesh['dp'=4,'row'=4,'col'=16] {'dp','row'}, dimensions={0} | all-to-all | bytes 131072 | tf_op jit(solution)/shard_map/all_to_all | solution.py:258
  134.7 13.9 %all_to_all.17 = f32[16,1,128]{2,1,0:T(1,128)S(1)} all-to-all(f32[16,1,128]{2,1,0:T(1,128)S(1)} %broadcast_in_dim.19), channel_id=1, replica_groups=mesh['dp'=4,'row'=4,'col'=16] {'col'}, dimensions={0} | all-to-all | bytes 16384 | tf_op jit(solution)/shard_map/all_to_all | solution.py:258
  150.0 5.2 %shard_map.80 = (f32[512,2048]{1,0:T(8,128)}, f32[1,1]{1,0:T(1,128)}) custom-call(f32[512,2048]{1,0:T(8,128)} %get-tuple-element.55.g_ref, f32[1,512]{1,0:T(1,128)S(1)} %copy-done.6, f32[1,2048]{1,0:T(1,128)S(1)} %copy-done.5, f32[16,128]{1,0:T(8,128)S(1)} %bitcast.37), custom_call_target="tpu_custom_call" | custom-call | flops 2097152 | bytes 8388608 | tf_op jit(solution)/shard_map/pallas_call | solution.py:210
  (77 shorter events, 15.0 us)
Async XLA Ops:
  0.6 23.2 %copy-start.8 = (bf16[128,512]{1,0:T(8,128)(2,1)S(1)}, bf16[128,512]{1,0:T(8,128)(2,1)}, u32[]{:S(2)}) copy-start(bf16[128,512]{1,0:T(8,128)(2,1)} %param.4) | copy-start | bytes 393220
  2.1 13.5 %collective-permute-start = (bf16[32,2048]{1,0:T(8,128)(2,1)S(1)}, bf16[32,2048]{1,0:T(8,128)(2,1)S(1)}, u32[]{:S(2)}, u32[]{:S(2)}) collective-permute-start(bf16[32,2048]{1,0:T(8,128)(2,1)S(1)} %get-tuple-element.68), channel_id=1, source_target_pairs={{0,64},{64,128},{128,192},{192,0},{1,65},{65,129},{129,193},{193,1... | collective-permute-start | bytes 393224 | tf_op jit(solution)/shard_map/ppermute | solution.py:241
  4.2 11.4 %collective-permute-start.1 = (bf16[32,2048]{1,0:T(8,128)(2,1)S(1)}, bf16[32,2048]{1,0:T(8,128)(2,1)S(1)}, u32[]{:S(2)}, u32[]{:S(2)}) collective-permute-start(bf16[32,2048]{1,0:T(8,128)(2,1)S(1)} %get-tuple-element.67), channel_id=1, source_target_pairs={{0,128},{64,192},{128,0},{192,64},{1,129},{65,193},{129,1},{193,65... | collective-permute-start | bytes 393224 | tf_op jit(solution)/shard_map/ppermute | solution.py:241
  6.7 8.9 %collective-permute-start.2 = (bf16[32,2048]{1,0:T(8,128)(2,1)S(1)}, bf16[32,2048]{1,0:T(8,128)(2,1)S(1)}, u32[]{:S(2)}, u32[]{:S(2)}) collective-permute-start(bf16[32,2048]{1,0:T(8,128)(2,1)S(1)} %get-tuple-element.66), channel_id=1, source_target_pairs={{0,192},{64,0},{128,64},{192,128},{1,193},{65,1},{129,65},{193,129... | collective-permute-start | bytes 393224 | tf_op jit(solution)/shard_map/ppermute | solution.py:241
  7.9 16.0 %collective-permute-start.3 = (bf16[32,2048]{1,0:T(8,128)(2,1)S(1)}, bf16[32,2048]{1,0:T(8,128)(2,1)S(1)}, u32[]{:S(2)}, u32[]{:S(2)}) collective-permute-start(bf16[32,2048]{1,0:T(8,128)(2,1)S(1)} %get-tuple-element.65), channel_id=1, source_target_pairs={{0,2},{1,3},{2,0},{3,1},{4,6},{5,7},{6,4},{7,5},{8,10},{9,11},{10,... | collective-permute-start | bytes 393224 | tf_op jit(solution)/shard_map/ppermute | solution.py:253
  14.9 9.0 %collective-permute-start.4 = (bf16[128,512]{1,0:T(8,128)(2,1)}, bf16[128,512]{1,0:T(8,128)(2,1)S(1)}, u32[]{:S(2)}, u32[]{:S(2)}) collective-permute-start(bf16[128,512]{1,0:T(8,128)(2,1)} %param.4), channel_id=1, source_target_pairs={{0,16},{16,0},{32,48},{48,32},{1,17},{17,1},{33,49},{49,33},{2,18}... | collective-permute-start | bytes 393224 | tf_op jit(solution)/shard_map/ppermute | solution.py:249
  23.9 17.3 %collective-permute-start.5 = (bf16[160,2048]{1,0:T(8,128)(2,1)S(1)}, bf16[160,2048]{1,0:T(8,128)(2,1)S(1)}, u32[]{:S(2)}, u32[]{:S(2)}) collective-permute-start(bf16[160,2048]{1,0:T(8,128)(2,1)S(1)} %constant_dynamic-update-slice_fusion), channel_id=1, source_target_pairs={{0,4},{1,5},{2,6},{3,7},{4,8},{5,9},{6,10},{7,11},{8,12},{9,13},{1... | collective-permute-start | bytes 1966088 | tf_op jit(solution)/shard_map/ppermute | solution.py:245
  25.3 15.9 %collective-permute-start.6 = (bf16[160,2048]{1,0:T(8,128)(2,1)S(1)}, bf16[160,2048]{1,0:T(8,128)(2,1)S(1)}, u32[]{:S(2)}, u32[]{:S(2)}) collective-permute-start(bf16[160,2048]{1,0:T(8,128)(2,1)S(1)} %constant_dynamic-update-slice_fusion), channel_id=1, source_target_pairs={{0,12},{1,13},{2,14},{3,15},{4,0},{5,1},{6,2},{7,3},{8,4},{9,5},{1... | collective-permute-start | bytes 1966088 | tf_op jit(solution)/shard_map/ppermute | solution.py:245
  26.8 14.4 %collective-permute-start.7 = (bf16[256,512]{1,0:T(8,128)(2,1)S(1)}, bf16[256,512]{1,0:T(8,128)(2,1)S(1)}, u32[]{:S(2)}, u32[]{:S(2)}) collective-permute-start(bf16[256,512]{1,0:T(8,128)(2,1)S(1)} %pad_maximum_fusion.2), channel_id=1, source_target_pairs={{0,32},{16,48},{32,0},{48,16},{1,33},{17,49},{33,1},{49,17},{2,34}... | collective-permute-start | bytes 786440 | tf_op jit(solution)/shard_map/ppermute | solution.py:249
  41.2 21.4 %collective-permute-start.11 = (bf16[512,512]{1,0:T(8,128)(2,1)S(1)}, bf16[512,512]{1,0:T(8,128)(2,1)S(1)}, u32[]{:S(2)}, u32[]{:S(2)}) collective-permute-start(bf16[512,512]{1,0:T(8,128)(2,1)S(1)} %pad_maximum_fusion.x0_ref), channel_id=1, source_target_pairs={{0,64},{64,128},{128,192},{192,0},{1,65},{65,129},{129,193},{193,1... | collective-permute-start | bytes 1572872 | tf_op jit(solution)/shard_map/ppermute | solution.py:241
  41.6 21.0 %collective-permute-start.12 = (bf16[512,512]{1,0:T(8,128)(2,1)S(1)}, bf16[512,512]{1,0:T(8,128)(2,1)S(1)}, u32[]{:S(2)}, u32[]{:S(2)}) collective-permute-start(bf16[512,512]{1,0:T(8,128)(2,1)S(1)} %pad_maximum_fusion.x0_ref), channel_id=1, source_target_pairs={{0,192},{64,0},{128,64},{192,128},{1,193},{65,1},{129,65},{193,129... | collective-permute-start | bytes 1572872 | tf_op jit(solution)/shard_map/ppermute | solution.py:241
  44.0 18.6 %collective-permute-start.10 = (bf16[96,2048]{1,0:T(8,128)(2,1)S(1)}, bf16[96,2048]{1,0:T(8,128)(2,1)}, u32[]{:S(2)}, u32[]{:S(2)}) collective-permute-start(bf16[96,2048]{1,0:T(8,128)(2,1)S(1)} %pad_maximum_fusion.1), channel_id=1, source_target_pairs={{0,2},{1,3},{2,0},{3,1},{4,6},{5,7},{6,4},{7,5},{8,10},{9,11},{10,... | collective-permute-start | bytes 1179656 | tf_op jit(solution)/shard_map/ppermute | solution.py:253
  44.2 18.5 %collective-permute-start.8 = (bf16[80,2048]{1,0:T(8,128)(2,1)S(1)}, bf16[80,2048]{1,0:T(8,128)(2,1)S(1)}, u32[]{:S(2)}, u32[]{:S(2)}) collective-permute-start(bf16[80,2048]{1,0:T(8,128)(2,1)S(1)} %slice.18), channel_id=1, source_target_pairs={{0,4},{1,5},{2,6},{3,7},{4,8},{5,9},{6,10},{7,11},{8,12},{9,13},{1... | collective-permute-start | bytes 983048 | tf_op jit(solution)/shard_map/ppermute | solution.py:245
  44.3 18.3 %collective-permute-start.9 = (bf16[80,2048]{1,0:T(8,128)(2,1)S(1)}, bf16[80,2048]{1,0:T(8,128)(2,1)S(1)}, u32[]{:S(2)}, u32[]{:S(2)}) collective-permute-start(bf16[80,2048]{1,0:T(8,128)(2,1)S(1)} %slice.19), channel_id=1, source_target_pairs={{0,12},{1,13},{2,14},{3,15},{4,0},{5,1},{6,2},{7,3},{8,4},{9,5},{1... | collective-permute-start | bytes 983048 | tf_op jit(solution)/shard_map/ppermute | solution.py:245
  62.7 15.1 %collective-permute-start.15 = (bf16[640,2048]{1,0:T(8,128)(2,1)S(1)}, bf16[640,2048]{1,0:T(8,128)(2,1)}, u32[]{:S(2)}, u32[]{:S(2)}) collective-permute-start(bf16[640,2048]{1,0:T(8,128)(2,1)S(1)} %constant_dynamic-update-slice_fusion.5.own_ref), channel_id=1, source_target_pairs={{0,1},{1,0},{2,3},{3,2},{4,5},{5,4},{6,7},{7,6},{8,9},{9,8},{10,11... | collective-permute-start | bytes 7864328 | tf_op jit(solution)/shard_map/ppermute | solution.py:237
  65.6 12.2 %collective-permute-start.13 = (bf16[96,2048]{1,0:T(8,128)(2,1)}, bf16[96,2048]{1,0:T(8,128)(2,1)}, u32[]{:S(2)}, u32[]{:S(2)}) collective-permute-start(bf16[96,2048]{1,0:T(8,128)(2,1)} %collective-permute-done.10), channel_id=1, source_target_pairs={{0,4},{1,5},{2,6},{3,7},{4,8},{5,9},{6,10},{7,11},{8,12},{9,13},{1... | collective-permute-start | bytes 1179656 | tf_op jit(solution)/shard_map/ppermute | solution.py:245
  66.1 11.7 %collective-permute-start.14 = (bf16[96,2048]{1,0:T(8,128)(2,1)}, bf16[96,2048]{1,0:T(8,128)(2,1)}, u32[]{:S(2)}, u32[]{:S(2)}) collective-permute-start(bf16[96,2048]{1,0:T(8,128)(2,1)} %collective-permute-done.10), channel_id=1, source_target_pairs={{0,12},{1,13},{2,14},{3,15},{4,0},{5,1},{6,2},{7,3},{8,4},{9,5},{1... | collective-permute-start | bytes 1179656 | tf_op jit(solution)/shard_map/ppermute | solution.py:245
  69.0 8.7 %collective-permute-start.16 = (bf16[256,512]{1,0:T(8,128)(2,1)}, bf16[256,512]{1,0:T(8,128)(2,1)S(1)}, u32[]{:S(2)}, u32[]{:S(2)}) collective-permute-start(bf16[256,512]{1,0:T(8,128)(2,1)} %slice.20), channel_id=1, source_target_pairs={{0,64},{64,128},{128,192},{192,0},{1,65},{65,129},{129,193},{193,1... | collective-permute-start | bytes 786440 | tf_op jit(solution)/shard_map/ppermute | solution.py:241
  69.8 8.0 %collective-permute-start.17 = (bf16[256,512]{1,0:T(8,128)(2,1)}, bf16[256,512]{1,0:T(8,128)(2,1)}, u32[]{:S(2)}, u32[]{:S(2)}) collective-permute-start(bf16[256,512]{1,0:T(8,128)(2,1)} %slice.21), channel_id=1, source_target_pairs={{0,192},{64,0},{128,64},{192,128},{1,193},{65,1},{129,65},{193,129... | collective-permute-start | bytes 786440 | tf_op jit(solution)/shard_map/ppermute | solution.py:241
  78.8 12.9 %collective-permute-start.18 = (bf16[48,2048]{1,0:T(8,128)(2,1)S(1)}, bf16[48,2048]{1,0:T(8,128)(2,1)S(1)}, u32[]{:S(2)}, u32[]{:S(2)}) collective-permute-start(bf16[48,2048]{1,0:T(8,128)(2,1)S(1)} %slice.22), channel_id=1, source_target_pairs={{0,4},{1,5},{2,6},{3,7},{4,8},{5,9},{6,10},{7,11},{8,12},{9,13},{1... | collective-permute-start | bytes 589832 | tf_op jit(solution)/shard_map/ppermute | solution.py:245
  79.8 11.9 %collective-permute-start.19 = (bf16[48,2048]{1,0:T(8,128)(2,1)S(1)}, bf16[48,2048]{1,0:T(8,128)(2,1)S(1)}, u32[]{:S(2)}, u32[]{:S(2)}) collective-permute-start(bf16[48,2048]{1,0:T(8,128)(2,1)S(1)} %slice.23), channel_id=1, source_target_pairs={{0,12},{1,13},{2,14},{3,15},{4,0},{5,1},{6,2},{7,3},{8,4},{9,5},{1... | collective-permute-start | bytes 589832 | tf_op jit(solution)/shard_map/ppermute | solution.py:245
  91.7 5.1 %collective-permute-start.20 = (bf16[384,2048]{1,0:T(8,128)(2,1)S(1)}, bf16[384,2048]{1,0:T(8,128)(2,1)S(1)}, u32[]{:S(2)}, u32[]{:S(2)}) collective-permute-start(bf16[384,2048]{1,0:T(8,128)(2,1)S(1)} %constant_dynamic-update-slice_fusion.10.own_ref), channel_id=1, source_target_pairs={{0,1},{1,0},{2,3},{3,2},{4,5},{5,4},{6,7},{7,6},{8,9},{9,8},{10,11... | collective-permute-start | bytes 4718600 | tf_op jit(solution)/shard_map/ppermute | solution.py:237
  96.9 20.3 %copy-start.4 = (f32[2048]{0:T(1024)S(1)}, f32[2048]{0:T(1024)}, u32[]{:S(2)}) copy-start(f32[2048]{0:T(1024)} %param.7) | copy-start | bytes 24580
  102.0 32.1 %copy-start.7 = (f32[512]{0:T(512)S(1)}, f32[512]{0:T(512)}, u32[]{:S(2)}) copy-start(f32[512]{0:T(512)} %param.6) | copy-start | bytes 6148
  (6 other events, 37.6 us)

commit v4 on v3

--- a/solution.py
+++ b/solution.py
@@ -9,25 +9,29 @@
 FF = 32768
 VMEM_LIMIT = 18 * 1024 * 1024
 COLS = 512
-PLACES = (0, 1, 3, 2)
-FIRST = [(s, t, far) for t in PLACES for s, far in ((0, 0), (1, 0), (2, 0), (3, 0), (0, 1))]
-SECOND = [(s, t, 1) for t in PLACES for s in (1, 2, 3)]
-
-
-def arrange_kernel(at_ref, x0_ref, x1_ref, x2a_ref, x2b_ref, x3_ref, first_ref, second_ref, x2_ref):
+FIRST = ((0, 0), (1, 0), (2, 0), (3, 0), (0, 1))
+FAR = ((1, 1), (2, 1), (3, 1))
+PARTS = (
+    [(s, t, far) for t in (0, 1, 3) for s, far in FIRST],
+    [(s, 2, far) for s, far in FIRST] + [(s, t, far) for t in (0, 1, 3) for s, far in FAR],
+    [(s, 2, far) for s, far in FAR],
+)
+
+
+def arrange_kernel(at_ref, x0_ref, x1_ref, x2a_ref, x2b_ref, x3_ref, a_ref, b_ref, c_ref, x2_ref):
     half = x2a_ref.shape[0]
     x2_ref[0:half, :] = x2a_ref[...]
     x2_ref[half:, :] = x2b_ref[...]
     pieces = (x0_ref, x1_ref, x2_ref, x3_ref)
 
-    for order, out_ref in ((FIRST, first_ref), (SECOND, second_ref)):
-        blocks = [block + (other,) for other in (0, 1) for block in order]
-        for k in range(len(blocks) // 4):
+    for part, out_ref in zip(PARTS, (a_ref, b_ref, c_ref)):
+        blocks = [block + (other,) for other in (0, 1) for block in part]
+        for k in range(0, len(blocks), 4):
             rows = []
-            for s, t, far, other in blocks[4 * k : 4 * k + 4]:
+            for s, t, far, other in blocks[k : k + 4]:
                 start = pl.multiple_of(at_ref[t] + at_ref[4 + far] + at_ref[6 + other], 32)
                 rows.append(pieces[s][pl.ds(start, 32), :])
-            out_ref[:, k * 128 : (k + 1) * 128] = jnp.concatenate(rows, axis=0).T
+            out_ref[:, k * 32 : (k + len(rows)) * 32] = jnp.concatenate(rows, axis=0).T
 
 
 def arrange(at, pieces):
@@ -35,10 +39,9 @@
     return pl.pallas_call(
         arrange_kernel,
         in_specs=[pl.BlockSpec(memory_space=pltpu.SMEM)] + [whole] * 5,
-        out_specs=[whole] * 2,
-        out_shape=[
-            jax.ShapeDtypeStruct((512, 1280), jnp.bfloat16),
-            jax.ShapeDtypeStruct((512, 768), jnp.bfloat16),
+        out_specs=[whole] * 3,
+        out_shape=[
+            jax.ShapeDtypeStruct((512, 64 * len(part)), jnp.bfloat16) for part in PARTS
         ],
         scratch_shapes=[pltpu.VMEM((512, 512), jnp.bfloat16)],
         compiler_params=PARAMS,
@@ -46,10 +49,19 @@
     )(at, *pieces)
 
 
-def first_kernel(x_ref, own_ref, other_ref, out_ref):
-    out_ref[...] = jnp.dot(
-        x_ref[:, 0:640], own_ref[...], preferred_element_type=jnp.float32
-    ) + jnp.dot(x_ref[:, 640:1280], other_ref[...], preferred_element_type=jnp.float32)
+def both(x_ref, own_ref, other_ref):
+    rows = own_ref.shape[0]
+    return jnp.dot(
+        x_ref[:, 0:rows], own_ref[...], preferred_element_type=jnp.float32
+    ) + jnp.dot(x_ref[:, rows : 2 * rows], other_ref[...], preferred_element_type=jnp.float32)
+
+
+def start_kernel(x_ref, own_ref, other_ref, out_ref):
+    out_ref[...] = both(x_ref, own_ref, other_ref)
+
+
+def add_kernel(x_ref, own_ref, other_ref, before_ref, out_ref):
+    out_ref[...] = before_ref[...] + both(x_ref, own_ref, other_ref)
 
 
 def across(value):
@@ -73,12 +85,8 @@
         row_ref[...] = jnp.sum(acc_ref[...].T, axis=0, keepdims=True)
 
 
-def second_kernel(
-    x_ref, own_ref, other_ref, first_ref, out_ref, col_ref, row_ref, acc_ref
-):
-    value = first_ref[...]
-    value += jnp.dot(x_ref[:, 0:384], own_ref[...], preferred_element_type=jnp.float32)
-    value += jnp.dot(x_ref[:, 384:768], other_ref[...], preferred_element_type=jnp.float32)
+def last_kernel(x_ref, own_ref, other_ref, before_ref, out_ref, col_ref, row_ref, acc_ref):
+    value = before_ref[...] + both(x_ref, own_ref, other_ref)
     out_ref[...] = value
     squares = value * value + 1e-30
     col_ref[...] = jnp.sum(squares, axis=0, keepdims=True)
@@ -93,42 +101,54 @@
     return pl.BlockSpec((rows, COLS), lambda j: (0, j))
 
 
-def in_hbm(value):
-    return pltpu.with_memory_space_constraint(value, pltpu.HBM)
+def in_vmem(value):
+    return pltpu.with_memory_space_constraint(value, pltpu.VMEM)
 
 
 G_SPEC = moving(512)
 PARAMS = pltpu.CompilerParams(vmem_limit_bytes=VMEM_LIMIT)
-COST = pl.CostEstimate(flops=2 * 512 * 1024 * 2048, bytes_accessed=9 << 20, transcendentals=0)
-
-
-def first_product(x, own, other):
-    return pl.pallas_call(
-        first_kernel,
+
+
+def cost_of(x):
+    return pl.CostEstimate(
+        flops=2 * 512 * x.shape[1] * 2048, bytes_accessed=9 << 20, transcendentals=0
+    )
+
+
+def product(x, own, other, before=None):
+    rows = own.shape[0]
+    specs = [fixed(512, 2 * rows), moving(rows), moving(rows)]
+    operands = [x, own, other]
+    if before is not None:
+        specs.append(G_SPEC)
+        operands.append(before)
+    return pl.pallas_call(
+        start_kernel if before is None else add_kernel,
         grid=(2048 // COLS,),
-        in_specs=[fixed(512, 1280), moving(640), moving(640)],
+        in_specs=specs,
         out_specs=G_SPEC,
         out_shape=jax.ShapeDtypeStruct((512, 2048), jnp.float32),
         compiler_params=PARAMS,
-        cost_estimate=COST,
-    )(x, own, other)
-
-
-def second_product(x, own, other, first):
-    return pl.pallas_call(
-        second_kernel,
+        cost_estimate=cost_of(x),
+    )(*operands)
+
+
+def last_product(x, own, other, before):
+    rows = own.shape[0]
+    return pl.pallas_call(
+        last_kernel,
         grid=(2048 // COLS,),
-        in_specs=[fixed(512, 768), moving(384), moving(384), G_SPEC],
+        in_specs=[fixed(512, 2 * rows), moving(rows), moving(rows), G_SPEC],
         out_specs=[G_SPEC, moving(1), fixed(1, 512)],
         out_shape=[
-            pltpu.HBM((512, 2048), jnp.float32),
+            pltpu.VMEM((512, 2048), jnp.float32),
             jax.ShapeDtypeStruct((1, 2048), jnp.float32),
             jax.ShapeDtypeStruct((1, 512), jnp.float32),
         ],
         scratch_shapes=[pltpu.VMEM((512, 128), jnp.float32)],
         compiler_params=PARAMS,
-        cost_estimate=COST,
-    )(x, own, other, first)
+        cost_estimate=cost_of(x),
+    )(x, own, other, before)
 
 
 def weigh_kernel(g_ref, moment_ref, parts_ref, row_ref, state_ref, out_ref, acc_ref, weighed_ref):
@@ -163,7 +183,7 @@
         cost_estimate=pl.CostEstimate(
             flops=4 * 512 * 2048, bytes_accessed=4 << 20, transcendentals=0
         ),
-    )(in_hbm(g), column_moment, column_parts, row_part)
+    )(in_vmem(g), column_moment, column_parts, row_part)
 
 
 def totals_kernel(moment_ref, parts_ref, state_ref, total_ref):
@@ -221,7 +241,7 @@
         cost_estimate=pl.CostEstimate(
             flops=2 * 512 * 2048, bytes_accessed=8 << 20, transcendentals=0
         ),
-    )(in_hbm(g), row_state, column_state, totals)
+    )(in_vmem(g), row_state, column_state, totals)
 
 
 def cyclic(size, stride, shift):
@@ -263,46 +283,48 @@
     low = lax.axis_index("row")
     col = lax.axis_index("col")
     y, high, core = col // 4, col // 2 % 2, col % 2
-    starts = [(low ^ ((y - t) % 4)) * 128 for t in range(4)]
+    places = [low ^ ((y - t) % 4) for t in range(4)]
+    starts = [(place % 2 * 2 + place // 2) * 128 for place in places]
     starts += [high * 64, (1 - high) * 64, core * 32, (1 - core) * 32]
     at = jnp.stack(starts).astype(jnp.int32)
     stage = lax.optimization_barrier
 
-    pair = jnp.concatenate([inputs, swap_row(inputs, 1)])
+    pair = jnp.concatenate([inputs, swap_row(inputs, 2)])
     by_group = stage(jnp.transpose(grad_out, (1, 0, 2)))
     groups = [
         lax.dynamic_index_in_dim(by_group, (me + s) % 4, 0, keepdims=False) for s in range(4)
     ]
     far0 = swap_z(groups[0])
     blocks = [move_x(groups[s], s) for s in (1, 2, 3)]
+    x0 = jnp.concatenate([pair, swap_row(pair, 1)])
     first = jnp.concatenate([groups[0]] + blocks + [far0])
-    first, rest, pair = stage((first, jnp.concatenate(blocks), pair))
+    first, rest, x0 = stage((first, jnp.concatenate(blocks), x0))
 
     far = swap_z(rest)
     first1, first3 = move_y(first, 1), move_y(first, -1)
-    x0 = jnp.concatenate([pair, swap_row(pair, 2)])
-    first1, first3, x0 = stage((first1, first3, x0))
-
+    x1, x3 = move_x(x0, 1), move_x(x0, -1)
+    far, first1, first3, x1, x3 = stage((far, first1, first3, x1, x3))
+
+    far1, far3 = move_y(far, 1), move_y(far, -1)
     first2a, first2b = move_y(first1[0:80], 1), move_y(first3[80:160], -1)
-    x1, x3 = move_x(x0, 1), move_x(x0, -1)
-    first2a, first2b, far, x1, x3 = stage((first2a, first2b, far, x1, x3))
-
-    far1, far3 = move_y(far, 1), move_y(far, -1)
-    own = jnp.concatenate([first, first1, first3, first2a, first2b])
-    other = swap_cores(own)
+    own_a = jnp.concatenate([first, first1, first3])
+    other_a = swap_cores(own_a)
     x2a, x2b = move_x(x1[0:256], 1), move_x(x3[256:512], -1)
-    far1, far3, other, x2a, x2b = stage((far1, far3, other, x2a, x2b))
+    far1, far3, first2a, first2b, other_a, x2a, x2b = stage(
+        (far1, far3, first2a, first2b, other_a, x2a, x2b)
+    )
 
     far2a, far2b = move_y(far1[0:48], 1), move_y(far3[48:96], -1)
-    x_first, x_second = arrange(at, (x0, x1, x2a, x2b, x3))
-    gradient = first_product(x_first, own, other)
-    far2a, far2b, gradient = stage((far2a, far2b, gradient))
-
-    far_own = jnp.concatenate([far, far1, far3, far2a, far2b])
-    far_other = swap_cores(far_own)
-    gradient, column_part, row_part = second_product(
-        x_second, far_own, far_other, gradient
-    )
+    own_b = jnp.concatenate([first2a, first2b, far, far1, far3])
+    other_b = swap_cores(own_b)
+    x_a, x_b, x_c = arrange(at, (x0, x1, x2a, x2b, x3))
+    gradient = product(x_a, own_a, other_a)
+    far2a, far2b, other_b, gradient = stage((far2a, far2b, other_b, gradient))
+
+    own_c = jnp.concatenate([far2a, far2b])
+    other_c = swap_cores(own_c)
+    gradient = product(x_b, own_b, other_b, gradient)
+    gradient, column_part, row_part = last_product(x_c, own_c, other_c, gradient)
     column_state, sums = weigh(
         gradient, column_moment[None], copies(column_part, "col"), row_part
     )

time: 156 us -> 160 us (1.026)
  waiting for transfers between devices: 45.3 us -> 29.8 us
  starting transfers between devices: 35.2 us -> 46.3 us
  blocking collectives: 41.6 us -> 48.3 us
  local copies, waits for them, and re-layouts: 9.86 us -> 14.7 us
  Pallas kernels: 22.2 us -> 18.9 us
    ppermute x2, waiting for transfers between devices: 22.5 us -> 6.39 us  [swap_row(): return lax.ppermute(value, 'row', flipped(4, mask))]
    ppermute x8, waiting for transfers between devices: 0.07 us -> 9.43 us  [move_y(): return lax.ppermute(value, 'col', cyclic(4, 4, shift % 4))]
    all_to_all x3, blocking collectives: 41.6 us -> 48.3 us  [copies(): return lax.all_to_all(rows, axis, 0, 0).reshape(16, value.shape[1])]
    ppermute x2, starting transfers between devices: 7.09 us -> 12.5 us  [swap_z(): return lax.ppermute(value, 'col', flipped(16, 2))]
    ppermute x2, waiting for transfers between devices: 15.5 us -> 10.1 us  [swap_z(): return lax.ppermute(value, 'col', flipped(16, 2))]
    ppermute x2, starting transfers between devices: 0.74 us -> 4.73 us  [swap_row(): return lax.ppermute(value, 'row', flipped(4, mask))]
    unnamed x33 -> x40, local copies, waits for them, and re-layouts: 6.21 us -> 9.39 us
    ppermute x2 -> x3, waiting for transfers between devices: 3.04 us -> 0.01 us  [swap_cores(): return lax.ppermute(value, 'col', flipped(16, 1))]
  transfers between devices with their start and end apart: 21 -> 22, of which waited for: 6 -> 5; matrix products, arithmetic and copies ran while one was open for 4% -> 2% of each run, Pallas kernels for 5% -> 6%
where the time goes in v4:
time: 160 us; the launch traced here: 159 us
  blocking collectives  48.3 us (30%)
  starting transfers between devices  46.3 us (29%)
  waiting for transfers between devices  29.8 us (19%)
  Pallas kernels  18.9 us (12%)
  local copies, waits for them, and re-layouts  14.7 us (9%)
    all_to_all x3, blocking collectives, copies(): return lax.all_to_all(rows, axis, 0, 0).reshape(16, value.shape[1])  48.3 us
    ppermute x2, starting transfers between devices, swap_z(): return lax.ppermute(value, 'col', flipped(16, 2))  12.5 us
    ppermute x7, starting transfers between devices, move_x(): return lax.ppermute(value, 'dp', cyclic(4, 1, shift % 4))  12.4 us
    ppermute x8, starting transfers between devices, move_y(): return lax.ppermute(value, 'col', cyclic(4, 4, shift % 4))  10.9 us
    ppermute x2, waiting for transfers between devices, swap_z(): return lax.ppermute(value, 'col', flipped(16, 2))  10.1 us
    ppermute x8, waiting for transfers between devices, move_y(): return lax.ppermute(value, 'col', cyclic(4, 4, shift % 4))  9.43 us
    unnamed x40, local copies, waits for them, and re-layouts  9.39 us
    pallas_call x2, Pallas kernels, product(): pl.pallas_call(start_kernel if before is None else add_kernel, grid=(2048...  8.57 us
  transfers between devices with their start and end apart: 22, of which 5 were waited for; matrix products, arithmetic and copies ran while one was open for 2% of the time, Pallas kernels for 6%

profile of v4, /device:TPU:1, one launch (start us, length us, event | category | flops | bytes accessed | tf_op | source)
XLA Modules:
  0.0 159.1 jit_solution(15496634975921852931)
XLA Ops:
  2.1 2.1 %collective-permute-start = (bf16[32,2048]{1,0:T(8,128)(2,1)S(1)}, bf16[32,2048]{1,0:T(8,128)(2,1)S(1)}, u32[]{:S(2)}, u32[]{:S(2)}) collective-permute-start(bf16[32,2048]{1,0:T(8,128)(2,1)S(1)} %get-tuple-element.70), channel_id=1, source_target_pairs={{0,64},{64,128},{128,192},{192,0},{1,65},{65,129},{129,193},{193,1... | collective-permute-start | bytes 393224 | tf_op jit(solution)/shard_map/ppermute | solution.py:261
  4.2 2.5 %collective-permute-start.1 = (bf16[32,2048]{1,0:T(8,128)(2,1)S(1)}, bf16[32,2048]{1,0:T(8,128)(2,1)S(1)}, u32[]{:S(2)}, u32[]{:S(2)}) collective-permute-start(bf16[32,2048]{1,0:T(8,128)(2,1)S(1)} %get-tuple-element.69), channel_id=1, source_target_pairs={{0,128},{64,192},{128,0},{192,64},{1,129},{65,193},{129,1},{193,65... | collective-permute-start | bytes 393224 | tf_op jit(solution)/shard_map/ppermute | solution.py:261
  7.8 3.0 %collective-permute-start.4 = (bf16[128,512]{1,0:T(8,128)(2,1)S(1)}, bf16[128,512]{1,0:T(8,128)(2,1)S(1)}, u32[]{:S(2)}, u32[]{:S(2)}) collective-permute-start(bf16[128,512]{1,0:T(8,128)(2,1)S(1)} %copy-done.12), channel_id=1, source_target_pairs={{0,32},{16,48},{32,0},{48,16},{1,33},{17,49},{33,1},{49,17},{2,34}... | collective-permute-start | bytes 393224 | tf_op jit(solution)/shard_map/ppermute | solution.py:269
  10.8 5.2 %collective-permute-start.3 = (bf16[32,2048]{1,0:T(8,128)(2,1)S(1)}, bf16[32,2048]{1,0:T(8,128)(2,1)S(1)}, u32[]{:S(2)}, u32[]{:S(2)}) collective-permute-start(bf16[32,2048]{1,0:T(8,128)(2,1)S(1)} %get-tuple-element.67), channel_id=1, source_target_pairs={{0,2},{1,3},{2,0},{3,1},{4,6},{5,7},{6,4},{7,5},{8,10},{9,11},{10,... | collective-permute-start | bytes 393224 | tf_op jit(solution)/shard_map/ppermute | solution.py:273
  17.9 2.7 %collective-permute-done.3 = bf16[32,2048]{1,0:T(8,128)(2,1)S(1)} collective-permute-done((bf16[32,2048]{1,0:T(8,128)(2,1)S(1)}, bf16[32,2048]{1,0:T(8,128)(2,1)S(1)}, u32[]{:S(2)}, u32[]{:S(2)}) %collective-permute-start.3) | collective-permute-done | bytes 131104 | tf_op jit(solution)/shard_map/ppermute | solution.py:273
  20.7 6.4 %collective-permute-done.5 = bf16[256,512]{1,0:T(8,128)(2,1)S(1)} collective-permute-done((bf16[256,512]{1,0:T(8,128)(2,1)S(1)}, bf16[256,512]{1,0:T(8,128)(2,1)S(1)}, u32[]{:S(2)}, u32[]{:S(2)}) %collective-permute-start.5) | collective-permute-done | bytes 262176 | tf_op jit(solution)/shard_map/ppermute | solution.py:269
  30.0 2.2 %collective-permute-start.10 = (bf16[512,512]{1,0:T(8,128)(2,1)S(1)}, bf16[512,512]{1,0:T(8,128)(2,1)S(1)}, u32[]{:S(2)}, u32[]{:S(2)}) collective-permute-start(bf16[512,512]{1,0:T(8,128)(2,1)S(1)} %pad_maximum_fusion.x0_ref), channel_id=1, source_target_pairs={{0,192},{64,0},{128,64},{192,128},{1,193},{65,1},{129,65},{193,129... | collective-permute-start | bytes 1572872 | tf_op jit(solution)/shard_map/ppermute | solution.py:261
  32.2 7.3 %collective-permute-start.6 = (bf16[96,2048]{1,0:T(8,128)(2,1)S(1)}, bf16[96,2048]{1,0:T(8,128)(2,1)S(1)}, u32[]{:S(2)}, u32[]{:S(2)}) collective-permute-start(bf16[96,2048]{1,0:T(8,128)(2,1)S(1)} %pad_maximum_fusion.1), channel_id=1, source_target_pairs={{0,2},{1,3},{2,0},{3,1},{4,6},{5,7},{6,4},{7,5},{8,10},{9,11},{10,... | collective-permute-start | bytes 1179656 | tf_op jit(solution)/shard_map/ppermute | solution.py:273
  39.6 7.4 %collective-permute-done.6 = bf16[96,2048]{1,0:T(8,128)(2,1)S(1)} collective-permute-done((bf16[96,2048]{1,0:T(8,128)(2,1)S(1)}, bf16[96,2048]{1,0:T(8,128)(2,1)S(1)}, u32[]{:S(2)}, u32[]{:S(2)}) %collective-permute-start.6) | collective-permute-done | bytes 393248 | tf_op jit(solution)/shard_map/ppermute | solution.py:273
  47.2 3.8 %collective-permute-start.15 = (bf16[480,2048]{1,0:T(8,128)(2,1)S(1)}, bf16[480,2048]{1,0:T(8,128)(2,1)S(1)}, u32[]{:S(2)}, u32[]{:S(2)}) collective-permute-start(bf16[480,2048]{1,0:T(8,128)(2,1)S(1)} %constant_dynamic-update-slice_fusion.5.own_ref), channel_id=1, source_target_pairs={{0,1},{1,0},{2,3},{3,2},{4,5},{5,4},{6,7},{7,6},{8,9},{9,8},{10,11... | collective-permute-start | bytes 5898248 | tf_op jit(solution)/shard_map/ppermute | solution.py:257
  51.4 4.0 %collective-permute-start.17 = (bf16[256,512]{1,0:T(8,128)(2,1)S(1)}, bf16[256,512]{1,0:T(8,128)(2,1)S(1)}, u32[]{:S(2)}, u32[]{:S(2)}) collective-permute-start(bf16[256,512]{1,0:T(8,128)(2,1)S(1)} %slice.21), channel_id=1, source_target_pairs={{0,192},{64,0},{128,64},{192,128},{1,193},{65,1},{129,65},{193,129... | collective-permute-start | bytes 786440 | tf_op jit(solution)/shard_map/ppermute | solution.py:261
  55.4 2.7 %collective-permute-start.12 = (bf16[96,2048]{1,0:T(8,128)(2,1)S(1)}, bf16[96,2048]{1,0:T(8,128)(2,1)S(1)}, u32[]{:S(2)}, u32[]{:S(2)}) collective-permute-start(bf16[96,2048]{1,0:T(8,128)(2,1)S(1)} %collective-permute-done.6), channel_id=1, source_target_pairs={{0,12},{1,13},{2,14},{3,15},{4,0},{5,1},{6,2},{7,3},{8,4},{9,5},{1... | collective-permute-start | bytes 1179656 | tf_op jit(solution)/shard_map/ppermute | solution.py:265
  58.2 3.8 %collective-permute-done.16.x2a_ref = bf16[256,512]{1,0:T(8,128)(2,1)S(1)} collective-permute-done((bf16[256,512]{1,0:T(8,128)(2,1)S(1)}, bf16[256,512]{1,0:T(8,128)(2,1)S(1)}, u32[]{:S(2)}, u32[]{:S(2)}) %collective-permute-start.16) | collective-permute-done | bytes 262176 | tf_op jit(solution)/shard_map/ppermute | solution.py:261
  62.0 2.7 %collective-permute-start.14 = (bf16[80,2048]{1,0:T(8,128)(2,1)S(1)}, bf16[80,2048]{1,0:T(8,128)(2,1)S(1)}, u32[]{:S(2)}, u32[]{:S(2)}) collective-permute-start(bf16[80,2048]{1,0:T(8,128)(2,1)S(1)} %slice.19), channel_id=1, source_target_pairs={{0,12},{1,13},{2,14},{3,15},{4,0},{5,1},{6,2},{7,3},{8,4},{9,5},{1... | collective-permute-start | bytes 983048 | tf_op jit(solution)/shard_map/ppermute | solution.py:265
  64.7 9.4 %collective-permute-done.13 = bf16[80,2048]{1,0:T(8,128)(2,1)S(1)} collective-permute-done((bf16[80,2048]{1,0:T(8,128)(2,1)S(1)}, bf16[80,2048]{1,0:T(8,128)(2,1)S(1)}, u32[]{:S(2)}, u32[]{:S(2)}) %collective-permute-start.13) | collective-permute-done | bytes 327712 | tf_op jit(solution)/shard_map/ppermute | solution.py:265
  82.6 2.7 %collective-permute-start.19 = (bf16[48,2048]{1,0:T(8,128)(2,1)}, bf16[48,2048]{1,0:T(8,128)(2,1)}, u32[]{:S(2)}, u32[]{:S(2)}) collective-permute-start(bf16[48,2048]{1,0:T(8,128)(2,1)} %slice.23), channel_id=1, source_target_pairs={{0,12},{1,13},{2,14},{3,15},{4,0},{5,1},{6,2},{7,3},{8,4},{9,5},{1... | collective-permute-start | bytes 589832 | tf_op jit(solution)/shard_map/ppermute | solution.py:265
  88.8 3.6 %shard_map.76.before_ref = f32[512,2048]{1,0:T(8,128)S(1)} custom-call(bf16[512,960]{1,0:T(8,128)(2,1)S(1)} %get-tuple-element.50.x_ref, bf16[480,2048]{1,0:T(8,128)(2,1)S(1)} %constant_dynamic-update-slice_fusion.5.own_ref, bf16[480,2048]{1,0:T(8,128)(2,1)S(1)} %copy-done.1), custom_call_target="tpu_custom_call" | custom-call | flops 2013265920 | bytes 9437184 | tf_op jit(solution)/shard_map/pallas_call | solution.py:125
  95.1 5.0 %shard_map.77.before_ref = f32[512,2048]{1,0:T(8,128)S(1)} custom-call(bf16[512,896]{1,0:T(8,128)(2,1)S(1)} %get-tuple-element.54.x_ref, bf16[448,2048]{1,0:T(8,128)(2,1)} %constant_dynamic-update-slice_fusion.8.own_ref, bf16[448,2048]{1,0:T(8,128)(2,1)} %collective-permute-done.20.other_ref, f32[512,2048]{1,0:T(8,128)S(1)} %shard_map.76.before_ref), custom_call_target="tpu_custom_call" | custom-call | flops 1879048192 | bytes 9437184 | tf_op jit(solution)/shard_map/pallas_call | solution.py:125
  100.1 3.0 %shard_map.78 = (f32[512,2048]{1,0:T(8,128)S(1)}, f32[1,2048]{1,0:T(1,128)S(1)}, f32[1,512]{1,0:T(1,128)S(1)}) custom-call(bf16[512,192]{1,0:T(8,128)(2,1)S(1)} %get-tuple-element.45.x_ref, bf16[96,2048]{1,0:T(8,128)(2,1)S(1)} %constant_dynamic-update-slice_fusion.13.own_ref, bf16[96,2048]{1,0:T(8,128)(2,1)S(1)} %collective-permute-done.21.other_ref, ...), custom_call_target="tpu_custom_call" | custom-call | flops 402653184 | bytes 9437184 | tf_op jit(solution)/shard_map/pallas_call | solution.py:138
  103.2 23.3 %all_to_all.15 = f32[16,1,2048]{2,1,0:T(1,128)S(1)} all-to-all(f32[16,1,2048]{2,1,0:T(1,128)S(1)} %broadcast_in_dim.17), channel_id=1, replica_groups=mesh['dp'=4,'row'=4,'col'=16] {'col'}, dimensions={0} | all-to-all | bytes 262144 | tf_op jit(solution)/shard_map/all_to_all | solution.py:278
  126.5 2.3 %shard_map.79 = (f32[1,2048]{1,0:T(1,128)}, f32[1,1024]{1,0:T(1,128)S(1)}) custom-call(f32[512,2048]{1,0:T(8,128)S(1)} %get-tuple-element.57.g_ref, f32[1,2048]{1,0:T(1,128)S(1)} %bitcast.38, f32[16,2048]{1,0:T(8,128)S(1)} %bitcast.35, f32[1,512]{1,0:T(1,128)S(1)} %get-tuple-element.59.row_ref), custom_call_target="tpu_custom_call" | custom-call | flops 4194304 | bytes 4194304 | tf_op jit(solution)/shard_map/pallas_call | solution.py:169
  128.8 11.1 %all_to_all.16 = f32[16,1,1024]{2,1,0:T(1,128)S(1)} all-to-all(f32[16,1,1024]{2,1,0:T(1,128)S(1)} %broadcast_in_dim.18), channel_id=1, replica_groups=mesh['dp'=4,'row'=4,'col'=16] {'dp','row'}, dimensions={0} | all-to-all | bytes 131072 | tf_op jit(solution)/shard_map/all_to_all | solution.py:278
  140.6 13.9 %all_to_all.17 = f32[16,1,128]{2,1,0:T(1,128)S(1)} all-to-all(f32[16,1,128]{2,1,0:T(1,128)S(1)} %broadcast_in_dim.19), channel_id=1, replica_groups=mesh['dp'=4,'row'=4,'col'=16] {'col'}, dimensions={0} | all-to-all | bytes 16384 | tf_op jit(solution)/shard_map/all_to_all | solution.py:278
  155.9 3.2 %shard_map.81 = (f32[512,2048]{1,0:T(8,128)}, f32[1,1]{1,0:T(1,128)}) custom-call(f32[512,2048]{1,0:T(8,128)S(1)} %get-tuple-element.57.g_ref, f32[1,512]{1,0:T(1,128)S(1)} %copy-done.8, f32[1,2048]{1,0:T(1,128)S(1)} %copy-done.7, f32[16,128]{1,0:T(8,128)S(1)} %bitcast.37), custom_call_target="tpu_custom_call" | custom-call | flops 2097152 | bytes 8388608 | tf_op jit(solution)/shard_map/pallas_call | solution.py:230
  (88 shorter events, 24.8 us)
Async XLA Ops:
  2.1 15.7 %collective-permute-start = (bf16[32,2048]{1,0:T(8,128)(2,1)S(1)}, bf16[32,2048]{1,0:T(8,128)(2,1)S(1)}, u32[]{:S(2)}, u32[]{:S(2)}) collective-permute-start(bf16[32,2048]{1,0:T(8,128)(2,1)S(1)} %get-tuple-element.70), channel_id=1, source_target_pairs={{0,64},{64,128},{128,192},{192,0},{1,65},{65,129},{129,193},{193,1... | collective-permute-start | bytes 393224 | tf_op jit(solution)/shard_map/ppermute | solution.py:261
  4.2 13.6 %collective-permute-start.1 = (bf16[32,2048]{1,0:T(8,128)(2,1)S(1)}, bf16[32,2048]{1,0:T(8,128)(2,1)S(1)}, u32[]{:S(2)}, u32[]{:S(2)}) collective-permute-start(bf16[32,2048]{1,0:T(8,128)(2,1)S(1)} %get-tuple-element.69), channel_id=1, source_target_pairs={{0,128},{64,192},{128,0},{192,64},{1,129},{65,193},{129,1},{193,65... | collective-permute-start | bytes 393224 | tf_op jit(solution)/shard_map/ppermute | solution.py:261
  6.7 11.2 %collective-permute-start.2 = (bf16[32,2048]{1,0:T(8,128)(2,1)S(1)}, bf16[32,2048]{1,0:T(8,128)(2,1)S(1)}, u32[]{:S(2)}, u32[]{:S(2)}) collective-permute-start(bf16[32,2048]{1,0:T(8,128)(2,1)S(1)} %get-tuple-element.68), channel_id=1, source_target_pairs={{0,192},{64,0},{128,64},{192,128},{1,193},{65,1},{129,65},{193,129... | collective-permute-start | bytes 393224 | tf_op jit(solution)/shard_map/ppermute | solution.py:261
  7.8 8.2 %collective-permute-start.4 = (bf16[128,512]{1,0:T(8,128)(2,1)S(1)}, bf16[128,512]{1,0:T(8,128)(2,1)S(1)}, u32[]{:S(2)}, u32[]{:S(2)}) collective-permute-start(bf16[128,512]{1,0:T(8,128)(2,1)S(1)} %copy-done.12), channel_id=1, source_target_pairs={{0,32},{16,48},{32,0},{48,16},{1,33},{17,49},{33,1},{49,17},{2,34}... | collective-permute-start | bytes 393224 | tf_op jit(solution)/shard_map/ppermute | solution.py:269
  10.8 9.8 %collective-permute-start.3 = (bf16[32,2048]{1,0:T(8,128)(2,1)S(1)}, bf16[32,2048]{1,0:T(8,128)(2,1)S(1)}, u32[]{:S(2)}, u32[]{:S(2)}) collective-permute-start(bf16[32,2048]{1,0:T(8,128)(2,1)S(1)} %get-tuple-element.67), channel_id=1, source_target_pairs={{0,2},{1,3},{2,0},{3,1},{4,6},{5,7},{6,4},{7,5},{8,10},{9,11},{10,... | collective-permute-start | bytes 393224 | tf_op jit(solution)/shard_map/ppermute | solution.py:273
  16.1 11.0 %collective-permute-start.5 = (bf16[256,512]{1,0:T(8,128)(2,1)S(1)}, bf16[256,512]{1,0:T(8,128)(2,1)S(1)}, u32[]{:S(2)}, u32[]{:S(2)}) collective-permute-start(bf16[256,512]{1,0:T(8,128)(2,1)S(1)} %pad_maximum_fusion.2), channel_id=1, source_target_pairs={{0,16},{16,0},{32,48},{48,32},{1,17},{17,1},{33,49},{49,33},{2,18}... | collective-permute-start | bytes 786440 | tf_op jit(solution)/shard_map/ppermute | solution.py:269
  27.1 19.9 %collective-permute-start.7 = (bf16[160,2048]{1,0:T(8,128)(2,1)S(1)}, bf16[160,2048]{1,0:T(8,128)(2,1)S(1)}, u32[]{:S(2)}, u32[]{:S(2)}) collective-permute-start(bf16[160,2048]{1,0:T(8,128)(2,1)S(1)} %constant_dynamic-update-slice_fusion), channel_id=1, source_target_pairs={{0,4},{1,5},{2,6},{3,7},{4,8},{5,9},{6,10},{7,11},{8,12},{9,13},{1... | collective-permute-start | bytes 1966088 | tf_op jit(solution)/shard_map/ppermute | solution.py:265
  28.5 18.6 %collective-permute-start.8 = (bf16[160,2048]{1,0:T(8,128)(2,1)S(1)}, bf16[160,2048]{1,0:T(8,128)(2,1)S(1)}, u32[]{:S(2)}, u32[]{:S(2)}) collective-permute-start(bf16[160,2048]{1,0:T(8,128)(2,1)S(1)} %constant_dynamic-update-slice_fusion), channel_id=1, source_target_pairs={{0,12},{1,13},{2,14},{3,15},{4,0},{5,1},{6,2},{7,3},{8,4},{9,5},{1... | collective-permute-start | bytes 1966088 | tf_op jit(solution)/shard_map/ppermute | solution.py:265
  30.0 17.0 %collective-permute-start.10 = (bf16[512,512]{1,0:T(8,128)(2,1)S(1)}, bf16[512,512]{1,0:T(8,128)(2,1)S(1)}, u32[]{:S(2)}, u32[]{:S(2)}) collective-permute-start(bf16[512,512]{1,0:T(8,128)(2,1)S(1)} %pad_maximum_fusion.x0_ref), channel_id=1, source_target_pairs={{0,192},{64,0},{128,64},{192,128},{1,193},{65,1},{129,65},{193,129... | collective-permute-start | bytes 1572872 | tf_op jit(solution)/shard_map/ppermute | solution.py:261
  32.2 14.8 %collective-permute-start.9 = (bf16[512,512]{1,0:T(8,128)(2,1)S(1)}, bf16[512,512]{1,0:T(8,128)(2,1)S(1)}, u32[]{:S(2)}, u32[]{:S(2)}) collective-permute-start(bf16[512,512]{1,0:T(8,128)(2,1)S(1)} %pad_maximum_fusion.x0_ref), channel_id=1, source_target_pairs={{0,64},{64,128},{128,192},{192,0},{1,65},{65,129},{129,193},{193,1... | collective-permute-start | bytes 1572872 | tf_op jit(solution)/shard_map/ppermute | solution.py:261
  32.2 14.8 %collective-permute-start.6 = (bf16[96,2048]{1,0:T(8,128)(2,1)S(1)}, bf16[96,2048]{1,0:T(8,128)(2,1)S(1)}, u32[]{:S(2)}, u32[]{:S(2)}) collective-permute-start(bf16[96,2048]{1,0:T(8,128)(2,1)S(1)} %pad_maximum_fusion.1), channel_id=1, source_target_pairs={{0,2},{1,3},{2,0},{3,1},{4,6},{5,7},{6,4},{7,5},{8,10},{9,11},{10,... | collective-permute-start | bytes 1179656 | tf_op jit(solution)/shard_map/ppermute | solution.py:273
  47.2 26.9 %collective-permute-start.15 = (bf16[480,2048]{1,0:T(8,128)(2,1)S(1)}, bf16[480,2048]{1,0:T(8,128)(2,1)S(1)}, u32[]{:S(2)}, u32[]{:S(2)}) collective-permute-start(bf16[480,2048]{1,0:T(8,128)(2,1)S(1)} %constant_dynamic-update-slice_fusion.5.own_ref), channel_id=1, source_target_pairs={{0,1},{1,0},{2,3},{3,2},{4,5},{5,4},{6,7},{7,6},{8,9},{9,8},{10,11... | collective-permute-start | bytes 5898248 | tf_op jit(solution)/shard_map/ppermute | solution.py:257
  51.0 11.0 %collective-permute-start.16 = (bf16[256,512]{1,0:T(8,128)(2,1)S(1)}, bf16[256,512]{1,0:T(8,128)(2,1)S(1)}, u32[]{:S(2)}, u32[]{:S(2)}) collective-permute-start(bf16[256,512]{1,0:T(8,128)(2,1)S(1)} %slice.20), channel_id=1, source_target_pairs={{0,64},{64,128},{128,192},{192,0},{1,65},{65,129},{129,193},{193,1... | collective-permute-start | bytes 786440 | tf_op jit(solution)/shard_map/ppermute | solution.py:261
  51.4 10.6 %collective-permute-start.17 = (bf16[256,512]{1,0:T(8,128)(2,1)S(1)}, bf16[256,512]{1,0:T(8,128)(2,1)S(1)}, u32[]{:S(2)}, u32[]{:S(2)}) collective-permute-start(bf16[256,512]{1,0:T(8,128)(2,1)S(1)} %slice.21), channel_id=1, source_target_pairs={{0,192},{64,0},{128,64},{192,128},{1,193},{65,1},{129,65},{193,129... | collective-permute-start | bytes 786440 | tf_op jit(solution)/shard_map/ppermute | solution.py:261
  55.4 18.6 %collective-permute-start.11 = (bf16[96,2048]{1,0:T(8,128)(2,1)S(1)}, bf16[96,2048]{1,0:T(8,128)(2,1)S(1)}, u32[]{:S(2)}, u32[]{:S(2)}) collective-permute-start(bf16[96,2048]{1,0:T(8,128)(2,1)S(1)} %collective-permute-done.6), channel_id=1, source_target_pairs={{0,4},{1,5},{2,6},{3,7},{4,8},{5,9},{6,10},{7,11},{8,12},{9,13},{1... | collective-permute-start | bytes 1179656 | tf_op jit(solution)/shard_map/ppermute | solution.py:265
  55.4 18.7 %collective-permute-start.12 = (bf16[96,2048]{1,0:T(8,128)(2,1)S(1)}, bf16[96,2048]{1,0:T(8,128)(2,1)S(1)}, u32[]{:S(2)}, u32[]{:S(2)}) collective-permute-start(bf16[96,2048]{1,0:T(8,128)(2,1)S(1)} %collective-permute-done.6), channel_id=1, source_target_pairs={{0,12},{1,13},{2,14},{3,15},{4,0},{5,1},{6,2},{7,3},{8,4},{9,5},{1... | collective-permute-start | bytes 1179656 | tf_op jit(solution)/shard_map/ppermute | solution.py:265
  62.0 16.2 %copy-start.2 = (bf16[256,512]{1,0:T(8,128)(2,1)}, bf16[256,512]{1,0:T(8,128)(2,1)S(1)}, u32[]{:S(2)}) copy-start(bf16[256,512]{1,0:T(8,128)(2,1)S(1)} %collective-permute-done.16.x2a_ref) | copy-start | bytes 786436
  62.0 12.1 %collective-permute-start.13 = (bf16[80,2048]{1,0:T(8,128)(2,1)S(1)}, bf16[80,2048]{1,0:T(8,128)(2,1)S(1)}, u32[]{:S(2)}, u32[]{:S(2)}) collective-permute-start(bf16[80,2048]{1,0:T(8,128)(2,1)S(1)} %slice.18), channel_id=1, source_target_pairs={{0,4},{1,5},{2,6},{3,7},{4,8},{5,9},{6,10},{7,11},{8,12},{9,13},{1... | collective-permute-start | bytes 983048 | tf_op jit(solution)/shard_map/ppermute | solution.py:265
  62.0 12.1 %collective-permute-start.14 = (bf16[80,2048]{1,0:T(8,128)(2,1)S(1)}, bf16[80,2048]{1,0:T(8,128)(2,1)S(1)}, u32[]{:S(2)}, u32[]{:S(2)}) collective-permute-start(bf16[80,2048]{1,0:T(8,128)(2,1)S(1)} %slice.19), channel_id=1, source_target_pairs={{0,12},{1,13},{2,14},{3,15},{4,0},{5,1},{6,2},{7,3},{8,4},{9,5},{1... | collective-permute-start | bytes 983048 | tf_op jit(solution)/shard_map/ppermute | solution.py:265
  78.2 14.3 %collective-permute-start.20 = (bf16[448,2048]{1,0:T(8,128)(2,1)}, bf16[448,2048]{1,0:T(8,128)(2,1)}, u32[]{:S(2)}, u32[]{:S(2)}) collective-permute-start(bf16[448,2048]{1,0:T(8,128)(2,1)} %constant_dynamic-update-slice_fusion.8.own_ref), channel_id=1, source_target_pairs={{0,1},{1,0},{2,3},{3,2},{4,5},{5,4},{6,7},{7,6},{8,9},{9,8},{10,11... | collective-permute-start | bytes 5505032 | tf_op jit(solution)/shard_map/ppermute | solution.py:257
  82.6 9.8 %collective-permute-start.18 = (bf16[48,2048]{1,0:T(8,128)(2,1)}, bf16[48,2048]{1,0:T(8,128)(2,1)}, u32[]{:S(2)}, u32[]{:S(2)}) collective-permute-start(bf16[48,2048]{1,0:T(8,128)(2,1)} %slice.22), channel_id=1, source_target_pairs={{0,4},{1,5},{2,6},{3,7},{4,8},{5,9},{6,10},{7,11},{8,12},{9,13},{1... | collective-permute-start | bytes 589832 | tf_op jit(solution)/shard_map/ppermute | solution.py:265
  82.6 9.8 %collective-permute-start.19 = (bf16[48,2048]{1,0:T(8,128)(2,1)}, bf16[48,2048]{1,0:T(8,128)(2,1)}, u32[]{:S(2)}, u32[]{:S(2)}) collective-permute-start(bf16[48,2048]{1,0:T(8,128)(2,1)} %slice.23), channel_id=1, source_target_pairs={{0,12},{1,13},{2,14},{3,15},{4,0},{5,1},{6,2},{7,3},{8,4},{9,5},{1... | collective-permute-start | bytes 589832 | tf_op jit(solution)/shard_map/ppermute | solution.py:265
  94.4 5.7 %collective-permute-start.21 = (bf16[96,2048]{1,0:T(8,128)(2,1)S(1)}, bf16[96,2048]{1,0:T(8,128)(2,1)S(1)}, u32[]{:S(2)}, u32[]{:S(2)}) collective-permute-start(bf16[96,2048]{1,0:T(8,128)(2,1)S(1)} %constant_dynamic-update-slice_fusion.13.own_ref), channel_id=1, source_target_pairs={{0,1},{1,0},{2,3},{3,2},{4,5},{5,4},{6,7},{7,6},{8,9},{9,8},{10,11... | collective-permute-start | bytes 1179656 | tf_op jit(solution)/shard_map/ppermute | solution.py:257
  100.0 26.5 %copy-start.6 = (f32[2048]{0:T(1024)S(1)}, f32[2048]{0:T(1024)}, u32[]{:S(2)}) copy-start(f32[2048]{0:T(1024)} %param.7) | copy-start | bytes 24580
  (11 other events, 53.9 us)

commit v5 on v3

--- a/solution.py
+++ b/solution.py
@@ -7,49 +7,41 @@
 
 D = 8192
 FF = 32768
-VMEM_LIMIT = 18 * 1024 * 1024
+VMEM_LIMIT = 20 * 1024 * 1024
 COLS = 512
-PLACES = (0, 1, 3, 2)
-FIRST = [(s, t, far) for t in PLACES for s, far in ((0, 0), (1, 0), (2, 0), (3, 0), (0, 1))]
-SECOND = [(s, t, 1) for t in PLACES for s in (1, 2, 3)]
-
-
-def arrange_kernel(at_ref, x0_ref, x1_ref, x2a_ref, x2b_ref, x3_ref, first_ref, second_ref, x2_ref):
-    half = x2a_ref.shape[0]
-    x2_ref[0:half, :] = x2a_ref[...]
-    x2_ref[half:, :] = x2b_ref[...]
-    pieces = (x0_ref, x1_ref, x2_ref, x3_ref)
-
-    for order, out_ref in ((FIRST, first_ref), (SECOND, second_ref)):
-        blocks = [block + (other,) for other in (0, 1) for block in order]
-        for k in range(len(blocks) // 4):
-            rows = []
-            for s, t, far, other in blocks[4 * k : 4 * k + 4]:
-                start = pl.multiple_of(at_ref[t] + at_ref[4 + far] + at_ref[6 + other], 32)
-                rows.append(pieces[s][pl.ds(start, 32), :])
-            out_ref[:, k * 128 : (k + 1) * 128] = jnp.concatenate(rows, axis=0).T
-
-
-def arrange(at, pieces):
+REPLICAS = (0, 1, 2, 3)
+
+
+def arrange_kernel(at_ref, even_ref, odd_ref, near_ref, far_ref):
+    for far, out_ref in ((0, near_ref), (1, far_ref)):
+        for other in (0, 1):
+            for t in range(4):
+                start = at_ref[t] + at_ref[4 + far] + at_ref[6 + other]
+                rows = []
+                for s in REPLICAS:
+                    piece = odd_ref if s % 2 else even_ref
+                    place = pl.multiple_of(start + s // 2 * 512, 32)
+                    rows.append(piece[pl.ds(place, 32), :])
+                column = other * 512 + t * 128
+                out_ref[:, column : column + 128] = jnp.concatenate(rows, axis=0).T
+
+
+def arrange(at, even, odd):
     whole = pl.BlockSpec(memory_space=pltpu.VMEM)
     return pl.pallas_call(
         arrange_kernel,
-        in_specs=[pl.BlockSpec(memory_space=pltpu.SMEM)] + [whole] * 5,
+        in_specs=[pl.BlockSpec(memory_space=pltpu.SMEM), whole, whole],
         out_specs=[whole] * 2,
-        out_shape=[
-            jax.ShapeDtypeStruct((512, 1280), jnp.bfloat16),
-            jax.ShapeDtypeStruct((512, 768), jnp.bfloat16),
-        ],
-        scratch_shapes=[pltpu.VMEM((512, 512), jnp.bfloat16)],
+        out_shape=[jax.ShapeDtypeStruct((512, 1024), jnp.bfloat16)] * 2,
         compiler_params=PARAMS,
         cost_estimate=pl.CostEstimate(flops=0, bytes_accessed=4 << 20, transcendentals=0),
-    )(at, *pieces)
-
-
-def first_kernel(x_ref, own_ref, other_ref, out_ref):
+    )(at, even, odd)
+
+
+def near_kernel(x_ref, own_ref, other_ref, out_ref):
     out_ref[...] = jnp.dot(
-        x_ref[:, 0:640], own_ref[...], preferred_element_type=jnp.float32
-    ) + jnp.dot(x_ref[:, 640:1280], other_ref[...], preferred_element_type=jnp.float32)
+        x_ref[:, 0:512], own_ref[...], preferred_element_type=jnp.float32
+    ) + jnp.dot(x_ref[:, 512:1024], other_ref[...], preferred_element_type=jnp.float32)
 
 
 def across(value):
@@ -73,12 +65,13 @@
         row_ref[...] = jnp.sum(acc_ref[...].T, axis=0, keepdims=True)
 
 
-def second_kernel(
-    x_ref, own_ref, other_ref, first_ref, out_ref, col_ref, row_ref, acc_ref
-):
-    value = first_ref[...]
-    value += jnp.dot(x_ref[:, 0:384], own_ref[...], preferred_element_type=jnp.float32)
-    value += jnp.dot(x_ref[:, 384:768], other_ref[...], preferred_element_type=jnp.float32)
+def far_kernel(x_ref, *refs):
+    blocks, (near_ref, out_ref, col_ref, row_ref, acc_ref) = refs[:8], refs[8:]
+    value = near_ref[...]
+    for half in (0, 1):
+        g = jnp.concatenate([ref[...] for ref in blocks[4 * half : 4 * half + 4]], axis=0)
+        x = x_ref[:, 512 * half : 512 * half + 512]
+        value += jnp.dot(x, g, preferred_element_type=jnp.float32)
     out_ref[...] = value
     squares = value * value + 1e-30
     col_ref[...] = jnp.sum(squares, axis=0, keepdims=True)
@@ -93,20 +86,22 @@
     return pl.BlockSpec((rows, COLS), lambda j: (0, j))
 
 
-def in_hbm(value):
-    return pltpu.with_memory_space_constraint(value, pltpu.HBM)
+def in_vmem(value):
+    return pltpu.with_memory_space_constraint(value, pltpu.VMEM)
 
 
 G_SPEC = moving(512)
 PARAMS = pltpu.CompilerParams(vmem_limit_bytes=VMEM_LIMIT)
+
+
 COST = pl.CostEstimate(flops=2 * 512 * 1024 * 2048, bytes_accessed=9 << 20, transcendentals=0)
 
 
-def first_product(x, own, other):
-    return pl.pallas_call(
-        first_kernel,
+def near_product(x, own, other):
+    return pl.pallas_call(
+        near_kernel,
         grid=(2048 // COLS,),
-        in_specs=[fixed(512, 1280), moving(640), moving(640)],
+        in_specs=[fixed(512, 1024), moving(512), moving(512)],
         out_specs=G_SPEC,
         out_shape=jax.ShapeDtypeStruct((512, 2048), jnp.float32),
         compiler_params=PARAMS,
@@ -114,21 +109,21 @@
     )(x, own, other)
 
 
-def second_product(x, own, other, first):
-    return pl.pallas_call(
-        second_kernel,
+def far_product(x, blocks, near):
+    return pl.pallas_call(
+        far_kernel,
         grid=(2048 // COLS,),
-        in_specs=[fixed(512, 768), moving(384), moving(384), G_SPEC],
+        in_specs=[fixed(512, 1024)] + [moving(128)] * 8 + [G_SPEC],
         out_specs=[G_SPEC, moving(1), fixed(1, 512)],
         out_shape=[
-            pltpu.HBM((512, 2048), jnp.float32),
+            pltpu.VMEM((512, 2048), jnp.float32),
             jax.ShapeDtypeStruct((1, 2048), jnp.float32),
             jax.ShapeDtypeStruct((1, 512), jnp.float32),
         ],
         scratch_shapes=[pltpu.VMEM((512, 128), jnp.float32)],
         compiler_params=PARAMS,
         cost_estimate=COST,
-    )(x, own, other, first)
+    )(x, *blocks, near)
 
 
 def weigh_kernel(g_ref, moment_ref, parts_ref, row_ref, state_ref, out_ref, acc_ref, weighed_ref):
@@ -163,7 +158,7 @@
         cost_estimate=pl.CostEstimate(
             flops=4 * 512 * 2048, bytes_accessed=4 << 20, transcendentals=0
         ),
-    )(in_hbm(g), column_moment, column_parts, row_part)
+    )(in_vmem(g), column_moment, column_parts, row_part)
 
 
 def totals_kernel(moment_ref, parts_ref, state_ref, total_ref):
@@ -221,7 +216,7 @@
         cost_estimate=pl.CostEstimate(
             flops=2 * 512 * 2048, bytes_accessed=8 << 20, transcendentals=0
         ),
-    )(in_hbm(g), row_state, column_state, totals)
+    )(in_vmem(g), row_state, column_state, totals)
 
 
 def cyclic(size, stride, shift):
@@ -237,8 +232,8 @@
     return lax.ppermute(value, "col", flipped(16, 1))
 
 
-def move_x(value, shift):
-    return lax.ppermute(value, "dp", cyclic(4, 1, shift % 4))
+def swap_x(value, mask):
+    return lax.ppermute(value, "dp", flipped(4, mask))
 
 
 def move_y(value, shift):
@@ -263,46 +258,37 @@
     low = lax.axis_index("row")
     col = lax.axis_index("col")
     y, high, core = col // 4, col // 2 % 2, col % 2
-    starts = [(low ^ ((y - t) % 4)) * 128 for t in range(4)]
+    places = [low ^ ((y - t) % 4) for t in range(4)]
+    starts = [(place % 2 * 2 + place // 2) * 128 for place in places]
     starts += [high * 64, (1 - high) * 64, core * 32, (1 - core) * 32]
     at = jnp.stack(starts).astype(jnp.int32)
     stage = lax.optimization_barrier
 
-    pair = jnp.concatenate([inputs, swap_row(inputs, 1)])
+    pair = jnp.concatenate([inputs, swap_row(inputs, 2)])
     by_group = stage(jnp.transpose(grad_out, (1, 0, 2)))
     groups = [
-        lax.dynamic_index_in_dim(by_group, (me + s) % 4, 0, keepdims=False) for s in range(4)
+        lax.dynamic_index_in_dim(by_group, me ^ s, 0, keepdims=False) for s in REPLICAS
     ]
-    far0 = swap_z(groups[0])
-    blocks = [move_x(groups[s], s) for s in (1, 2, 3)]
-    first = jnp.concatenate([groups[0]] + blocks + [far0])
-    first, rest, pair = stage((first, jnp.concatenate(blocks), pair))
-
-    far = swap_z(rest)
-    first1, first3 = move_y(first, 1), move_y(first, -1)
-    x0 = jnp.concatenate([pair, swap_row(pair, 2)])
-    first1, first3, x0 = stage((first1, first3, x0))
-
-    first2a, first2b = move_y(first1[0:80], 1), move_y(first3[80:160], -1)
-    x1, x3 = move_x(x0, 1), move_x(x0, -1)
-    first2a, first2b, far, x1, x3 = stage((first2a, first2b, far, x1, x3))
-
-    far1, far3 = move_y(far, 1), move_y(far, -1)
-    own = jnp.concatenate([first, first1, first3, first2a, first2b])
+    blocks = [groups[0]] + [swap_x(groups[s], s) for s in (1, 2, 3)]
+    x0 = jnp.concatenate([pair, swap_row(pair, 1)])
+    near, x0 = stage((jnp.concatenate(blocks), x0))
+
+    even = jnp.concatenate([x0, swap_x(x0, 2)])
+    far = swap_z(near)
+    nears = [move_y(near, t) for t in (1, 2, 3)]
+    far, even, *nears = stage((far, even, *nears))
+
+    own = jnp.concatenate([near, *nears])
     other = swap_cores(own)
-    x2a, x2b = move_x(x1[0:256], 1), move_x(x3[256:512], -1)
-    far1, far3, other, x2a, x2b = stage((far1, far3, other, x2a, x2b))
-
-    far2a, far2b = move_y(far1[0:48], 1), move_y(far3[48:96], -1)
-    x_first, x_second = arrange(at, (x0, x1, x2a, x2b, x3))
-    gradient = first_product(x_first, own, other)
-    far2a, far2b, gradient = stage((far2a, far2b, gradient))
-
-    far_own = jnp.concatenate([far, far1, far3, far2a, far2b])
-    far_other = swap_cores(far_own)
-    gradient, column_part, row_part = second_product(
-        x_second, far_own, far_other, gradient
-    )
+    odd = swap_x(even, 1)
+    fars = [move_y(far, t) for t in (1, 2, 3)]
+    other, odd, *fars = stage((other, odd, *fars))
+
+    fars = [far, *fars]
+    others = [swap_cores(block) for block in fars]
+    x_near, x_far = arrange(at, even, odd)
+    gradient = near_product(x_near, own, other)
+    gradient, column_part, row_part = far_product(x_far, fars + others, gradient)
     column_state, sums = weigh(
         gradient, column_moment[None], copies(column_part, "col"), row_part
     )

time: 156 us -> 151 us (0.968)
  starting transfers between devices: 35.2 us -> 45.3 us
  waiting for transfers between devices: 45.3 us -> 37.1 us
  Pallas kernels: 22.2 us -> 16.2 us
  local copies, waits for them, and re-layouts: 9.86 us -> 7.05 us
  blocking collectives: 41.6 us -> 43.8 us
    ppermute x8 -> x6, waiting for transfers between devices: 0.07 us -> 32.2 us  [move_y(): return lax.ppermute(value, 'col', cyclic(4, 4, shift % 4))]
    ppermute x2, waiting for transfers between devices: 22.5 us -> 2.94 us  [swap_row(): return lax.ppermute(value, 'row', flipped(4, mask))]
    ppermute x2 -> x1, waiting for transfers between devices: 15.5 us -> 0.01 us  [swap_z(): return lax.ppermute(value, 'col', flipped(16, 2))]
    ppermute x2 -> x5, starting transfers between devices: 4.97 us -> 17.7 us  [swap_cores(): return lax.ppermute(value, 'col', flipped(16, 1))]
    ppermute x2, starting transfers between devices: 0.74 us -> 6.77 us  [swap_row(): return lax.ppermute(value, 'row', flipped(4, mask))]
    ppermute x7 -> x5, starting transfers between devices: 11.2 us -> 6.81 us  [swap_x(): return lax.ppermute(value, 'dp', flipped(4, mask))]
    ppermute x8 -> x6, starting transfers between devices: 11.2 us -> 7.17 us  [move_y(): return lax.ppermute(value, 'col', cyclic(4, 4, shift % 4))]
    slice x6 -> x0, local copies, waits for them, and re-layouts: 3.38 us -> none  [the longest x2 1.88 us: per_device(): far2a, far2b = (move_y(far1[0:48], 1), move_y(far3[48:96], -1))]
  transfers between devices with their start and end apart: 21 -> 19, of which waited for: 6 -> 9; matrix products, arithmetic and copies ran while one was open for 4% -> 1% of each run, Pallas kernels for 5% -> 3%
where the time goes in v5:
time: 151 us; the launch traced here: 150 us
  starting transfers between devices  45.3 us (30%)
  blocking collectives  43.8 us (29%)
  waiting for transfers between devices  37.1 us (25%)
  Pallas kernels  16.2 us (11%)
  local copies, waits for them, and re-layouts  7.05 us (5%)
    all_to_all x3, blocking collectives, copies(): return lax.all_to_all(rows, axis, 0, 0).reshape(16, value.shape[1])  43.8 us
    ppermute x6, waiting for transfers between devices, move_y(): return lax.ppermute(value, 'col', cyclic(4, 4, shift % 4))  32.2 us
    ppermute x5, starting transfers between devices, swap_cores(): return lax.ppermute(value, 'col', flipped(16, 1))  17.7 us
    ppermute x6, starting transfers between devices, move_y(): return lax.ppermute(value, 'col', cyclic(4, 4, shift % 4))  7.17 us
    ppermute x1, starting transfers between devices, swap_z(): return lax.ppermute(value, 'col', flipped(16, 2))  6.82 us
    ppermute x5, starting transfers between devices, swap_x(): return lax.ppermute(value, 'dp', flipped(4, mask))  6.81 us
    unnamed x24, local copies, waits for them, and re-layouts  6.77 us
    ppermute x2, starting transfers between devices, swap_row(): return lax.ppermute(value, 'row', flipped(4, mask))  6.77 us
  transfers between devices with their start and end apart: 19, of which 9 were waited for; matrix products, arithmetic and copies ran while one was open for 1% of the time, Pallas kernels for 3%

profile of v5, /device:TPU:1, one launch (start us, length us, event | category | flops | bytes accessed | tf_op | source)
XLA Modules:
  0.0 150.4 jit_solution(3360848626214238908)
XLA Ops:
  0.6 3.9 %collective-permute-start.3 = (bf16[128,512]{1,0:T(8,128)(2,1)}, bf16[128,512]{1,0:T(8,128)(2,1)S(1)}, u32[]{:S(2)}, u32[]{:S(2)}) collective-permute-start(bf16[128,512]{1,0:T(8,128)(2,1)} %param.4), channel_id=1, source_target_pairs={{0,32},{16,48},{32,0},{48,16},{1,33},{17,49},{33,1},{49,17},{2,34}... | collective-permute-start | bytes 393224 | tf_op jit(solution)/shard_map/ppermute | solution.py:244
  4.5 1.3 copy.15
  6.0 2.6 %collective-permute-start.2 = (bf16[32,2048]{1,0:T(8,128)(2,1)S(1)}, bf16[32,2048]{1,0:T(8,128)(2,1)S(1)}, u32[]{:S(2)}, u32[]{:S(2)}) collective-permute-start(bf16[32,2048]{1,0:T(8,128)(2,1)S(1)} %get-tuple-element.51), channel_id=1, source_target_pairs={{0,192},{64,128},{128,64},{192,0},{1,193},{65,129},{129,65},{193,1... | collective-permute-start | bytes 393224 | tf_op jit(solution)/shard_map/ppermute | solution.py:236
  9.3 2.9 %collective-permute-start.4 = (bf16[256,512]{1,0:T(8,128)(2,1)S(1)}, bf16[256,512]{1,0:T(8,128)(2,1)S(1)}, u32[]{:S(2)}, u32[]{:S(2)}) collective-permute-start(bf16[256,512]{1,0:T(8,128)(2,1)S(1)} %pad_maximum_fusion.3), channel_id=1, source_target_pairs={{0,16},{16,0},{32,48},{48,32},{1,17},{17,1},{33,49},{49,33},{2,18}... | collective-permute-start | bytes 786440 | tf_op jit(solution)/shard_map/ppermute | solution.py:244
  14.2 2.9 %collective-permute-done.4 = bf16[256,512]{1,0:T(8,128)(2,1)S(1)} collective-permute-done((bf16[256,512]{1,0:T(8,128)(2,1)S(1)}, bf16[256,512]{1,0:T(8,128)(2,1)S(1)}, u32[]{:S(2)}, u32[]{:S(2)}) %collective-permute-start.4) | collective-permute-done | bytes 262176 | tf_op jit(solution)/shard_map/ppermute | solution.py:244
  17.2 3.1 %collective-permute-start.6 = (bf16[512,512]{1,0:T(8,128)(2,1)S(1)}, bf16[512,512]{1,0:T(8,128)(2,1)S(1)}, u32[]{:S(2)}, u32[]{:S(2)}) collective-permute-start(bf16[512,512]{1,0:T(8,128)(2,1)S(1)} %pad_maximum_fusion.2), channel_id=1, source_target_pairs={{0,128},{64,192},{128,0},{192,64},{1,129},{65,193},{129,1},{193,65... | collective-permute-start | bytes 1572872 | tf_op jit(solution)/shard_map/ppermute | solution.py:236
  20.3 2.7 %collective-permute-start.9 = (bf16[128,2048]{1,0:T(8,128)(2,1)S(1)}, bf16[128,2048]{1,0:T(8,128)(2,1)S(1)}, u32[]{:S(2)}, u32[]{:S(2)}) collective-permute-start(bf16[128,2048]{1,0:T(8,128)(2,1)S(1)} %pad_maximum_fusion.1), channel_id=1, source_target_pairs={{0,12},{1,13},{2,14},{3,15},{4,0},{5,1},{6,2},{7,3},{8,4},{9,5},{1... | collective-permute-start | bytes 1572872 | tf_op jit(solution)/shard_map/ppermute | solution.py:240
  24.1 6.8 %collective-permute-start.5 = (bf16[128,2048]{1,0:T(8,128)(2,1)S(1)}, bf16[128,2048]{1,0:T(8,128)(2,1)}, u32[]{:S(2)}, u32[]{:S(2)}) collective-permute-start(bf16[128,2048]{1,0:T(8,128)(2,1)S(1)} %pad_maximum_fusion.1), channel_id=1, source_target_pairs={{0,2},{1,3},{2,0},{3,1},{4,6},{5,7},{6,4},{7,5},{8,10},{9,11},{10,... | collective-permute-start | bytes 1572872 | tf_op jit(solution)/shard_map/ppermute | solution.py:248
  31.1 1.8 %collective-permute-done.9 = bf16[128,2048]{1,0:T(8,128)(2,1)S(1)} collective-permute-done((bf16[128,2048]{1,0:T(8,128)(2,1)S(1)}, bf16[128,2048]{1,0:T(8,128)(2,1)S(1)}, u32[]{:S(2)}, u32[]{:S(2)}) %collective-permute-start.9) | collective-permute-done | bytes 524320 | tf_op jit(solution)/shard_map/ppermute | solution.py:240
  32.9 2.5 %collective-permute-done.8 = bf16[128,2048]{1,0:T(8,128)(2,1)S(1)} collective-permute-done((bf16[128,2048]{1,0:T(8,128)(2,1)S(1)}, bf16[128,2048]{1,0:T(8,128)(2,1)S(1)}, u32[]{:S(2)}, u32[]{:S(2)}) %collective-permute-start.8) | collective-permute-done | bytes 524320 | tf_op jit(solution)/shard_map/ppermute | solution.py:240
  35.4 14.3 %collective-permute-done.7 = bf16[128,2048]{1,0:T(8,128)(2,1)S(1)} collective-permute-done((bf16[128,2048]{1,0:T(8,128)(2,1)S(1)}, bf16[128,2048]{1,0:T(8,128)(2,1)S(1)}, u32[]{:S(2)}, u32[]{:S(2)}) %collective-permute-start.7) | collective-permute-done | bytes 524320 | tf_op jit(solution)/shard_map/ppermute | solution.py:240
  49.8 4.8 %collective-permute-start.10 = (bf16[512,2048]{1,0:T(8,128)(2,1)S(1)}, bf16[512,2048]{1,0:T(8,128)(2,1)S(1)}, u32[]{:S(2)}, u32[]{:S(2)}) collective-permute-start(bf16[512,2048]{1,0:T(8,128)(2,1)S(1)} %constant_dynamic-update-slice_fusion.own_ref), channel_id=1, source_target_pairs={{0,1},{1,0},{2,3},{3,2},{4,5},{5,4},{6,7},{7,6},{8,9},{9,8},{10,11... | collective-permute-start | bytes 6291464 | tf_op jit(solution)/shard_map/ppermute | solution.py:232
  54.9 2.0 %collective-permute-start.14 = (bf16[128,2048]{1,0:T(8,128)(2,1)}, bf16[128,2048]{1,0:T(8,128)(2,1)}, u32[]{:S(2)}, u32[]{:S(2)}) collective-permute-start(bf16[128,2048]{1,0:T(8,128)(2,1)} %collective-permute-done.5.refs_0_), channel_id=1, source_target_pairs={{0,12},{1,13},{2,14},{3,15},{4,0},{5,1},{6,2},{7,3},{8,4},{9,5},{1... | collective-permute-start | bytes 1572872 | tf_op jit(solution)/shard_map/ppermute | solution.py:240
  56.9 1.4 collective-permute-start.13
  58.3 10.4 %collective-permute-done.14.refs_3_ = bf16[128,2048]{1,0:T(8,128)(2,1)} collective-permute-done((bf16[128,2048]{1,0:T(8,128)(2,1)}, bf16[128,2048]{1,0:T(8,128)(2,1)}, u32[]{:S(2)}, u32[]{:S(2)}) %collective-permute-start.14) | collective-permute-done | bytes 524320 | tf_op jit(solution)/shard_map/ppermute | solution.py:240
  68.7 11.9 %collective-permute-start.15 = (bf16[128,2048]{1,0:T(8,128)(2,1)}, bf16[128,2048]{1,0:T(8,128)(2,1)}, u32[]{:S(2)}, u32[]{:S(2)}) collective-permute-start(bf16[128,2048]{1,0:T(8,128)(2,1)} %collective-permute-done.5.refs_0_), channel_id=1, source_target_pairs={{0,1},{1,0},{2,3},{3,2},{4,5},{5,4},{6,7},{7,6},{8,9},{9,8},{10,11... | collective-permute-start | bytes 1572872 | tf_op jit(solution)/shard_map/ppermute | solution.py:232
  80.6 3.2 %collective-permute-done.12.refs_1_ = bf16[128,2048]{1,0:T(8,128)(2,1)} collective-permute-done((bf16[128,2048]{1,0:T(8,128)(2,1)}, bf16[128,2048]{1,0:T(8,128)(2,1)}, u32[]{:S(2)}, u32[]{:S(2)}) %collective-permute-start.12) | collective-permute-done | bytes 524320 | tf_op jit(solution)/shard_map/ppermute | solution.py:240
  90.0 3.5 %shard_map.76.refs_8_ = f32[512,2048]{1,0:T(8,128)S(1)} custom-call(bf16[512,1024]{1,0:T(8,128)(2,1)S(1)} %get-tuple-element.39.x_ref, bf16[512,2048]{1,0:T(8,128)(2,1)S(1)} %constant_dynamic-update-slice_fusion.own_ref, bf16[512,2048]{1,0:T(8,128)(2,1)S(1)} %copy-done.1), custom_call_target="tpu_custom_call" | custom-call | flops 2147483648 | bytes 9437184 | tf_op jit(solution)/shard_map/pallas_call | solution.py:101
  93.5 5.4 %shard_map.77 = (f32[512,2048]{1,0:T(8,128)S(1)}, f32[1,2048]{1,0:T(1,128)S(1)}, f32[1,512]{1,0:T(1,128)S(1)}) custom-call(bf16[512,1024]{1,0:T(8,128)(2,1)S(1)} %get-tuple-element.35.x_ref, bf16[128,2048]{1,0:T(8,128)(2,1)} %collective-permute-done.5.refs_0_, bf16[128,2048]{1,0:T(8,128)(2,1)} %collective-permute-done.12.refs_1_, ...), custom_call_target="tpu_custom_call" | custom-call | flops 2147483648 | bytes 9437184 | tf_op jit(solution)/shard_map/pallas_call | solution.py:113
  99.1 18.9 %all_to_all.15 = f32[16,1,2048]{2,1,0:T(1,128)S(1)} all-to-all(f32[16,1,2048]{2,1,0:T(1,128)S(1)} %broadcast_in_dim.17), channel_id=1, replica_groups=mesh['dp'=4,'row'=4,'col'=16] {'col'}, dimensions={0} | all-to-all | bytes 262144 | tf_op jit(solution)/shard_map/all_to_all | solution.py:253
  118.0 2.3 %shard_map.78 = (f32[1,2048]{1,0:T(1,128)}, f32[1,1024]{1,0:T(1,128)S(1)}) custom-call(f32[512,2048]{1,0:T(8,128)S(1)} %get-tuple-element.41.g_ref, f32[1,2048]{1,0:T(1,128)S(1)} %bitcast.37, f32[16,2048]{1,0:T(8,128)S(1)} %bitcast.34, f32[1,512]{1,0:T(1,128)S(1)} %get-tuple-element.43.row_ref), custom_call_target="tpu_custom_call" | custom-call | flops 4194304 | bytes 4194304 | tf_op jit(solution)/shard_map/pallas_call | solution.py:144
  120.3 10.0 %all_to_all.16 = f32[16,1,1024]{2,1,0:T(1,128)S(1)} all-to-all(f32[16,1,1024]{2,1,0:T(1,128)S(1)} %broadcast_in_dim.18), channel_id=1, replica_groups=mesh['dp'=4,'row'=4,'col'=16] {'dp','row'}, dimensions={0} | all-to-all | bytes 131072 | tf_op jit(solution)/shard_map/all_to_all | solution.py:253
  131.0 14.9 %all_to_all.17 = f32[16,1,128]{2,1,0:T(1,128)S(1)} all-to-all(f32[16,1,128]{2,1,0:T(1,128)S(1)} %broadcast_in_dim.19), channel_id=1, replica_groups=mesh['dp'=4,'row'=4,'col'=16] {'col'}, dimensions={0} | all-to-all | bytes 16384 | tf_op jit(solution)/shard_map/all_to_all | solution.py:253
  147.2 3.2 %shard_map.80 = (f32[512,2048]{1,0:T(8,128)}, f32[1,1]{1,0:T(1,128)}) custom-call(f32[512,2048]{1,0:T(8,128)S(1)} %get-tuple-element.41.g_ref, f32[1,512]{1,0:T(1,128)S(1)} %copy-done.6, f32[1,2048]{1,0:T(1,128)S(1)} %copy-done.5, f32[16,128]{1,0:T(8,128)S(1)} %bitcast.36), custom_call_target="tpu_custom_call" | custom-call | flops 2097152 | bytes 8388608 | tf_op jit(solution)/shard_map/pallas_call | solution.py:205
  (57 shorter events, 12.9 us)
Async XLA Ops:
  0.6 8.7 %copy-start.8 = (bf16[128,512]{1,0:T(8,128)(2,1)S(1)}, bf16[128,512]{1,0:T(8,128)(2,1)}, u32[]{:S(2)}) copy-start(bf16[128,512]{1,0:T(8,128)(2,1)} %param.4) | copy-start | bytes 393220
  0.6 8.7 %collective-permute-start.3 = (bf16[128,512]{1,0:T(8,128)(2,1)}, bf16[128,512]{1,0:T(8,128)(2,1)S(1)}, u32[]{:S(2)}, u32[]{:S(2)}) collective-permute-start(bf16[128,512]{1,0:T(8,128)(2,1)} %param.4), channel_id=1, source_target_pairs={{0,32},{16,48},{32,0},{48,16},{1,33},{17,49},{33,1},{49,17},{2,34}... | collective-permute-start | bytes 393224 | tf_op jit(solution)/shard_map/ppermute | solution.py:244
  6.0 7.5 %collective-permute-start.2 = (bf16[32,2048]{1,0:T(8,128)(2,1)S(1)}, bf16[32,2048]{1,0:T(8,128)(2,1)S(1)}, u32[]{:S(2)}, u32[]{:S(2)}) collective-permute-start(bf16[32,2048]{1,0:T(8,128)(2,1)S(1)} %get-tuple-element.51), channel_id=1, source_target_pairs={{0,192},{64,128},{128,64},{192,0},{1,193},{65,129},{129,65},{193,1... | collective-permute-start | bytes 393224 | tf_op jit(solution)/shard_map/ppermute | solution.py:236
  8.5 5.4 %collective-permute-start.1 = (bf16[32,2048]{1,0:T(8,128)(2,1)S(1)}, bf16[32,2048]{1,0:T(8,128)(2,1)S(1)}, u32[]{:S(2)}, u32[]{:S(2)}) collective-permute-start(bf16[32,2048]{1,0:T(8,128)(2,1)S(1)} %get-tuple-element.52), channel_id=1, source_target_pairs={{0,128},{64,192},{128,0},{192,64},{1,129},{65,193},{129,1},{193,65... | collective-permute-start | bytes 393224 | tf_op jit(solution)/shard_map/ppermute | solution.py:236
  9.0 5.1 %collective-permute-start = (bf16[32,2048]{1,0:T(8,128)(2,1)S(1)}, bf16[32,2048]{1,0:T(8,128)(2,1)S(1)}, u32[]{:S(2)}, u32[]{:S(2)}) collective-permute-start(bf16[32,2048]{1,0:T(8,128)(2,1)S(1)} %get-tuple-element.53), channel_id=1, source_target_pairs={{0,64},{64,0},{128,192},{192,128},{1,65},{65,1},{129,193},{193,129... | collective-permute-start | bytes 393224 | tf_op jit(solution)/shard_map/ppermute | solution.py:236
  9.3 7.8 %collective-permute-start.4 = (bf16[256,512]{1,0:T(8,128)(2,1)S(1)}, bf16[256,512]{1,0:T(8,128)(2,1)S(1)}, u32[]{:S(2)}, u32[]{:S(2)}) collective-permute-start(bf16[256,512]{1,0:T(8,128)(2,1)S(1)} %pad_maximum_fusion.3), channel_id=1, source_target_pairs={{0,16},{16,0},{32,48},{48,32},{1,17},{17,1},{33,49},{49,33},{2,18}... | collective-permute-start | bytes 786440 | tf_op jit(solution)/shard_map/ppermute | solution.py:244
  17.2 13.8 %collective-permute-start.6 = (bf16[512,512]{1,0:T(8,128)(2,1)S(1)}, bf16[512,512]{1,0:T(8,128)(2,1)S(1)}, u32[]{:S(2)}, u32[]{:S(2)}) collective-permute-start(bf16[512,512]{1,0:T(8,128)(2,1)S(1)} %pad_maximum_fusion.2), channel_id=1, source_target_pairs={{0,128},{64,192},{128,0},{192,64},{1,129},{65,193},{129,1},{193,65... | collective-permute-start | bytes 1572872 | tf_op jit(solution)/shard_map/ppermute | solution.py:236
  20.3 12.6 %collective-permute-start.9 = (bf16[128,2048]{1,0:T(8,128)(2,1)S(1)}, bf16[128,2048]{1,0:T(8,128)(2,1)S(1)}, u32[]{:S(2)}, u32[]{:S(2)}) collective-permute-start(bf16[128,2048]{1,0:T(8,128)(2,1)S(1)} %pad_maximum_fusion.1), channel_id=1, source_target_pairs={{0,12},{1,13},{2,14},{3,15},{4,0},{5,1},{6,2},{7,3},{8,4},{9,5},{1... | collective-permute-start | bytes 1572872 | tf_op jit(solution)/shard_map/ppermute | solution.py:240
  23.1 12.3 %collective-permute-start.8 = (bf16[128,2048]{1,0:T(8,128)(2,1)S(1)}, bf16[128,2048]{1,0:T(8,128)(2,1)S(1)}, u32[]{:S(2)}, u32[]{:S(2)}) collective-permute-start(bf16[128,2048]{1,0:T(8,128)(2,1)S(1)} %pad_maximum_fusion.1), channel_id=1, source_target_pairs={{0,8},{1,9},{2,10},{3,11},{4,12},{5,13},{6,14},{7,15},{8,0},{9,1},... | collective-permute-start | bytes 1572872 | tf_op jit(solution)/shard_map/ppermute | solution.py:240
  23.4 26.2 %collective-permute-start.7 = (bf16[128,2048]{1,0:T(8,128)(2,1)S(1)}, bf16[128,2048]{1,0:T(8,128)(2,1)S(1)}, u32[]{:S(2)}, u32[]{:S(2)}) collective-permute-start(bf16[128,2048]{1,0:T(8,128)(2,1)S(1)} %pad_maximum_fusion.1), channel_id=1, source_target_pairs={{0,4},{1,5},{2,6},{3,7},{4,8},{5,9},{6,10},{7,11},{8,12},{9,13},{1... | collective-permute-start | bytes 1572872 | tf_op jit(solution)/shard_map/ppermute | solution.py:240
  24.1 25.5 %collective-permute-start.5 = (bf16[128,2048]{1,0:T(8,128)(2,1)S(1)}, bf16[128,2048]{1,0:T(8,128)(2,1)}, u32[]{:S(2)}, u32[]{:S(2)}) collective-permute-start(bf16[128,2048]{1,0:T(8,128)(2,1)S(1)} %pad_maximum_fusion.1), channel_id=1, source_target_pairs={{0,2},{1,3},{2,0},{3,1},{4,6},{5,7},{6,4},{7,5},{8,10},{9,11},{10,... | collective-permute-start | bytes 1572872 | tf_op jit(solution)/shard_map/ppermute | solution.py:248
  49.8 35.0 %collective-permute-start.10 = (bf16[512,2048]{1,0:T(8,128)(2,1)S(1)}, bf16[512,2048]{1,0:T(8,128)(2,1)S(1)}, u32[]{:S(2)}, u32[]{:S(2)}) collective-permute-start(bf16[512,2048]{1,0:T(8,128)(2,1)S(1)} %constant_dynamic-update-slice_fusion.own_ref), channel_id=1, source_target_pairs={{0,1},{1,0},{2,3},{3,2},{4,5},{5,4},{6,7},{7,6},{8,9},{9,8},{10,11... | collective-permute-start | bytes 6291464 | tf_op jit(solution)/shard_map/ppermute | solution.py:232
  54.6 29.2 %collective-permute-start.11 = (bf16[1024,512]{1,0:T(8,128)(2,1)S(1)}, bf16[1024,512]{1,0:T(8,128)(2,1)S(1)}, u32[]{:S(2)}, u32[]{:S(2)}) collective-permute-start(bf16[1024,512]{1,0:T(8,128)(2,1)S(1)} %pad_maximum_fusion.even_ref), channel_id=1, source_target_pairs={{0,64},{64,0},{128,192},{192,128},{1,65},{65,1},{129,193},{193,129... | collective-permute-start | bytes 3145736 | tf_op jit(solution)/shard_map/ppermute | solution.py:236
  54.9 13.8 %collective-permute-start.14 = (bf16[128,2048]{1,0:T(8,128)(2,1)}, bf16[128,2048]{1,0:T(8,128)(2,1)}, u32[]{:S(2)}, u32[]{:S(2)}) collective-permute-start(bf16[128,2048]{1,0:T(8,128)(2,1)} %collective-permute-done.5.refs_0_), channel_id=1, source_target_pairs={{0,12},{1,13},{2,14},{3,15},{4,0},{5,1},{6,2},{7,3},{8,4},{9,5},{1... | collective-permute-start | bytes 1572872 | tf_op jit(solution)/shard_map/ppermute | solution.py:240
  56.9 23.7 %collective-permute-start.13 = (bf16[128,2048]{1,0:T(8,128)(2,1)}, bf16[128,2048]{1,0:T(8,128)(2,1)}, u32[]{:S(2)}, u32[]{:S(2)}) collective-permute-start(bf16[128,2048]{1,0:T(8,128)(2,1)} %collective-permute-done.5.refs_0_), channel_id=1, source_target_pairs={{0,8},{1,9},{2,10},{3,11},{4,12},{5,13},{6,14},{7,15},{8,0},{9,1},... | collective-permute-start | bytes 1572872 | tf_op jit(solution)/shard_map/ppermute | solution.py:240
  58.3 25.5 %collective-permute-start.12 = (bf16[128,2048]{1,0:T(8,128)(2,1)}, bf16[128,2048]{1,0:T(8,128)(2,1)}, u32[]{:S(2)}, u32[]{:S(2)}) collective-permute-start(bf16[128,2048]{1,0:T(8,128)(2,1)} %collective-permute-done.5.refs_0_), channel_id=1, source_target_pairs={{0,4},{1,5},{2,6},{3,7},{4,8},{5,9},{6,10},{7,11},{8,12},{9,13},{1... | collective-permute-start | bytes 1572872 | tf_op jit(solution)/shard_map/ppermute | solution.py:240
  68.7 24.8 %collective-permute-start.15 = (bf16[128,2048]{1,0:T(8,128)(2,1)}, bf16[128,2048]{1,0:T(8,128)(2,1)}, u32[]{:S(2)}, u32[]{:S(2)}) collective-permute-start(bf16[128,2048]{1,0:T(8,128)(2,1)} %collective-permute-done.5.refs_0_), channel_id=1, source_target_pairs={{0,1},{1,0},{2,3},{3,2},{4,5},{5,4},{6,7},{7,6},{8,9},{9,8},{10,11... | collective-permute-start | bytes 1572872 | tf_op jit(solution)/shard_map/ppermute | solution.py:232
  84.8 1.3 copy-start
  86.1 7.4 %collective-permute-start.16 = (bf16[128,2048]{1,0:T(8,128)(2,1)}, bf16[128,2048]{1,0:T(8,128)(2,1)}, u32[]{:S(2)}, u32[]{:S(2)}) collective-permute-start(bf16[128,2048]{1,0:T(8,128)(2,1)} %collective-permute-done.12.refs_1_), channel_id=1, source_target_pairs={{0,1},{1,0},{2,3},{3,2},{4,5},{5,4},{6,7},{7,6},{8,9},{9,8},{10,11... | collective-permute-start | bytes 1572872 | tf_op jit(solution)/shard_map/ppermute | solution.py:232
  86.6 6.9 %collective-permute-start.17 = (bf16[128,2048]{1,0:T(8,128)(2,1)}, bf16[128,2048]{1,0:T(8,128)(2,1)}, u32[]{:S(2)}, u32[]{:S(2)}) collective-permute-start(bf16[128,2048]{1,0:T(8,128)(2,1)} %collective-permute-done.13.refs_2_), channel_id=1, source_target_pairs={{0,1},{1,0},{2,3},{3,2},{4,5},{5,4},{6,7},{7,6},{8,9},{9,8},{10,11... | collective-permute-start | bytes 1572872 | tf_op jit(solution)/shard_map/ppermute | solution.py:232
  86.6 6.9 %collective-permute-start.18 = (bf16[128,2048]{1,0:T(8,128)(2,1)}, bf16[128,2048]{1,0:T(8,128)(2,1)}, u32[]{:S(2)}, u32[]{:S(2)}) collective-permute-start(bf16[128,2048]{1,0:T(8,128)(2,1)} %collective-permute-done.14.refs_3_), channel_id=1, source_target_pairs={{0,1},{1,0},{2,3},{3,2},{4,5},{5,4},{6,7},{7,6},{8,9},{9,8},{10,11... | collective-permute-start | bytes 1572872 | tf_op jit(solution)/shard_map/ppermute | solution.py:232
  88.4 1.6 %copy-start.1 = (bf16[512,2048]{1,0:T(8,128)(2,1)S(1)}, bf16[512,2048]{1,0:T(8,128)(2,1)}, u32[]{:S(2)}) copy-start(bf16[512,2048]{1,0:T(8,128)(2,1)} %copy-done) | copy-start | bytes 6291460
  93.5 24.5 %copy-start.4 = (f32[2048]{0:T(1024)S(1)}, f32[2048]{0:T(1024)}, u32[]{:S(2)}) copy-start(f32[2048]{0:T(1024)} %param.7) | copy-start | bytes 24580
  118.0 12.3 %copy-start.7 = (f32[512]{0:T(512)S(1)}, f32[512]{0:T(512)}, u32[]{:S(2)}) copy-start(f32[512]{0:T(512)} %param.6) | copy-start | bytes 6148
  (4 other events, 3.6 us)

commit v6 on v5

--- a/solution.py
+++ b/solution.py
@@ -10,6 +10,22 @@
 VMEM_LIMIT = 20 * 1024 * 1024
 COLS = 512
 REPLICAS = (0, 1, 2, 3)
+
+
+def after_kernel(at_ref, *refs):
+    for k in range(at_ref.shape[0]):
+        refs[-1][k] = at_ref[k]
+
+
+def after(at, *blocks):
+    return pl.pallas_call(
+        after_kernel,
+        in_specs=[pl.BlockSpec(memory_space=pltpu.SMEM)]
+        + [pl.BlockSpec(memory_space=pl.ANY)] * len(blocks),
+        out_specs=pl.BlockSpec(memory_space=pltpu.SMEM),
+        out_shape=jax.ShapeDtypeStruct(at.shape, at.dtype),
+        cost_estimate=pl.CostEstimate(flops=1 << 34, bytes_accessed=0, transcendentals=0),
+    )(at, *blocks)
 
 
 def arrange_kernel(at_ref, even_ref, odd_ref, near_ref, far_ref):
@@ -126,11 +142,14 @@
     )(x, *blocks, near)
 
 
-def weigh_kernel(g_ref, moment_ref, parts_ref, row_ref, state_ref, out_ref, acc_ref, weighed_ref):
+def weigh_kernel(
+    g_ref, moment_ref, parts_ref, row_ref, state_ref, copy_ref, out_ref, acc_ref, weighed_ref
+):
     step = pl.program_id(0)
     sums = jnp.sum(parts_ref[...], axis=0, keepdims=True)
     state = 0.8 * moment_ref[...] + 0.2 * sums / D
     state_ref[...] = state
+    copy_ref[...] = state
     scaled = g_ref[...] * lax.rsqrt(state)
     gather_rows(step, across(scaled * scaled), acc_ref, weighed_ref)
 
@@ -145,9 +164,10 @@
         weigh_kernel,
         grid=(2048 // COLS,),
         in_specs=[G_SPEC, moving(1), moving(16), fixed(1, 512)],
-        out_specs=[moving(1), fixed(1, 1024)],
+        out_specs=[moving(1), moving(1), fixed(1, 1024)],
         out_shape=[
             jax.ShapeDtypeStruct((1, 2048), jnp.float32),
+            pltpu.VMEM((1, 2048), jnp.float32),
             jax.ShapeDtypeStruct((1, 1024), jnp.float32),
         ],
         scratch_shapes=[
@@ -161,10 +181,11 @@
     )(in_vmem(g), column_moment, column_parts, row_part)
 
 
-def totals_kernel(moment_ref, parts_ref, state_ref, total_ref):
+def totals_kernel(moment_ref, parts_ref, state_ref, copy_ref, total_ref):
     sums = jnp.sum(parts_ref[...], axis=0, keepdims=True)
     state = 0.8 * moment_ref[...] + 0.2 * sums[:, 0:512] / FF
     state_ref[...] = state
+    copy_ref[...] = state
     squares = jnp.sum(sums[:, 512:1024] / state)
     lane = lax.broadcasted_iota(jnp.int32, (1, 128), 1)
     total_ref[...] = jnp.where(lane == 0, squares, jnp.where(lane == 1, jnp.sum(state), 0.0))
@@ -175,6 +196,7 @@
         totals_kernel,
         out_shape=[
             jax.ShapeDtypeStruct((1, 512), jnp.float32),
+            pltpu.VMEM((1, 512), jnp.float32),
             jax.ShapeDtypeStruct((1, 128), jnp.float32),
         ],
         compiler_params=PARAMS,
@@ -216,7 +238,7 @@
         cost_estimate=pl.CostEstimate(
             flops=2 * 512 * 2048, bytes_accessed=8 << 20, transcendentals=0
         ),
-    )(in_vmem(g), row_state, column_state, totals)
+    )(in_vmem(g), in_vmem(row_state), in_vmem(column_state), totals)
 
 
 def cyclic(size, stride, shift):
@@ -271,29 +293,31 @@
     ]
     blocks = [groups[0]] + [swap_x(groups[s], s) for s in (1, 2, 3)]
     x0 = jnp.concatenate([pair, swap_row(pair, 1)])
-    near, x0 = stage((jnp.concatenate(blocks), x0))
-
-    even = jnp.concatenate([x0, swap_x(x0, 2)])
+    near, x0, at = stage((jnp.concatenate(blocks), x0, at))
+
     far = swap_z(near)
     nears = [move_y(near, t) for t in (1, 2, 3)]
-    far, even, *nears = stage((far, even, *nears))
+    even = jnp.concatenate([x0, swap_x(x0, 2)])
+    at = after(at, far)
+    far, even, at, *nears = stage((far, even, at, *nears))
 
     own = jnp.concatenate([near, *nears])
     other = swap_cores(own)
     odd = swap_x(even, 1)
     fars = [move_y(far, t) for t in (1, 2, 3)]
-    other, odd, *fars = stage((other, odd, *fars))
+    at = after(at, *fars)
+    other, odd, at, far, *fars = stage((other, odd, at, far, *fars))
 
     fars = [far, *fars]
     others = [swap_cores(block) for block in fars]
     x_near, x_far = arrange(at, even, odd)
     gradient = near_product(x_near, own, other)
     gradient, column_part, row_part = far_product(x_far, fars + others, gradient)
-    column_state, sums = weigh(
+    column_state, columns, sums = weigh(
         gradient, column_moment[None], copies(column_part, "col"), row_part
     )
-    row_state, totals = totals_of(row_moment[None], copies(sums, ("dp", "row")))
-    update, row_mean = clip(gradient, row_state, column_state, copies(totals, "col"))
+    row_state, rows, totals = totals_of(row_moment[None], copies(sums, ("dp", "row")))
+    update, row_mean = clip(gradient, rows, columns, copies(totals, "col"))
     return (update, row_state[0], column_state[0], row_mean[0, 0])
 
 

time: 151 us -> 150 us (level)
  starting transfers between devices: 45.3 us -> 29.1 us
  waiting for transfers between devices: 37.1 us -> 43.8 us
  Pallas kernels: 16.2 us -> 19.9 us
  other arithmetic: 0.16 us -> 2.15 us
  local copies, waits for them, and re-layouts: 7.05 us -> 8.84 us
    ppermute x5, starting transfers between devices: 17.7 us -> 2.55 us  [swap_cores(): return lax.ppermute(value, 'col', flipped(16, 1))]
    ppermute x1, waiting for transfers between devices: 0.01 us -> 5.91 us  [swap_z(): return lax.ppermute(value, 'col', flipped(16, 2))]
    ppermute x5, waiting for transfers between devices: 2.01 us -> 4.45 us  [swap_x(): return lax.ppermute(value, 'dp', flipped(4, mask))]
    pallas_call x0 -> x2, Pallas kernels: none -> 2.37 us  [after(): pl.pallas_call(after_kernel, in_specs=[pl.BlockSpec(memory_space=pltpu.SM...]
    ppermute x6, starting transfers between devices: 7.17 us -> 5.24 us  [move_y(): return lax.ppermute(value, 'col', cyclic(4, 4, shift % 4))]
    unnamed x24 -> x30, local copies, waits for them, and re-layouts: 6.77 us -> 6.94 us
  transfers between devices with their start and end apart: 19 -> 19, of which waited for: 9 -> 11; matrix products, arithmetic and copies ran while one was open for 1% -> 6% of each run, Pallas kernels for 3% -> 6%
where the time goes in v6:
time: 150 us
  blocking collectives  45 us (30%)
  waiting for transfers between devices  43.8 us (29%)
  starting transfers between devices  29.1 us (19%)
  Pallas kernels  19.9 us (13%)
  local copies, waits for them, and re-layouts  8.84 us (6%)
  other arithmetic  2.15 us (1%)
    all_to_all x3, blocking collectives, copies(): return lax.all_to_all(rows, axis, 0, 0).reshape(16, value.shape[1])  45 us
    ppermute x6, waiting for transfers between devices, move_y(): return lax.ppermute(value, 'col', cyclic(4, 4, shift % 4))  31.3 us
    ppermute x5, starting transfers between devices, swap_x(): return lax.ppermute(value, 'dp', flipped(4, mask))  7.32 us
    ppermute x1, starting transfers between devices, swap_z(): return lax.ppermute(value, 'col', flipped(16, 2))  7.21 us
    unnamed x30, local copies, waits for them, and re-layouts  6.94 us
    ppermute x2, starting transfers between devices, swap_row(): return lax.ppermute(value, 'row', flipped(4, mask))  6.76 us
    ppermute x1, waiting for transfers between devices, swap_z(): return lax.ppermute(value, 'col', flipped(16, 2))  5.91 us
    ppermute x6, starting transfers between devices, move_y(): return lax.ppermute(value, 'col', cyclic(4, 4, shift % 4))  5.24 us
  transfers between devices with their start and end apart: 19, of which 11 were waited for; matrix products, arithmetic and copies ran while one was open for 6% of the time, Pallas kernels for 6%

profile of v6, /device:TPU:1, one launch (start us, length us, event | category | flops | bytes accessed | tf_op | source)
XLA Modules:
  0.0 149.7 jit_solution(2798854717037952190)
XLA Ops:
  0.6 3.9 %collective-permute-start.3 = (bf16[128,512]{1,0:T(8,128)(2,1)}, bf16[128,512]{1,0:T(8,128)(2,1)S(1)}, u32[]{:S(2)}, u32[]{:S(2)}) collective-permute-start(bf16[128,512]{1,0:T(8,128)(2,1)} %param.4), channel_id=1, source_target_pairs={{0,32},{16,48},{32,0},{48,16},{1,33},{17,49},{33,1},{49,17},{2,34}... | collective-permute-start | bytes 393224 | tf_op jit(solution)/shard_map/ppermute | solution.py:266
  4.5 1.3 copy.15
  6.0 2.6 %collective-permute-start.2 = (bf16[32,2048]{1,0:T(8,128)(2,1)S(1)}, bf16[32,2048]{1,0:T(8,128)(2,1)S(1)}, u32[]{:S(2)}, u32[]{:S(2)}) collective-permute-start(bf16[32,2048]{1,0:T(8,128)(2,1)S(1)} %get-tuple-element.63), channel_id=1, source_target_pairs={{0,192},{64,128},{128,64},{192,0},{1,193},{65,129},{129,65},{193,1... | collective-permute-start | bytes 393224 | tf_op jit(solution)/shard_map/ppermute | solution.py:258
  9.3 2.9 %collective-permute-start.4 = (bf16[256,512]{1,0:T(8,128)(2,1)S(1)}, bf16[256,512]{1,0:T(8,128)(2,1)S(1)}, u32[]{:S(2)}, u32[]{:S(2)}) collective-permute-start(bf16[256,512]{1,0:T(8,128)(2,1)S(1)} %pad_maximum_fusion.3), channel_id=1, source_target_pairs={{0,16},{16,0},{32,48},{48,32},{1,17},{17,1},{33,49},{49,33},{2,18}... | collective-permute-start | bytes 786440 | tf_op jit(solution)/shard_map/ppermute | solution.py:266
  15.0 2.1 %collective-permute-done.4 = bf16[256,512]{1,0:T(8,128)(2,1)S(1)} collective-permute-done((bf16[256,512]{1,0:T(8,128)(2,1)S(1)}, bf16[256,512]{1,0:T(8,128)(2,1)S(1)}, u32[]{:S(2)}, u32[]{:S(2)}) %collective-permute-start.4) | collective-permute-done | bytes 262176 | tf_op jit(solution)/shard_map/ppermute | solution.py:266
  17.2 7.2 %collective-permute-start.5 = (bf16[128,2048]{1,0:T(8,128)(2,1)}, bf16[128,2048]{1,0:T(8,128)(2,1)S(1)}, u32[]{:S(2)}, u32[]{:S(2)}) collective-permute-start(bf16[128,2048]{1,0:T(8,128)(2,1)} %pad_maximum_fusion.1), channel_id=1, source_target_pairs={{0,2},{1,3},{2,0},{3,1},{4,6},{5,7},{6,4},{7,5},{8,10},{9,11},{10,... | collective-permute-start | bytes 1572872 | tf_op jit(solution)/shard_map/ppermute | solution.py:270
  24.4 2.7 %collective-permute-start.9 = (bf16[128,2048]{1,0:T(8,128)(2,1)}, bf16[128,2048]{1,0:T(8,128)(2,1)}, u32[]{:S(2)}, u32[]{:S(2)}) collective-permute-start(bf16[128,2048]{1,0:T(8,128)(2,1)} %pad_maximum_fusion.1), channel_id=1, source_target_pairs={{0,12},{1,13},{2,14},{3,15},{4,0},{5,1},{6,2},{7,3},{8,4},{9,5},{1... | collective-permute-start | bytes 1572872 | tf_op jit(solution)/shard_map/ppermute | solution.py:262
  28.2 2.7 %collective-permute-start.6 = (bf16[512,512]{1,0:T(8,128)(2,1)S(1)}, bf16[512,512]{1,0:T(8,128)(2,1)}, u32[]{:S(2)}, u32[]{:S(2)}) collective-permute-start(bf16[512,512]{1,0:T(8,128)(2,1)S(1)} %pad_maximum_fusion.2), channel_id=1, source_target_pairs={{0,128},{64,192},{128,0},{192,64},{1,129},{65,193},{129,1},{193,65... | collective-permute-start | bytes 1572872 | tf_op jit(solution)/shard_map/ppermute | solution.py:258
  32.0 5.9 %collective-permute-done.5.refs_0_ = bf16[128,2048]{1,0:T(8,128)(2,1)S(1)} collective-permute-done((bf16[128,2048]{1,0:T(8,128)(2,1)}, bf16[128,2048]{1,0:T(8,128)(2,1)S(1)}, u32[]{:S(2)}, u32[]{:S(2)}) %collective-permute-start.5) | collective-permute-done | bytes 524320 | tf_op jit(solution)/shard_map/ppermute | solution.py:270
  40.2 1.3 pad_maximum_fusion.even_ref
  41.5 12.5 %collective-permute-done.7 = bf16[128,2048]{1,0:T(8,128)(2,1)} collective-permute-done((bf16[128,2048]{1,0:T(8,128)(2,1)}, bf16[128,2048]{1,0:T(8,128)(2,1)}, u32[]{:S(2)}, u32[]{:S(2)}) %collective-permute-start.7) | collective-permute-done | bytes 524320 | tf_op jit(solution)/shard_map/ppermute | solution.py:262
  59.9 1.2 collective-permute-start.11
  61.2 6.0 %collective-permute-done.14.refs_2_.refs_3_ = bf16[128,2048]{1,0:T(8,128)(2,1)S(1)} collective-permute-done((bf16[128,2048]{1,0:T(8,128)(2,1)S(1)}, bf16[128,2048]{1,0:T(8,128)(2,1)S(1)}, u32[]{:S(2)}, u32[]{:S(2)}) %collective-permute-start.14) | collective-permute-done | bytes 524320 | tf_op jit(solution)/shard_map/ppermute | solution.py:262
  68.8 12.0 %collective-permute-done.12.refs_0_.refs_1_ = bf16[128,2048]{1,0:T(8,128)(2,1)} collective-permute-done((bf16[128,2048]{1,0:T(8,128)(2,1)S(1)}, bf16[128,2048]{1,0:T(8,128)(2,1)}, u32[]{:S(2)}, u32[]{:S(2)}) %collective-permute-start.12) | collective-permute-done | bytes 524320 | tf_op jit(solution)/shard_map/ppermute | solution.py:262
  80.8 1.2 shard_map.76.at_ref
  82.0 2.8 %collective-permute-done.11.odd_ref = bf16[1024,512]{1,0:T(8,128)(2,1)} collective-permute-done((bf16[1024,512]{1,0:T(8,128)(2,1)S(1)}, bf16[1024,512]{1,0:T(8,128)(2,1)}, u32[]{:S(2)}, u32[]{:S(2)}) %collective-permute-start.11) | collective-permute-done | bytes 1048608 | tf_op jit(solution)/shard_map/ppermute | solution.py:258
  86.8 1.9 %shard_map.77 = (bf16[512,1024]{1,0:T(8,128)(2,1)S(1)}, bf16[512,1024]{1,0:T(8,128)(2,1)S(1)}) custom-call(s32[8]{0:T(128)S(1)} %copy-done.9, bf16[1024,512]{1,0:T(8,128)(2,1)S(1)} %pad_maximum_fusion.even_ref, bf16[1024,512]{1,0:T(8,128)(2,1)} %collective-permute-done.11.odd_ref), custom_call_target="tpu_custom_call" | custom-call | bytes 4194304 | tf_op jit(solution)/shard_map/pallas_call | solution.py:47
  88.8 4.7 %shard_map.78.refs_8_ = f32[512,2048]{1,0:T(8,128)S(1)} custom-call(bf16[512,1024]{1,0:T(8,128)(2,1)S(1)} %get-tuple-element.49.x_ref, bf16[512,2048]{1,0:T(8,128)(2,1)S(1)} %constant_dynamic-update-slice_fusion.own_ref, bf16[512,2048]{1,0:T(8,128)(2,1)} %collective-permute-done.10.other_ref), custom_call_target="tpu_custom_call" | custom-call | flops 2147483648 | bytes 9437184 | tf_op jit(solution)/shard_map/pallas_call | solution.py:117
  93.5 4.9 %shard_map.79 = (f32[512,2048]{1,0:T(8,128)S(1)}, f32[1,2048]{1,0:T(1,128)S(1)}, f32[1,512]{1,0:T(1,128)S(1)}) custom-call(bf16[512,1024]{1,0:T(8,128)(2,1)S(1)} %get-tuple-element.44.x_ref, bf16[128,2048]{1,0:T(8,128)(2,1)S(1)} %copy-done.2, bf16[128,2048]{1,0:T(8,128)(2,1)} %collective-permute-done.12.refs_0_.refs_1_, bf16[128,2048]{1,0:T(8,128)(2,1)S(1)} %copy-done.6, ...), custom_call_target="tpu_custom_call" | custom-call | flops 2147483648 | bytes 9437184 | tf_op jit(solution)/shard_map/pallas_call | solution.py:129
  98.5 19.3 %all_to_all.15 = f32[16,1,2048]{2,1,0:T(1,128)S(1)} all-to-all(f32[16,1,2048]{2,1,0:T(1,128)S(1)} %broadcast_in_dim.17), channel_id=1, replica_groups=mesh['dp'=4,'row'=4,'col'=16] {'col'}, dimensions={0} | all-to-all | bytes 262144 | tf_op jit(solution)/shard_map/all_to_all | solution.py:275
  117.8 2.3 %shard_map.80 = (f32[1,2048]{1,0:T(1,128)}, f32[1,2048]{1,0:T(1,128)S(1)}, f32[1,1024]{1,0:T(1,128)S(1)}) custom-call(f32[512,2048]{1,0:T(8,128)S(1)} %get-tuple-element.51.g_ref, f32[1,2048]{1,0:T(1,128)S(1)} %bitcast.37, f32[16,2048]{1,0:T(8,128)S(1)} %bitcast.34, f32[1,512]{1,0:T(1,128)S(1)} %get-tuple-element.53.row_ref), custom_call_target="tpu_custom_call" | custom-call | flops 4194304 | bytes 4194304 | tf_op jit(solution)/shard_map/pallas_call | solution.py:163
  120.1 11.0 %all_to_all.16 = f32[16,1,1024]{2,1,0:T(1,128)S(1)} all-to-all(f32[16,1,1024]{2,1,0:T(1,128)S(1)} %broadcast_in_dim.18), channel_id=1, replica_groups=mesh['dp'=4,'row'=4,'col'=16] {'dp','row'}, dimensions={0} | all-to-all | bytes 131072 | tf_op jit(solution)/shard_map/all_to_all | solution.py:275
  131.8 14.7 %all_to_all.17 = f32[16,1,128]{2,1,0:T(1,128)S(1)} all-to-all(f32[16,1,128]{2,1,0:T(1,128)S(1)} %broadcast_in_dim.19), channel_id=1, replica_groups=mesh['dp'=4,'row'=4,'col'=16] {'col'}, dimensions={0} | all-to-all | bytes 16384 | tf_op jit(solution)/shard_map/all_to_all | solution.py:275
  146.5 3.2 %shard_map.82 = (f32[512,2048]{1,0:T(8,128)}, f32[1,1]{1,0:T(1,128)}) custom-call(f32[512,2048]{1,0:T(8,128)S(1)} %get-tuple-element.51.g_ref, f32[1,512]{1,0:T(1,128)S(1)} %get-tuple-element.55.row_ref, f32[1,2048]{1,0:T(1,128)S(1)} %get-tuple-element.56.col_ref, f32[16,128]{1,0:T(8,128)S(1)} %bitcast.36), custom_call_target="tpu_custom_call" | custom-call | flops 2097152 | bytes 8388608 | tf_op jit(solution)/shard_map/pallas_call | solution.py:227
  (65 shorter events, 18.4 us)
Async XLA Ops:
  0.6 8.7 %copy-start.11 = (bf16[128,512]{1,0:T(8,128)(2,1)S(1)}, bf16[128,512]{1,0:T(8,128)(2,1)}, u32[]{:S(2)}) copy-start(bf16[128,512]{1,0:T(8,128)(2,1)} %param.4) | copy-start | bytes 393220
  0.6 8.7 %collective-permute-start.3 = (bf16[128,512]{1,0:T(8,128)(2,1)}, bf16[128,512]{1,0:T(8,128)(2,1)S(1)}, u32[]{:S(2)}, u32[]{:S(2)}) collective-permute-start(bf16[128,512]{1,0:T(8,128)(2,1)} %param.4), channel_id=1, source_target_pairs={{0,32},{16,48},{32,0},{48,16},{1,33},{17,49},{33,1},{49,17},{2,34}... | collective-permute-start | bytes 393224 | tf_op jit(solution)/shard_map/ppermute | solution.py:266
  6.0 7.5 %collective-permute-start.2 = (bf16[32,2048]{1,0:T(8,128)(2,1)S(1)}, bf16[32,2048]{1,0:T(8,128)(2,1)S(1)}, u32[]{:S(2)}, u32[]{:S(2)}) collective-permute-start(bf16[32,2048]{1,0:T(8,128)(2,1)S(1)} %get-tuple-element.63), channel_id=1, source_target_pairs={{0,192},{64,128},{128,64},{192,0},{1,193},{65,129},{129,65},{193,1... | collective-permute-start | bytes 393224 | tf_op jit(solution)/shard_map/ppermute | solution.py:258
  8.5 5.4 %collective-permute-start.1 = (bf16[32,2048]{1,0:T(8,128)(2,1)S(1)}, bf16[32,2048]{1,0:T(8,128)(2,1)S(1)}, u32[]{:S(2)}, u32[]{:S(2)}) collective-permute-start(bf16[32,2048]{1,0:T(8,128)(2,1)S(1)} %get-tuple-element.64), channel_id=1, source_target_pairs={{0,128},{64,192},{128,0},{192,64},{1,129},{65,193},{129,1},{193,65... | collective-permute-start | bytes 393224 | tf_op jit(solution)/shard_map/ppermute | solution.py:258
  9.0 5.1 %collective-permute-start = (bf16[32,2048]{1,0:T(8,128)(2,1)S(1)}, bf16[32,2048]{1,0:T(8,128)(2,1)S(1)}, u32[]{:S(2)}, u32[]{:S(2)}) collective-permute-start(bf16[32,2048]{1,0:T(8,128)(2,1)S(1)} %get-tuple-element.65), channel_id=1, source_target_pairs={{0,64},{64,0},{128,192},{192,128},{1,65},{65,1},{129,193},{193,129... | collective-permute-start | bytes 393224 | tf_op jit(solution)/shard_map/ppermute | solution.py:258
  9.3 7.8 %collective-permute-start.4 = (bf16[256,512]{1,0:T(8,128)(2,1)S(1)}, bf16[256,512]{1,0:T(8,128)(2,1)S(1)}, u32[]{:S(2)}, u32[]{:S(2)}) collective-permute-start(bf16[256,512]{1,0:T(8,128)(2,1)S(1)} %pad_maximum_fusion.3), channel_id=1, source_target_pairs={{0,16},{16,0},{32,48},{48,32},{1,17},{17,1},{33,49},{49,33},{2,18}... | collective-permute-start | bytes 786440 | tf_op jit(solution)/shard_map/ppermute | solution.py:266
  17.2 22.7 %copy-start.10 = (bf16[512,512]{1,0:T(8,128)(2,1)}, bf16[512,512]{1,0:T(8,128)(2,1)S(1)}, u32[]{:S(2)}) copy-start(bf16[512,512]{1,0:T(8,128)(2,1)S(1)} %pad_maximum_fusion.2) | copy-start | bytes 1572868
  17.2 20.7 %collective-permute-start.5 = (bf16[128,2048]{1,0:T(8,128)(2,1)}, bf16[128,2048]{1,0:T(8,128)(2,1)S(1)}, u32[]{:S(2)}, u32[]{:S(2)}) collective-permute-start(bf16[128,2048]{1,0:T(8,128)(2,1)} %pad_maximum_fusion.1), channel_id=1, source_target_pairs={{0,2},{1,3},{2,0},{3,1},{4,6},{5,7},{6,4},{7,5},{8,10},{9,11},{10,... | collective-permute-start | bytes 1572872 | tf_op jit(solution)/shard_map/ppermute | solution.py:270
  24.4 17.1 %collective-permute-start.9 = (bf16[128,2048]{1,0:T(8,128)(2,1)}, bf16[128,2048]{1,0:T(8,128)(2,1)}, u32[]{:S(2)}, u32[]{:S(2)}) collective-permute-start(bf16[128,2048]{1,0:T(8,128)(2,1)} %pad_maximum_fusion.1), channel_id=1, source_target_pairs={{0,12},{1,13},{2,14},{3,15},{4,0},{5,1},{6,2},{7,3},{8,4},{9,5},{1... | collective-permute-start | bytes 1572872 | tf_op jit(solution)/shard_map/ppermute | solution.py:262
  27.2 14.4 %collective-permute-start.8 = (bf16[128,2048]{1,0:T(8,128)(2,1)}, bf16[128,2048]{1,0:T(8,128)(2,1)}, u32[]{:S(2)}, u32[]{:S(2)}) collective-permute-start(bf16[128,2048]{1,0:T(8,128)(2,1)} %pad_maximum_fusion.1), channel_id=1, source_target_pairs={{0,8},{1,9},{2,10},{3,11},{4,12},{5,13},{6,14},{7,15},{8,0},{9,1},... | collective-permute-start | bytes 1572872 | tf_op jit(solution)/shard_map/ppermute | solution.py:262
  27.5 26.6 %collective-permute-start.7 = (bf16[128,2048]{1,0:T(8,128)(2,1)}, bf16[128,2048]{1,0:T(8,128)(2,1)}, u32[]{:S(2)}, u32[]{:S(2)}) collective-permute-start(bf16[128,2048]{1,0:T(8,128)(2,1)} %pad_maximum_fusion.1), channel_id=1, source_target_pairs={{0,4},{1,5},{2,6},{3,7},{4,8},{5,9},{6,10},{7,11},{8,12},{9,13},{1... | collective-permute-start | bytes 1572872 | tf_op jit(solution)/shard_map/ppermute | solution.py:262
  28.2 12.0 %collective-permute-start.6 = (bf16[512,512]{1,0:T(8,128)(2,1)S(1)}, bf16[512,512]{1,0:T(8,128)(2,1)}, u32[]{:S(2)}, u32[]{:S(2)}) collective-permute-start(bf16[512,512]{1,0:T(8,128)(2,1)S(1)} %pad_maximum_fusion.2), channel_id=1, source_target_pairs={{0,128},{64,192},{128,0},{192,64},{1,129},{65,193},{129,1},{193,65... | collective-permute-start | bytes 1572872 | tf_op jit(solution)/shard_map/ppermute | solution.py:258
  39.9 14.1 %copy-start.1 = (bf16[128,2048]{1,0:T(8,128)(2,1)S(1)}, bf16[128,2048]{1,0:T(8,128)(2,1)}, u32[]{:S(2)}) copy-start(bf16[128,2048]{1,0:T(8,128)(2,1)} %copy-done) | copy-start | bytes 1572868
  54.1 13.1 %collective-permute-start.14 = (bf16[128,2048]{1,0:T(8,128)(2,1)S(1)}, bf16[128,2048]{1,0:T(8,128)(2,1)S(1)}, u32[]{:S(2)}, u32[]{:S(2)}) collective-permute-start(bf16[128,2048]{1,0:T(8,128)(2,1)S(1)} %copy-done.1), channel_id=1, source_target_pairs={{0,12},{1,13},{2,14},{3,15},{4,0},{5,1},{6,2},{7,3},{8,4},{9,5},{1... | collective-permute-start | bytes 1572872 | tf_op jit(solution)/shard_map/ppermute | solution.py:262
  54.1 13.9 %collective-permute-start.13 = (bf16[128,2048]{1,0:T(8,128)(2,1)S(1)}, bf16[128,2048]{1,0:T(8,128)(2,1)S(1)}, u32[]{:S(2)}, u32[]{:S(2)}) collective-permute-start(bf16[128,2048]{1,0:T(8,128)(2,1)S(1)} %copy-done.1), channel_id=1, source_target_pairs={{0,8},{1,9},{2,10},{3,11},{4,12},{5,13},{6,14},{7,15},{8,0},{9,1},... | collective-permute-start | bytes 1572872 | tf_op jit(solution)/shard_map/ppermute | solution.py:262
  54.4 26.3 %collective-permute-start.12 = (bf16[128,2048]{1,0:T(8,128)(2,1)S(1)}, bf16[128,2048]{1,0:T(8,128)(2,1)}, u32[]{:S(2)}, u32[]{:S(2)}) collective-permute-start(bf16[128,2048]{1,0:T(8,128)(2,1)S(1)} %copy-done.1), channel_id=1, source_target_pairs={{0,4},{1,5},{2,6},{3,7},{4,8},{5,9},{6,10},{7,11},{8,12},{9,13},{1... | collective-permute-start | bytes 1572872 | tf_op jit(solution)/shard_map/ppermute | solution.py:262
  58.8 26.0 %collective-permute-start.10 = (bf16[512,2048]{1,0:T(8,128)(2,1)S(1)}, bf16[512,2048]{1,0:T(8,128)(2,1)}, u32[]{:S(2)}, u32[]{:S(2)}) collective-permute-start(bf16[512,2048]{1,0:T(8,128)(2,1)S(1)} %constant_dynamic-update-slice_fusion.own_ref), channel_id=1, source_target_pairs={{0,1},{1,0},{2,3},{3,2},{4,5},{5,4},{6,7},{7,6},{8,9},{9,8},{10,11... | collective-permute-start | bytes 6291464 | tf_op jit(solution)/shard_map/ppermute | solution.py:254
  59.9 24.8 %collective-permute-start.11 = (bf16[1024,512]{1,0:T(8,128)(2,1)S(1)}, bf16[1024,512]{1,0:T(8,128)(2,1)}, u32[]{:S(2)}, u32[]{:S(2)}) collective-permute-start(bf16[1024,512]{1,0:T(8,128)(2,1)S(1)} %pad_maximum_fusion.even_ref), channel_id=1, source_target_pairs={{0,64},{64,0},{128,192},{192,128},{1,65},{65,1},{129,193},{193,129... | collective-permute-start | bytes 3145736 | tf_op jit(solution)/shard_map/ppermute | solution.py:258
  84.8 8.7 %collective-permute-start.15 = (bf16[128,2048]{1,0:T(8,128)(2,1)}, bf16[128,2048]{1,0:T(8,128)(2,1)S(1)}, u32[]{:S(2)}, u32[]{:S(2)}) collective-permute-start(bf16[128,2048]{1,0:T(8,128)(2,1)} %copy-done), channel_id=1, source_target_pairs={{0,1},{1,0},{2,3},{3,2},{4,5},{5,4},{6,7},{7,6},{8,9},{9,8},{10,11... | collective-permute-start | bytes 1572872 | tf_op jit(solution)/shard_map/ppermute | solution.py:254
  85.6 7.8 %collective-permute-start.16 = (bf16[128,2048]{1,0:T(8,128)(2,1)}, bf16[128,2048]{1,0:T(8,128)(2,1)S(1)}, u32[]{:S(2)}, u32[]{:S(2)}) collective-permute-start(bf16[128,2048]{1,0:T(8,128)(2,1)} %collective-permute-done.12.refs_0_.refs_1_), channel_id=1, source_target_pairs={{0,1},{1,0},{2,3},{3,2},{4,5},{5,4},{6,7},{7,6},{8,9},{9,8},{10,11... | collective-permute-start | bytes 1572872 | tf_op jit(solution)/shard_map/ppermute | solution.py:254
  85.6 7.8 %collective-permute-start.17 = (bf16[128,2048]{1,0:T(8,128)(2,1)}, bf16[128,2048]{1,0:T(8,128)(2,1)S(1)}, u32[]{:S(2)}, u32[]{:S(2)}) collective-permute-start(bf16[128,2048]{1,0:T(8,128)(2,1)} %copy-done.5), channel_id=1, source_target_pairs={{0,1},{1,0},{2,3},{3,2},{4,5},{5,4},{6,7},{7,6},{8,9},{9,8},{10,11... | collective-permute-start | bytes 1572872 | tf_op jit(solution)/shard_map/ppermute | solution.py:254
  86.2 7.3 %collective-permute-start.18 = (bf16[128,2048]{1,0:T(8,128)(2,1)}, bf16[128,2048]{1,0:T(8,128)(2,1)S(1)}, u32[]{:S(2)}, u32[]{:S(2)}) collective-permute-start(bf16[128,2048]{1,0:T(8,128)(2,1)} %copy-done.3), channel_id=1, source_target_pairs={{0,1},{1,0},{2,3},{3,2},{4,5},{5,4},{6,7},{7,6},{8,9},{9,8},{10,11... | collective-permute-start | bytes 1572872 | tf_op jit(solution)/shard_map/ppermute | solution.py:254
  93.5 24.3 %copy-start.7 = (f32[2048]{0:T(1024)S(1)}, f32[2048]{0:T(1024)}, u32[]{:S(2)}) copy-start(f32[2048]{0:T(1024)} %param.7) | copy-start | bytes 24580
  117.8 13.4 %copy-start.8 = (f32[512]{0:T(512)S(1)}, f32[512]{0:T(512)}, u32[]{:S(2)}) copy-start(f32[512]{0:T(512)} %param.6) | copy-start | bytes 6148
  (7 other events, 17.3 us)

commit v7 on v6

--- a/solution.py
+++ b/solution.py
@@ -9,49 +9,40 @@
 FF = 32768
 VMEM_LIMIT = 20 * 1024 * 1024
 COLS = 512
-REPLICAS = (0, 1, 2, 3)
-
-
-def after_kernel(at_ref, *refs):
-    for k in range(at_ref.shape[0]):
-        refs[-1][k] = at_ref[k]
-
-
-def after(at, *blocks):
+def after_kernel(value_ref, tile_ref, out_ref):
+    del tile_ref
+    out_ref[...] = value_ref[...]
+
+
+def after(value, block):
     return pl.pallas_call(
         after_kernel,
-        in_specs=[pl.BlockSpec(memory_space=pltpu.SMEM)]
-        + [pl.BlockSpec(memory_space=pl.ANY)] * len(blocks),
-        out_specs=pl.BlockSpec(memory_space=pltpu.SMEM),
-        out_shape=jax.ShapeDtypeStruct(at.shape, at.dtype),
+        out_shape=jax.ShapeDtypeStruct(value.shape, value.dtype),
         cost_estimate=pl.CostEstimate(flops=1 << 34, bytes_accessed=0, transcendentals=0),
-    )(at, *blocks)
-
-
-def arrange_kernel(at_ref, even_ref, odd_ref, near_ref, far_ref):
-    for far, out_ref in ((0, near_ref), (1, far_ref)):
+    )(value, block[0:16, 0:128])
+
+
+def arrange_kernel(at_ref, *refs):
+    pieces = refs[:4]
+    for far, out_ref in enumerate(refs[4:]):
         for other in (0, 1):
             for t in range(4):
-                start = at_ref[t] + at_ref[4 + far] + at_ref[6 + other]
-                rows = []
-                for s in REPLICAS:
-                    piece = odd_ref if s % 2 else even_ref
-                    place = pl.multiple_of(start + s // 2 * 512, 32)
-                    rows.append(piece[pl.ds(place, 32), :])
+                start = pl.multiple_of(at_ref[t] + at_ref[4 + far] + at_ref[6 + other], 32)
+                rows = [piece[pl.ds(start, 32), :] for piece in pieces]
                 column = other * 512 + t * 128
                 out_ref[:, column : column + 128] = jnp.concatenate(rows, axis=0).T
 
 
-def arrange(at, even, odd):
+def arrange(at, pieces):
     whole = pl.BlockSpec(memory_space=pltpu.VMEM)
     return pl.pallas_call(
         arrange_kernel,
-        in_specs=[pl.BlockSpec(memory_space=pltpu.SMEM), whole, whole],
+        in_specs=[pl.BlockSpec(memory_space=pltpu.SMEM)] + [whole] * 4,
         out_specs=[whole] * 2,
         out_shape=[jax.ShapeDtypeStruct((512, 1024), jnp.bfloat16)] * 2,
         compiler_params=PARAMS,
         cost_estimate=pl.CostEstimate(flops=0, bytes_accessed=4 << 20, transcendentals=0),
-    )(at, even, odd)
+    )(at, *pieces)
 
 
 def near_kernel(x_ref, own_ref, other_ref, out_ref):
@@ -289,7 +280,7 @@
     pair = jnp.concatenate([inputs, swap_row(inputs, 2)])
     by_group = stage(jnp.transpose(grad_out, (1, 0, 2)))
     groups = [
-        lax.dynamic_index_in_dim(by_group, me ^ s, 0, keepdims=False) for s in REPLICAS
+        lax.dynamic_index_in_dim(by_group, me ^ s, 0, keepdims=False) for s in range(4)
     ]
     blocks = [groups[0]] + [swap_x(groups[s], s) for s in (1, 2, 3)]
     x0 = jnp.concatenate([pair, swap_row(pair, 1)])
@@ -297,24 +288,23 @@
 
     far = swap_z(near)
     nears = [move_y(near, t) for t in (1, 2, 3)]
-    even = jnp.concatenate([x0, swap_x(x0, 2)])
-    at = after(at, far)
-    far, even, at, *nears = stage((far, even, at, *nears))
+    x2 = swap_x(x0, 2)
+    moment = after(column_moment[None], far)
+    far, moment, x0, x2, *nears = stage((far, moment, x0, x2, *nears))
 
     own = jnp.concatenate([near, *nears])
     other = swap_cores(own)
-    odd = swap_x(even, 1)
+    x1, x3 = swap_x(x0, 1), swap_x(x0, 3)
     fars = [move_y(far, t) for t in (1, 2, 3)]
-    at = after(at, *fars)
-    other, odd, at, far, *fars = stage((other, odd, at, far, *fars))
+    x_near, x_far = arrange(at, (x0, x1, x2, x3))
+    other, x_near, x_far, far, *fars = stage((other, x_near, x_far, far, *fars))
 
     fars = [far, *fars]
     others = [swap_cores(block) for block in fars]
-    x_near, x_far = arrange(at, even, odd)
     gradient = near_product(x_near, own, other)
     gradient, column_part, row_part = far_product(x_far, fars + others, gradient)
     column_state, columns, sums = weigh(
-        gradient, column_moment[None], copies(column_part, "col"), row_part
+        gradient, moment, copies(column_part, "col"), row_part
     )
     row_state, rows, totals = totals_of(row_moment[None], copies(sums, ("dp", "row")))
     update, row_mean = clip(gradient, rows, columns, copies(totals, "col"))

time: 150 us -> 144 us (0.960)
  starting transfers between devices: 29.1 us -> 36.2 us
  waiting for transfers between devices: 43.8 us -> 39.9 us
  Pallas kernels: 19.9 us -> 16.8 us
  blocking collectives: 45 us -> 42.3 us
  local copies, waits for them, and re-layouts: 8.84 us -> 6.55 us
    ppermute x6, waiting for transfers between devices: 31.3 us -> 20.5 us  [move_y(): return lax.ppermute(value, 'col', cyclic(4, 4, shift % 4))]
    ppermute x5 -> x6, waiting for transfers between devices: 4.45 us -> 14.7 us  [swap_x(): return lax.ppermute(value, 'dp', flipped(4, mask))]
    ppermute x6, starting transfers between devices: 5.24 us -> 9.74 us  [move_y(): return lax.ppermute(value, 'col', cyclic(4, 4, shift % 4))]
    all_to_all x3, blocking collectives: 45 us -> 42.3 us  [copies(): return lax.all_to_all(rows, axis, 0, 0).reshape(16, value.shape[1])]
    ppermute x5 -> x6, starting transfers between devices: 7.32 us -> 9.73 us  [swap_x(): return lax.ppermute(value, 'dp', flipped(4, mask))]
    unnamed x30 -> x12, local copies, waits for them, and re-layouts: 6.94 us -> 4.63 us
    ppermute x2, waiting for transfers between devices: 2.15 us -> 0.01 us  [swap_row(): return lax.ppermute(value, 'row', flipped(4, mask))]
    ppermute x5, starting transfers between devices: 2.55 us -> 4.62 us  [swap_cores(): return lax.ppermute(value, 'col', flipped(16, 1))]
  transfers between devices with their start and end apart: 19 -> 20, of which waited for: 11 -> 9; matrix products, arithmetic and copies ran while one was open for 6% -> 3% of each run, Pallas kernels for 6% -> 5%
where the time goes in v7:
time: 144 us; the launch traced here: 143 us
  blocking collectives  42.3 us (29%)
  waiting for transfers between devices  39.9 us (28%)
  starting transfers between devices  36.2 us (25%)
  Pallas kernels  16.8 us (12%)
  local copies, waits for them, and re-layouts  6.55 us (5%)
    all_to_all x3, blocking collectives, copies(): return lax.all_to_all(rows, axis, 0, 0).reshape(16, value.shape[1])  42.3 us
    ppermute x6, waiting for transfers between devices, move_y(): return lax.ppermute(value, 'col', cyclic(4, 4, shift % 4))  20.5 us
    ppermute x6, waiting for transfers between devices, swap_x(): return lax.ppermute(value, 'dp', flipped(4, mask))  14.7 us
    ppermute x6, starting transfers between devices, move_y(): return lax.ppermute(value, 'col', cyclic(4, 4, shift % 4))  9.74 us
    ppermute x6, starting transfers between devices, swap_x(): return lax.ppermute(value, 'dp', flipped(4, mask))  9.73 us
    ppermute x2, starting transfers between devices, swap_row(): return lax.ppermute(value, 'row', flipped(4, mask))  6.16 us
    ppermute x1, starting transfers between devices, swap_z(): return lax.ppermute(value, 'col', flipped(16, 2))  5.93 us
    ppermute x1, waiting for transfers between devices, swap_z(): return lax.ppermute(value, 'col', flipped(16, 2))  4.7 us
  transfers between devices with their start and end apart: 20, of which 9 were waited for; matrix products, arithmetic and copies ran while one was open for 3% of the time, Pallas kernels for 5%

profile of v7, /device:TPU:1, one launch (start us, length us, event | category | flops | bytes accessed | tf_op | source)
XLA Modules:
  0.0 143.5 jit_solution(2518698291640618430)
XLA Ops:
  0.6 3.9 %collective-permute-start.3 = (bf16[128,512]{1,0:T(8,128)(2,1)}, bf16[128,512]{1,0:T(8,128)(2,1)S(1)}, u32[]{:S(2)}, u32[]{:S(2)}) collective-permute-start(bf16[128,512]{1,0:T(8,128)(2,1)} %param.4), channel_id=1, source_target_pairs={{0,32},{16,48},{32,0},{48,16},{1,33},{17,49},{33,1},{49,17},{2,34}... | collective-permute-start | bytes 393224 | tf_op jit(solution)/shard_map/ppermute | solution.py:257
  7.3 2.5 %collective-permute-start.1 = (bf16[32,2048]{1,0:T(8,128)(2,1)S(1)}, bf16[32,2048]{1,0:T(8,128)(2,1)S(1)}, u32[]{:S(2)}, u32[]{:S(2)}) collective-permute-start(bf16[32,2048]{1,0:T(8,128)(2,1)S(1)} %get-tuple-element.66), channel_id=1, source_target_pairs={{0,128},{64,192},{128,0},{192,64},{1,129},{65,193},{129,1},{193,65... | collective-permute-start | bytes 393224 | tf_op jit(solution)/shard_map/ppermute | solution.py:249
  9.9 2.3 %collective-permute-start.4 = (bf16[256,512]{1,0:T(8,128)(2,1)S(1)}, bf16[256,512]{1,0:T(8,128)(2,1)S(1)}, u32[]{:S(2)}, u32[]{:S(2)}) collective-permute-start(bf16[256,512]{1,0:T(8,128)(2,1)S(1)} %pad_maximum_fusion.2), channel_id=1, source_target_pairs={{0,16},{16,0},{32,48},{48,32},{1,17},{17,1},{33,49},{49,33},{2,18}... | collective-permute-start | bytes 786440 | tf_op jit(solution)/shard_map/ppermute | solution.py:257
  12.3 2.5 %collective-permute-done.1 = bf16[32,2048]{1,0:T(8,128)(2,1)S(1)} collective-permute-done((bf16[32,2048]{1,0:T(8,128)(2,1)S(1)}, bf16[32,2048]{1,0:T(8,128)(2,1)S(1)}, u32[]{:S(2)}, u32[]{:S(2)}) %collective-permute-start.1) | collective-permute-done | bytes 131104 | tf_op jit(solution)/shard_map/ppermute | solution.py:249
  14.8 2.8 %collective-permute-done.2 = bf16[32,2048]{1,0:T(8,128)(2,1)S(1)} collective-permute-done((bf16[32,2048]{1,0:T(8,128)(2,1)S(1)}, bf16[32,2048]{1,0:T(8,128)(2,1)S(1)}, u32[]{:S(2)}, u32[]{:S(2)}) %collective-permute-start.2) | collective-permute-done | bytes 131104 | tf_op jit(solution)/shard_map/ppermute | solution.py:249
  18.5 5.9 %collective-permute-start.5 = (bf16[128,2048]{1,0:T(8,128)(2,1)}, bf16[128,2048]{1,0:T(8,128)(2,1)S(1)}, u32[]{:S(2)}, u32[]{:S(2)}) collective-permute-start(bf16[128,2048]{1,0:T(8,128)(2,1)} %pad_maximum_fusion), channel_id=1, source_target_pairs={{0,2},{1,3},{2,0},{3,1},{4,6},{5,7},{6,4},{7,5},{8,10},{9,11},{10,... | collective-permute-start | bytes 1572872 | tf_op jit(solution)/shard_map/ppermute | solution.py:261
  25.7 2.6 %collective-permute-start.8 = (bf16[128,2048]{1,0:T(8,128)(2,1)}, bf16[128,2048]{1,0:T(8,128)(2,1)}, u32[]{:S(2)}, u32[]{:S(2)}) collective-permute-start(bf16[128,2048]{1,0:T(8,128)(2,1)} %pad_maximum_fusion), channel_id=1, source_target_pairs={{0,8},{1,9},{2,10},{3,11},{4,12},{5,13},{6,14},{7,15},{8,0},{9,1},... | collective-permute-start | bytes 1572872 | tf_op jit(solution)/shard_map/ppermute | solution.py:253
  29.4 2.7 %collective-permute-start.6 = (bf16[512,512]{1,0:T(8,128)(2,1)S(1)}, bf16[512,512]{1,0:T(8,128)(2,1)}, u32[]{:S(2)}, u32[]{:S(2)}) collective-permute-start(bf16[512,512]{1,0:T(8,128)(2,1)S(1)} %pad_maximum_fusion.1.refs_0_), channel_id=1, source_target_pairs={{0,128},{64,192},{128,0},{192,64},{1,129},{65,193},{129,1},{193,65... | collective-permute-start | bytes 1572872 | tf_op jit(solution)/shard_map/ppermute | solution.py:249
  33.2 4.7 %collective-permute-done.5.refs_0_ = bf16[128,2048]{1,0:T(8,128)(2,1)S(1)} collective-permute-done((bf16[128,2048]{1,0:T(8,128)(2,1)}, bf16[128,2048]{1,0:T(8,128)(2,1)S(1)}, u32[]{:S(2)}, u32[]{:S(2)}) %collective-permute-start.5) | collective-permute-done | bytes 524320 | tf_op jit(solution)/shard_map/ppermute | solution.py:261
  41.4 8.2 %collective-permute-done.8 = bf16[128,2048]{1,0:T(8,128)(2,1)} collective-permute-done((bf16[128,2048]{1,0:T(8,128)(2,1)}, bf16[128,2048]{1,0:T(8,128)(2,1)}, u32[]{:S(2)}, u32[]{:S(2)}) %collective-permute-start.8) | collective-permute-done | bytes 524320 | tf_op jit(solution)/shard_map/ppermute | solution.py:253
  53.9 2.2 %collective-permute-start.10 = (bf16[512,2048]{1,0:T(8,128)(2,1)S(1)}, bf16[512,2048]{1,0:T(8,128)(2,1)S(1)}, u32[]{:S(2)}, u32[]{:S(2)}) collective-permute-start(bf16[512,2048]{1,0:T(8,128)(2,1)S(1)} %constant_dynamic-update-slice_fusion.own_ref), channel_id=1, source_target_pairs={{0,1},{1,0},{2,3},{3,2},{4,5},{5,4},{6,7},{7,6},{8,9},{9,8},{10,11... | collective-permute-start | bytes 6291464 | tf_op jit(solution)/shard_map/ppermute | solution.py:245
  57.3 1.8 %collective-permute-start.12 = (bf16[512,512]{1,0:T(8,128)(2,1)S(1)}, bf16[512,512]{1,0:T(8,128)(2,1)S(1)}, u32[]{:S(2)}, u32[]{:S(2)}) collective-permute-start(bf16[512,512]{1,0:T(8,128)(2,1)S(1)} %pad_maximum_fusion.1.refs_0_), channel_id=1, source_target_pairs={{0,192},{64,128},{128,64},{192,0},{1,193},{65,129},{129,65},{193,1... | collective-permute-start | bytes 1572872 | tf_op jit(solution)/shard_map/ppermute | solution.py:249
  60.0 2.1 %collective-permute-start.14 = (bf16[128,2048]{1,0:T(8,128)(2,1)S(1)}, bf16[128,2048]{1,0:T(8,128)(2,1)S(1)}, u32[]{:S(2)}, u32[]{:S(2)}) collective-permute-start(bf16[128,2048]{1,0:T(8,128)(2,1)S(1)} %collective-permute-done.5.refs_0_), channel_id=1, source_target_pairs={{0,8},{1,9},{2,10},{3,11},{4,12},{5,13},{6,14},{7,15},{8,0},{9,1},... | collective-permute-start | bytes 1572872 | tf_op jit(solution)/shard_map/ppermute | solution.py:253
  62.1 7.5 %collective-permute-done.11.refs_1_ = bf16[512,512]{1,0:T(8,128)(2,1)S(1)} collective-permute-done((bf16[512,512]{1,0:T(8,128)(2,1)S(1)}, bf16[512,512]{1,0:T(8,128)(2,1)S(1)}, u32[]{:S(2)}, u32[]{:S(2)}) %collective-permute-start.11) | collective-permute-done | bytes 524320 | tf_op jit(solution)/shard_map/ppermute | solution.py:249
  69.6 1.8 %collective-permute-start.15 = (bf16[128,2048]{1,0:T(8,128)(2,1)S(1)}, bf16[128,2048]{1,0:T(8,128)(2,1)S(1)}, u32[]{:S(2)}, u32[]{:S(2)}) collective-permute-start(bf16[128,2048]{1,0:T(8,128)(2,1)S(1)} %collective-permute-done.5.refs_0_), channel_id=1, source_target_pairs={{0,12},{1,13},{2,14},{3,15},{4,0},{5,1},{6,2},{7,3},{8,4},{9,5},{1... | collective-permute-start | bytes 1572872 | tf_op jit(solution)/shard_map/ppermute | solution.py:253
  73.4 11.3 %collective-permute-done.14.refs_2_ = bf16[128,2048]{1,0:T(8,128)(2,1)S(1)} collective-permute-done((bf16[128,2048]{1,0:T(8,128)(2,1)S(1)}, bf16[128,2048]{1,0:T(8,128)(2,1)S(1)}, u32[]{:S(2)}, u32[]{:S(2)}) %collective-permute-start.14) | collective-permute-done | bytes 524320 | tf_op jit(solution)/shard_map/ppermute | solution.py:253
  84.7 1.8 %collective-permute-start.16 = (bf16[128,2048]{1,0:T(8,128)(2,1)S(1)}, bf16[128,2048]{1,0:T(8,128)(2,1)S(1)}, u32[]{:S(2)}, u32[]{:S(2)}) collective-permute-start(bf16[128,2048]{1,0:T(8,128)(2,1)S(1)} %collective-permute-done.5.refs_0_), channel_id=1, source_target_pairs={{0,1},{1,0},{2,3},{3,2},{4,5},{5,4},{6,7},{7,6},{8,9},{9,8},{10,11... | collective-permute-start | bytes 1572872 | tf_op jit(solution)/shard_map/ppermute | solution.py:245
  87.1 3.5 %shard_map.77.refs_8_ = f32[512,2048]{1,0:T(8,128)S(1)} custom-call(bf16[512,1024]{1,0:T(8,128)(2,1)S(1)} %get-tuple-element.50.x_ref, bf16[512,2048]{1,0:T(8,128)(2,1)S(1)} %constant_dynamic-update-slice_fusion.own_ref, bf16[512,2048]{1,0:T(8,128)(2,1)S(1)} %collective-permute-done.10.other_ref), custom_call_target="tpu_custom_call" | custom-call | flops 2147483648 | bytes 9437184 | tf_op jit(solution)/shard_map/pallas_call | solution.py:108
  90.7 4.2 %shard_map.78 = (f32[512,2048]{1,0:T(8,128)S(1)}, f32[1,2048]{1,0:T(1,128)S(1)}, f32[1,512]{1,0:T(1,128)S(1)}) custom-call(bf16[512,1024]{1,0:T(8,128)(2,1)S(1)} %get-tuple-element.45.x_ref, bf16[128,2048]{1,0:T(8,128)(2,1)S(1)} %collective-permute-done.5.refs_0_, bf16[128,2048]{1,0:T(8,128)(2,1)S(1)} %collective-permute-done.13.refs_1_, ...), custom_call_target="tpu_custom_call" | custom-call | flops 2147483648 | bytes 9437184 | tf_op jit(solution)/shard_map/pallas_call | solution.py:120
  95.0 17.8 %all_to_all.15 = f32[16,1,2048]{2,1,0:T(1,128)S(1)} all-to-all(f32[16,1,2048]{2,1,0:T(1,128)S(1)} %broadcast_in_dim.17), channel_id=1, replica_groups=mesh['dp'=4,'row'=4,'col'=16] {'col'}, dimensions={0} | all-to-all | bytes 262144 | tf_op jit(solution)/shard_map/all_to_all | solution.py:266
  112.9 2.3 %shard_map.79 = (f32[1,2048]{1,0:T(1,128)}, f32[1,2048]{1,0:T(1,128)S(1)}, f32[1,1024]{1,0:T(1,128)S(1)}) custom-call(f32[512,2048]{1,0:T(8,128)S(1)} %get-tuple-element.52.g_ref, f32[1,2048]{1,0:T(1,128)S(1)} %copy-done, f32[16,2048]{1,0:T(8,128)S(1)} %bitcast.34, f32[1,512]{1,0:T(1,128)S(1)} %get-tuple-element.55.row_ref), custom_call_target="tpu_custom_call" | custom-call | flops 4194304 | bytes 4194304 | tf_op jit(solution)/shard_map/pallas_call | solution.py:154
  115.2 10.5 %all_to_all.16 = f32[16,1,1024]{2,1,0:T(1,128)S(1)} all-to-all(f32[16,1,1024]{2,1,0:T(1,128)S(1)} %broadcast_in_dim.18), channel_id=1, replica_groups=mesh['dp'=4,'row'=4,'col'=16] {'dp','row'}, dimensions={0} | all-to-all | bytes 131072 | tf_op jit(solution)/shard_map/all_to_all | solution.py:266
  126.4 13.9 %all_to_all.17 = f32[16,1,128]{2,1,0:T(1,128)S(1)} all-to-all(f32[16,1,128]{2,1,0:T(1,128)S(1)} %broadcast_in_dim.19), channel_id=1, replica_groups=mesh['dp'=4,'row'=4,'col'=16] {'col'}, dimensions={0} | all-to-all | bytes 16384 | tf_op jit(solution)/shard_map/all_to_all | solution.py:266
  140.3 3.2 %shard_map.81 = (f32[512,2048]{1,0:T(8,128)}, f32[1,1]{1,0:T(1,128)}) custom-call(f32[512,2048]{1,0:T(8,128)S(1)} %get-tuple-element.52.g_ref, f32[1,512]{1,0:T(1,128)S(1)} %get-tuple-element.57.row_ref, f32[1,2048]{1,0:T(1,128)S(1)} %get-tuple-element.58.col_ref, f32[16,128]{1,0:T(8,128)S(1)} %bitcast.36), custom_call_target="tpu_custom_call" | custom-call | flops 2097152 | bytes 8388608 | tf_op jit(solution)/shard_map/pallas_call | solution.py:218
  (48 shorter events, 20.6 us)
Async XLA Ops:
  0.6 9.3 %copy-start.2 = (bf16[128,512]{1,0:T(8,128)(2,1)S(1)}, bf16[128,512]{1,0:T(8,128)(2,1)}, u32[]{:S(2)}) copy-start(bf16[128,512]{1,0:T(8,128)(2,1)} %param.4) | copy-start | bytes 393220
  0.6 9.3 %collective-permute-start.3 = (bf16[128,512]{1,0:T(8,128)(2,1)}, bf16[128,512]{1,0:T(8,128)(2,1)S(1)}, u32[]{:S(2)}, u32[]{:S(2)}) collective-permute-start(bf16[128,512]{1,0:T(8,128)(2,1)} %param.4), channel_id=1, source_target_pairs={{0,32},{16,48},{32,0},{48,16},{1,33},{17,49},{33,1},{49,17},{2,34}... | collective-permute-start | bytes 393224 | tf_op jit(solution)/shard_map/ppermute | solution.py:257
  6.0 6.3 %collective-permute-start = (bf16[32,2048]{1,0:T(8,128)(2,1)S(1)}, bf16[32,2048]{1,0:T(8,128)(2,1)S(1)}, u32[]{:S(2)}, u32[]{:S(2)}) collective-permute-start(bf16[32,2048]{1,0:T(8,128)(2,1)S(1)} %get-tuple-element.67), channel_id=1, source_target_pairs={{0,64},{64,0},{128,192},{192,128},{1,65},{65,1},{129,193},{193,129... | collective-permute-start | bytes 393224 | tf_op jit(solution)/shard_map/ppermute | solution.py:249
  7.3 7.5 %collective-permute-start.1 = (bf16[32,2048]{1,0:T(8,128)(2,1)S(1)}, bf16[32,2048]{1,0:T(8,128)(2,1)S(1)}, u32[]{:S(2)}, u32[]{:S(2)}) collective-permute-start(bf16[32,2048]{1,0:T(8,128)(2,1)S(1)} %get-tuple-element.66), channel_id=1, source_target_pairs={{0,128},{64,192},{128,0},{192,64},{1,129},{65,193},{129,1},{193,65... | collective-permute-start | bytes 393224 | tf_op jit(solution)/shard_map/ppermute | solution.py:249
  9.7 7.9 %collective-permute-start.2 = (bf16[32,2048]{1,0:T(8,128)(2,1)S(1)}, bf16[32,2048]{1,0:T(8,128)(2,1)S(1)}, u32[]{:S(2)}, u32[]{:S(2)}) collective-permute-start(bf16[32,2048]{1,0:T(8,128)(2,1)S(1)} %get-tuple-element.65), channel_id=1, source_target_pairs={{0,192},{64,128},{128,64},{192,0},{1,193},{65,129},{129,65},{193,1... | collective-permute-start | bytes 393224 | tf_op jit(solution)/shard_map/ppermute | solution.py:249
  9.9 8.5 %collective-permute-start.4 = (bf16[256,512]{1,0:T(8,128)(2,1)S(1)}, bf16[256,512]{1,0:T(8,128)(2,1)S(1)}, u32[]{:S(2)}, u32[]{:S(2)}) collective-permute-start(bf16[256,512]{1,0:T(8,128)(2,1)S(1)} %pad_maximum_fusion.2), channel_id=1, source_target_pairs={{0,16},{16,0},{32,48},{48,32},{1,17},{17,1},{33,49},{49,33},{2,18}... | collective-permute-start | bytes 786440 | tf_op jit(solution)/shard_map/ppermute | solution.py:257
  18.5 19.4 %collective-permute-start.5 = (bf16[128,2048]{1,0:T(8,128)(2,1)}, bf16[128,2048]{1,0:T(8,128)(2,1)S(1)}, u32[]{:S(2)}, u32[]{:S(2)}) collective-permute-start(bf16[128,2048]{1,0:T(8,128)(2,1)} %pad_maximum_fusion), channel_id=1, source_target_pairs={{0,2},{1,3},{2,0},{3,1},{4,6},{5,7},{6,4},{7,5},{8,10},{9,11},{10,... | collective-permute-start | bytes 1572872 | tf_op jit(solution)/shard_map/ppermute | solution.py:261
  24.4 17.0 %collective-permute-start.7 = (bf16[128,2048]{1,0:T(8,128)(2,1)}, bf16[128,2048]{1,0:T(8,128)(2,1)}, u32[]{:S(2)}, u32[]{:S(2)}) collective-permute-start(bf16[128,2048]{1,0:T(8,128)(2,1)} %pad_maximum_fusion), channel_id=1, source_target_pairs={{0,4},{1,5},{2,6},{3,7},{4,8},{5,9},{6,10},{7,11},{8,12},{9,13},{1... | collective-permute-start | bytes 1572872 | tf_op jit(solution)/shard_map/ppermute | solution.py:253
  25.7 24.0 %collective-permute-start.8 = (bf16[128,2048]{1,0:T(8,128)(2,1)}, bf16[128,2048]{1,0:T(8,128)(2,1)}, u32[]{:S(2)}, u32[]{:S(2)}) collective-permute-start(bf16[128,2048]{1,0:T(8,128)(2,1)} %pad_maximum_fusion), channel_id=1, source_target_pairs={{0,8},{1,9},{2,10},{3,11},{4,12},{5,13},{6,14},{7,15},{8,0},{9,1},... | collective-permute-start | bytes 1572872 | tf_op jit(solution)/shard_map/ppermute | solution.py:253
  28.3 22.3 %collective-permute-start.9 = (bf16[128,2048]{1,0:T(8,128)(2,1)}, bf16[128,2048]{1,0:T(8,128)(2,1)}, u32[]{:S(2)}, u32[]{:S(2)}) collective-permute-start(bf16[128,2048]{1,0:T(8,128)(2,1)} %pad_maximum_fusion), channel_id=1, source_target_pairs={{0,12},{1,13},{2,14},{3,15},{4,0},{5,1},{6,2},{7,3},{8,4},{9,5},{1... | collective-permute-start | bytes 1572872 | tf_op jit(solution)/shard_map/ppermute | solution.py:253
  29.4 12.0 %collective-permute-start.6 = (bf16[512,512]{1,0:T(8,128)(2,1)S(1)}, bf16[512,512]{1,0:T(8,128)(2,1)}, u32[]{:S(2)}, u32[]{:S(2)}) collective-permute-start(bf16[512,512]{1,0:T(8,128)(2,1)S(1)} %pad_maximum_fusion.1.refs_0_), channel_id=1, source_target_pairs={{0,128},{64,192},{128,0},{192,64},{1,129},{65,193},{129,1},{193,65... | collective-permute-start | bytes 1572872 | tf_op jit(solution)/shard_map/ppermute | solution.py:249
  53.9 30.8 %collective-permute-start.10 = (bf16[512,2048]{1,0:T(8,128)(2,1)S(1)}, bf16[512,2048]{1,0:T(8,128)(2,1)S(1)}, u32[]{:S(2)}, u32[]{:S(2)}) collective-permute-start(bf16[512,2048]{1,0:T(8,128)(2,1)S(1)} %constant_dynamic-update-slice_fusion.own_ref), channel_id=1, source_target_pairs={{0,1},{1,0},{2,3},{3,2},{4,5},{5,4},{6,7},{7,6},{8,9},{9,8},{10,11... | collective-permute-start | bytes 6291464 | tf_op jit(solution)/shard_map/ppermute | solution.py:245
  56.1 13.5 %collective-permute-start.11 = (bf16[512,512]{1,0:T(8,128)(2,1)S(1)}, bf16[512,512]{1,0:T(8,128)(2,1)S(1)}, u32[]{:S(2)}, u32[]{:S(2)}) collective-permute-start(bf16[512,512]{1,0:T(8,128)(2,1)S(1)} %pad_maximum_fusion.1.refs_0_), channel_id=1, source_target_pairs={{0,64},{64,0},{128,192},{192,128},{1,65},{65,1},{129,193},{193,129... | collective-permute-start | bytes 1572872 | tf_op jit(solution)/shard_map/ppermute | solution.py:249
  57.3 14.4 %collective-permute-start.12 = (bf16[512,512]{1,0:T(8,128)(2,1)S(1)}, bf16[512,512]{1,0:T(8,128)(2,1)S(1)}, u32[]{:S(2)}, u32[]{:S(2)}) collective-permute-start(bf16[512,512]{1,0:T(8,128)(2,1)S(1)} %pad_maximum_fusion.1.refs_0_), channel_id=1, source_target_pairs={{0,192},{64,128},{128,64},{192,0},{1,193},{65,129},{129,65},{193,1... | collective-permute-start | bytes 1572872 | tf_op jit(solution)/shard_map/ppermute | solution.py:249
  59.1 14.3 %collective-permute-start.13 = (bf16[128,2048]{1,0:T(8,128)(2,1)S(1)}, bf16[128,2048]{1,0:T(8,128)(2,1)S(1)}, u32[]{:S(2)}, u32[]{:S(2)}) collective-permute-start(bf16[128,2048]{1,0:T(8,128)(2,1)S(1)} %collective-permute-done.5.refs_0_), channel_id=1, source_target_pairs={{0,4},{1,5},{2,6},{3,7},{4,8},{5,9},{6,10},{7,11},{8,12},{9,13},{1... | collective-permute-start | bytes 1572872 | tf_op jit(solution)/shard_map/ppermute | solution.py:253
  60.0 24.7 %collective-permute-start.14 = (bf16[128,2048]{1,0:T(8,128)(2,1)S(1)}, bf16[128,2048]{1,0:T(8,128)(2,1)S(1)}, u32[]{:S(2)}, u32[]{:S(2)}) collective-permute-start(bf16[128,2048]{1,0:T(8,128)(2,1)S(1)} %collective-permute-done.5.refs_0_), channel_id=1, source_target_pairs={{0,8},{1,9},{2,10},{3,11},{4,12},{5,13},{6,14},{7,15},{8,0},{9,1},... | collective-permute-start | bytes 1572872 | tf_op jit(solution)/shard_map/ppermute | solution.py:253
  69.6 15.1 %collective-permute-start.15 = (bf16[128,2048]{1,0:T(8,128)(2,1)S(1)}, bf16[128,2048]{1,0:T(8,128)(2,1)S(1)}, u32[]{:S(2)}, u32[]{:S(2)}) collective-permute-start(bf16[128,2048]{1,0:T(8,128)(2,1)S(1)} %collective-permute-done.5.refs_0_), channel_id=1, source_target_pairs={{0,12},{1,13},{2,14},{3,15},{4,0},{5,1},{6,2},{7,3},{8,4},{9,5},{1... | collective-permute-start | bytes 1572872 | tf_op jit(solution)/shard_map/ppermute | solution.py:253
  84.7 5.9 %collective-permute-start.16 = (bf16[128,2048]{1,0:T(8,128)(2,1)S(1)}, bf16[128,2048]{1,0:T(8,128)(2,1)S(1)}, u32[]{:S(2)}, u32[]{:S(2)}) collective-permute-start(bf16[128,2048]{1,0:T(8,128)(2,1)S(1)} %collective-permute-done.5.refs_0_), channel_id=1, source_target_pairs={{0,1},{1,0},{2,3},{3,2},{4,5},{5,4},{6,7},{7,6},{8,9},{9,8},{10,11... | collective-permute-start | bytes 1572872 | tf_op jit(solution)/shard_map/ppermute | solution.py:245
  86.5 4.1 %collective-permute-start.17 = (bf16[128,2048]{1,0:T(8,128)(2,1)S(1)}, bf16[128,2048]{1,0:T(8,128)(2,1)S(1)}, u32[]{:S(2)}, u32[]{:S(2)}) collective-permute-start(bf16[128,2048]{1,0:T(8,128)(2,1)S(1)} %collective-permute-done.13.refs_1_), channel_id=1, source_target_pairs={{0,1},{1,0},{2,3},{3,2},{4,5},{5,4},{6,7},{7,6},{8,9},{9,8},{10,11... | collective-permute-start | bytes 1572872 | tf_op jit(solution)/shard_map/ppermute | solution.py:245
  86.6 4.0 %collective-permute-start.18 = (bf16[128,2048]{1,0:T(8,128)(2,1)S(1)}, bf16[128,2048]{1,0:T(8,128)(2,1)S(1)}, u32[]{:S(2)}, u32[]{:S(2)}) collective-permute-start(bf16[128,2048]{1,0:T(8,128)(2,1)S(1)} %collective-permute-done.14.refs_2_), channel_id=1, source_target_pairs={{0,1},{1,0},{2,3},{3,2},{4,5},{5,4},{6,7},{7,6},{8,9},{9,8},{10,11... | collective-permute-start | bytes 1572872 | tf_op jit(solution)/shard_map/ppermute | solution.py:245
  87.0 3.6 %collective-permute-start.19 = (bf16[128,2048]{1,0:T(8,128)(2,1)S(1)}, bf16[128,2048]{1,0:T(8,128)(2,1)S(1)}, u32[]{:S(2)}, u32[]{:S(2)}) collective-permute-start(bf16[128,2048]{1,0:T(8,128)(2,1)S(1)} %collective-permute-done.15.refs_3_), channel_id=1, source_target_pairs={{0,1},{1,0},{2,3},{3,2},{4,5},{5,4},{6,7},{7,6},{8,9},{9,8},{10,11... | collective-permute-start | bytes 1572872 | tf_op jit(solution)/shard_map/ppermute | solution.py:245
  90.6 22.3 %copy-start = (f32[1,2048]{1,0:T(1,128)S(1)}, f32[1,2048]{1,0:T(1,128)}, u32[]{:S(2)}) copy-start(f32[1,2048]{1,0:T(1,128)} %shard_map.75.moment_ref) | copy-start | bytes 24580
  112.9 12.8 %copy-start.1 = (f32[512]{0:T(512)S(1)}, f32[512]{0:T(512)}, u32[]{:S(2)}) copy-start(f32[512]{0:T(512)} %param.6) | copy-start | bytes 6148

commit v8 on v7

--- a/solution.py
+++ b/solution.py
@@ -9,17 +9,17 @@
 FF = 32768
 VMEM_LIMIT = 20 * 1024 * 1024
 COLS = 512
-def after_kernel(value_ref, tile_ref, out_ref):
-    del tile_ref
-    out_ref[...] = value_ref[...]
-
-
-def after(value, block):
+def after_kernel(*refs):
+    refs[-1][...] = jnp.zeros_like(refs[-1])
+
+
+def after(*blocks):
     return pl.pallas_call(
         after_kernel,
-        out_shape=jax.ShapeDtypeStruct(value.shape, value.dtype),
+        in_specs=[pl.BlockSpec(memory_space=pl.ANY)] * len(blocks),
+        out_shape=pltpu.VMEM((8, 128), jnp.float32),
         cost_estimate=pl.CostEstimate(flops=1 << 34, bytes_accessed=0, transcendentals=0),
-    )(value, block[0:16, 0:128])
+    )(*blocks)
 
 
 def arrange_kernel(at_ref, *refs):
@@ -45,7 +45,8 @@
     )(at, *pieces)
 
 
-def near_kernel(x_ref, own_ref, other_ref, out_ref):
+def near_kernel(x_ref, own_ref, other_ref, first_ref, second_ref, out_ref):
+    del first_ref, second_ref
     out_ref[...] = jnp.dot(
         x_ref[:, 0:512], own_ref[...], preferred_element_type=jnp.float32
     ) + jnp.dot(x_ref[:, 512:1024], other_ref[...], preferred_element_type=jnp.float32)
@@ -104,16 +105,16 @@
 COST = pl.CostEstimate(flops=2 * 512 * 1024 * 2048, bytes_accessed=9 << 20, transcendentals=0)
 
 
-def near_product(x, own, other):
+def near_product(x, own, other, tokens):
     return pl.pallas_call(
         near_kernel,
         grid=(2048 // COLS,),
-        in_specs=[fixed(512, 1024), moving(512), moving(512)],
+        in_specs=[fixed(512, 1024), moving(512), moving(512), fixed(8, 128), fixed(8, 128)],
         out_specs=G_SPEC,
         out_shape=jax.ShapeDtypeStruct((512, 2048), jnp.float32),
         compiler_params=PARAMS,
         cost_estimate=COST,
-    )(x, own, other)
+    )(x, own, other, *tokens)
 
 
 def far_product(x, blocks, near):
@@ -289,22 +290,23 @@
     far = swap_z(near)
     nears = [move_y(near, t) for t in (1, 2, 3)]
     x2 = swap_x(x0, 2)
-    moment = after(column_moment[None], far)
-    far, moment, x0, x2, *nears = stage((far, moment, x0, x2, *nears))
+    early = after(far)
+    far, early, x0, x2, *nears = stage((far, early, x0, x2, *nears))
 
     own = jnp.concatenate([near, *nears])
     other = swap_cores(own)
     x1, x3 = swap_x(x0, 1), swap_x(x0, 3)
     fars = [move_y(far, t) for t in (1, 2, 3)]
     x_near, x_far = arrange(at, (x0, x1, x2, x3))
-    other, x_near, x_far, far, *fars = stage((other, x_near, x_far, far, *fars))
+    late = after(*fars)
+    late, x_near, x_far, far, *fars = stage((late, x_near, x_far, far, *fars))
 
     fars = [far, *fars]
     others = [swap_cores(block) for block in fars]
-    gradient = near_product(x_near, own, other)
+    gradient = near_product(x_near, own, other, (early, late))
     gradient, column_part, row_part = far_product(x_far, fars + others, gradient)
     column_state, columns, sums = weigh(
-        gradient, moment, copies(column_part, "col"), row_part
+        gradient, column_moment[None], copies(column_part, "col"), row_part
     )
     row_state, rows, totals = totals_of(row_moment[None], copies(sums, ("dp", "row")))
     update, row_mean = clip(gradient, rows, columns, copies(totals, "col"))

time: 144 us -> 140 us (0.972)
  waiting for transfers between devices: 39.9 us -> 34.5 us
  blocking collectives: 42.3 us -> 39.4 us
  local copies, waits for them, and re-layouts: 6.55 us -> 8.73 us
    ppermute x6, waiting for transfers between devices: 14.7 us -> 8.59 us  [swap_x(): return lax.ppermute(value, 'dp', flipped(4, mask))]
    all_to_all x3, blocking collectives: 42.3 us -> 39.4 us  [copies(): return lax.all_to_all(rows, axis, 0, 0).reshape(16, value.shape[1])]
    unnamed x12 -> x24, local copies, waits for them, and re-layouts: 4.63 us -> 7.41 us
  transfers between devices with their start and end apart: 20 -> 20, of which waited for: 9 -> 8; matrix products, arithmetic and copies ran while one was open for 3% -> 5% of each run, Pallas kernels for 5% -> 5%
where the time goes in v8:
time: 140 us; the launch traced here: 139 us
  blocking collectives  39.4 us (28%)
  starting transfers between devices  37.2 us (27%)
  waiting for transfers between devices  34.5 us (25%)
  Pallas kernels  17.4 us (12%)
  local copies, waits for them, and re-layouts  8.73 us (6%)
    all_to_all x3, blocking collectives, copies(): return lax.all_to_all(rows, axis, 0, 0).reshape(16, value.shape[1])  39.4 us
    ppermute x6, waiting for transfers between devices, move_y(): return lax.ppermute(value, 'col', cyclic(4, 4, shift % 4))  21.2 us
    ppermute x6, starting transfers between devices, swap_x(): return lax.ppermute(value, 'dp', flipped(4, mask))  9.72 us
    ppermute x6, starting transfers between devices, move_y(): return lax.ppermute(value, 'col', cyclic(4, 4, shift % 4))  9.58 us
    ppermute x6, waiting for transfers between devices, swap_x(): return lax.ppermute(value, 'dp', flipped(4, mask))  8.59 us
    unnamed x24, local copies, waits for them, and re-layouts  7.41 us
    ppermute x2, starting transfers between devices, swap_row(): return lax.ppermute(value, 'row', flipped(4, mask))  6.16 us
    ppermute x1, starting transfers between devices, swap_z(): return lax.ppermute(value, 'col', flipped(16, 2))  5.93 us
  transfers between devices with their start and end apart: 20, of which 8 were waited for; matrix products, arithmetic and copies ran while one was open for 5% of the time, Pallas kernels for 5%

profile of v8, /device:TPU:1, one launch (start us, length us, event | category | flops | bytes accessed | tf_op | source)
XLA Modules:
  0.0 138.9 jit_solution(13815240855705714350)
XLA Ops:
  0.6 3.9 %collective-permute-start.3 = (bf16[128,512]{1,0:T(8,128)(2,1)}, bf16[128,512]{1,0:T(8,128)(2,1)S(1)}, u32[]{:S(2)}, u32[]{:S(2)}) collective-permute-start(bf16[128,512]{1,0:T(8,128)(2,1)} %param.4), channel_id=1, source_target_pairs={{0,32},{16,48},{32,0},{48,16},{1,33},{17,49},{33,1},{49,17},{2,34}... | collective-permute-start | bytes 393224 | tf_op jit(solution)/shard_map/ppermute | solution.py:258
  7.3 2.5 %collective-permute-start.1 = (bf16[32,2048]{1,0:T(8,128)(2,1)S(1)}, bf16[32,2048]{1,0:T(8,128)(2,1)S(1)}, u32[]{:S(2)}, u32[]{:S(2)}) collective-permute-start(bf16[32,2048]{1,0:T(8,128)(2,1)S(1)} %get-tuple-element.66), channel_id=1, source_target_pairs={{0,128},{64,192},{128,0},{192,64},{1,129},{65,193},{129,1},{193,65... | collective-permute-start | bytes 393224 | tf_op jit(solution)/shard_map/ppermute | solution.py:250
  9.9 2.3 %collective-permute-start.4 = (bf16[256,512]{1,0:T(8,128)(2,1)S(1)}, bf16[256,512]{1,0:T(8,128)(2,1)S(1)}, u32[]{:S(2)}, u32[]{:S(2)}) collective-permute-start(bf16[256,512]{1,0:T(8,128)(2,1)S(1)} %pad_maximum_fusion.2), channel_id=1, source_target_pairs={{0,16},{16,0},{32,48},{48,32},{1,17},{17,1},{33,49},{49,33},{2,18}... | collective-permute-start | bytes 786440 | tf_op jit(solution)/shard_map/ppermute | solution.py:258
  12.3 2.5 %collective-permute-done.1 = bf16[32,2048]{1,0:T(8,128)(2,1)S(1)} collective-permute-done((bf16[32,2048]{1,0:T(8,128)(2,1)S(1)}, bf16[32,2048]{1,0:T(8,128)(2,1)S(1)}, u32[]{:S(2)}, u32[]{:S(2)}) %collective-permute-start.1) | collective-permute-done | bytes 131104 | tf_op jit(solution)/shard_map/ppermute | solution.py:250
  14.8 2.8 %collective-permute-done.2 = bf16[32,2048]{1,0:T(8,128)(2,1)S(1)} collective-permute-done((bf16[32,2048]{1,0:T(8,128)(2,1)S(1)}, bf16[32,2048]{1,0:T(8,128)(2,1)S(1)}, u32[]{:S(2)}, u32[]{:S(2)}) %collective-permute-start.2) | collective-permute-done | bytes 131104 | tf_op jit(solution)/shard_map/ppermute | solution.py:250
  18.5 5.9 %collective-permute-start.5 = (bf16[128,2048]{1,0:T(8,128)(2,1)}, bf16[128,2048]{1,0:T(8,128)(2,1)S(1)}, u32[]{:S(2)}, u32[]{:S(2)}) collective-permute-start(bf16[128,2048]{1,0:T(8,128)(2,1)} %pad_maximum_fusion), channel_id=1, source_target_pairs={{0,2},{1,3},{2,0},{3,1},{4,6},{5,7},{6,4},{7,5},{8,10},{9,11},{10,... | collective-permute-start | bytes 1572872 | tf_op jit(solution)/shard_map/ppermute | solution.py:262
  25.7 2.6 %collective-permute-start.8 = (bf16[128,2048]{1,0:T(8,128)(2,1)}, bf16[128,2048]{1,0:T(8,128)(2,1)}, u32[]{:S(2)}, u32[]{:S(2)}) collective-permute-start(bf16[128,2048]{1,0:T(8,128)(2,1)} %pad_maximum_fusion), channel_id=1, source_target_pairs={{0,8},{1,9},{2,10},{3,11},{4,12},{5,13},{6,14},{7,15},{8,0},{9,1},... | collective-permute-start | bytes 1572872 | tf_op jit(solution)/shard_map/ppermute | solution.py:254
  29.4 2.7 %collective-permute-start.6 = (bf16[512,512]{1,0:T(8,128)(2,1)S(1)}, bf16[512,512]{1,0:T(8,128)(2,1)}, u32[]{:S(2)}, u32[]{:S(2)}) collective-permute-start(bf16[512,512]{1,0:T(8,128)(2,1)S(1)} %pad_maximum_fusion.1.refs_0_), channel_id=1, source_target_pairs={{0,128},{64,192},{128,0},{192,64},{1,129},{65,193},{129,1},{193,65... | collective-permute-start | bytes 1572872 | tf_op jit(solution)/shard_map/ppermute | solution.py:250
  33.2 4.7 %collective-permute-done.5.refs_0_ = bf16[128,2048]{1,0:T(8,128)(2,1)S(1)} collective-permute-done((bf16[128,2048]{1,0:T(8,128)(2,1)}, bf16[128,2048]{1,0:T(8,128)(2,1)S(1)}, u32[]{:S(2)}, u32[]{:S(2)}) %collective-permute-start.5) | collective-permute-done | bytes 524320 | tf_op jit(solution)/shard_map/ppermute | solution.py:262
  38.7 2.7 %collective-permute-done.6.refs_2_ = bf16[512,512]{1,0:T(8,128)(2,1)} collective-permute-done((bf16[512,512]{1,0:T(8,128)(2,1)S(1)}, bf16[512,512]{1,0:T(8,128)(2,1)}, u32[]{:S(2)}, u32[]{:S(2)}) %collective-permute-start.6) | collective-permute-done | bytes 524320 | tf_op jit(solution)/shard_map/ppermute | solution.py:250
  41.4 8.2 %collective-permute-done.8 = bf16[128,2048]{1,0:T(8,128)(2,1)} collective-permute-done((bf16[128,2048]{1,0:T(8,128)(2,1)}, bf16[128,2048]{1,0:T(8,128)(2,1)}, u32[]{:S(2)}, u32[]{:S(2)}) %collective-permute-start.8) | collective-permute-done | bytes 524320 | tf_op jit(solution)/shard_map/ppermute | solution.py:254
  51.9 1.8 %collective-permute-start.14 = (bf16[512,512]{1,0:T(8,128)(2,1)S(1)}, bf16[512,512]{1,0:T(8,128)(2,1)S(1)}, u32[]{:S(2)}, u32[]{:S(2)}) collective-permute-start(bf16[512,512]{1,0:T(8,128)(2,1)S(1)} %pad_maximum_fusion.1.refs_0_), channel_id=1, source_target_pairs={{0,192},{64,128},{128,64},{192,0},{1,193},{65,129},{129,65},{193,1... | collective-permute-start | bytes 1572872 | tf_op jit(solution)/shard_map/ppermute | solution.py:250
  55.3 3.0 %collective-permute-start.11 = (bf16[128,2048]{1,0:T(8,128)(2,1)}, bf16[128,2048]{1,0:T(8,128)(2,1)}, u32[]{:S(2)}, u32[]{:S(2)}) collective-permute-start(bf16[128,2048]{1,0:T(8,128)(2,1)} %copy-done.4), channel_id=1, source_target_pairs={{0,8},{1,9},{2,10},{3,11},{4,12},{5,13},{6,14},{7,15},{8,0},{9,1},... | collective-permute-start | bytes 1572872 | tf_op jit(solution)/shard_map/ppermute | solution.py:254
  62.0 2.9 %collective-permute-start.19 = (bf16[512,2048]{1,0:T(8,128)(2,1)S(1)}, bf16[512,2048]{1,0:T(8,128)(2,1)}, u32[]{:S(2)}, u32[]{:S(2)}) collective-permute-start(bf16[512,2048]{1,0:T(8,128)(2,1)S(1)} %constant_dynamic-update-slice_fusion.own_ref), channel_id=1, source_target_pairs={{0,1},{1,0},{2,3},{3,2},{4,5},{5,4},{6,7},{7,6},{8,9},{9,8},{10,11... | collective-permute-start | bytes 6291464 | tf_op jit(solution)/shard_map/ppermute | solution.py:246
  65.0 1.7 %shard_map.77 = (bf16[512,1024]{1,0:T(8,128)(2,1)S(1)}, bf16[512,1024]{1,0:T(8,128)(2,1)S(1)}) custom-call(s32[8]{0:T(128)S(1)} %stack.35.at_ref, bf16[512,512]{1,0:T(8,128)(2,1)S(1)} %pad_maximum_fusion.1.refs_0_, bf16[512,512]{1,0:T(8,128)(2,1)S(1)} %collective-permute-done.13.refs_1_, bf16[512,512]{1,0:T(8,128)(2,1)} %collective-permute-done.6.refs_2_, ...), custom_call_target="tpu_custom_call" | custom-call | bytes 4194304 | tf_op jit(solution)/shard_map/pallas_call | solution.py:38
  68.7 12.0 %collective-permute-done.11.refs_1_.refs_2_ = bf16[128,2048]{1,0:T(8,128)(2,1)} collective-permute-done((bf16[128,2048]{1,0:T(8,128)(2,1)}, bf16[128,2048]{1,0:T(8,128)(2,1)}, u32[]{:S(2)}, u32[]{:S(2)}) %collective-permute-start.11) | collective-permute-done | bytes 524320 | tf_op jit(solution)/shard_map/ppermute | solution.py:254
  80.7 2.1 %collective-permute-start.15 = (bf16[128,2048]{1,0:T(8,128)(2,1)}, bf16[128,2048]{1,0:T(8,128)(2,1)S(1)}, u32[]{:S(2)}, u32[]{:S(2)}) collective-permute-start(bf16[128,2048]{1,0:T(8,128)(2,1)} %copy-done.4), channel_id=1, source_target_pairs={{0,1},{1,0},{2,3},{3,2},{4,5},{5,4},{6,7},{7,6},{8,9},{9,8},{10,11... | collective-permute-start | bytes 1572872 | tf_op jit(solution)/shard_map/ppermute | solution.py:246
  83.6 4.6 %shard_map.78.refs_8_ = f32[512,2048]{1,0:T(8,128)S(1)} custom-call(bf16[512,1024]{1,0:T(8,128)(2,1)S(1)} %copy-done.3, bf16[512,2048]{1,0:T(8,128)(2,1)S(1)} %constant_dynamic-update-slice_fusion.own_ref, bf16[512,2048]{1,0:T(8,128)(2,1)} %collective-permute-done.19.other_ref, f32[8,128]{1,0:T(8,128)S(1)} %shard_map.75.first_ref, ...), custom_call_target="tpu_custom_call" | custom-call | flops 2147483648 | bytes 9437184 | tf_op jit(solution)/shard_map/pallas_call | solution.py:109
  88.2 5.0 %shard_map.79 = (f32[512,2048]{1,0:T(8,128)S(1)}, f32[1,2048]{1,0:T(1,128)S(1)}, f32[1,512]{1,0:T(1,128)S(1)}) custom-call(bf16[512,1024]{1,0:T(8,128)(2,1)S(1)} %copy-done.1, bf16[128,2048]{1,0:T(8,128)(2,1)S(1)} %copy-done.5, bf16[128,2048]{1,0:T(8,128)(2,1)} %collective-permute-done.10.refs_0_.refs_1_, ...), custom_call_target="tpu_custom_call" | custom-call | flops 2147483648 | bytes 9437184 | tf_op jit(solution)/shard_map/pallas_call | solution.py:121
  93.3 13.4 %all_to_all.15 = f32[16,1,2048]{2,1,0:T(1,128)S(1)} all-to-all(f32[16,1,2048]{2,1,0:T(1,128)S(1)} %broadcast_in_dim.17), channel_id=1, replica_groups=mesh['dp'=4,'row'=4,'col'=16] {'col'}, dimensions={0} | all-to-all | bytes 262144 | tf_op jit(solution)/shard_map/all_to_all | solution.py:267
  106.8 2.3 %shard_map.80 = (f32[1,2048]{1,0:T(1,128)}, f32[1,2048]{1,0:T(1,128)S(1)}, f32[1,1024]{1,0:T(1,128)S(1)}) custom-call(f32[512,2048]{1,0:T(8,128)S(1)} %get-tuple-element.53.g_ref, f32[1,2048]{1,0:T(1,128)S(1)} %bitcast.37, f32[16,2048]{1,0:T(8,128)S(1)} %bitcast.34, f32[1,512]{1,0:T(1,128)S(1)} %get-tuple-element.55.row_ref), custom_call_target="tpu_custom_call" | custom-call | flops 4194304 | bytes 4194304 | tf_op jit(solution)/shard_map/pallas_call | solution.py:155
  109.1 12.3 %all_to_all.16 = f32[16,1,1024]{2,1,0:T(1,128)S(1)} all-to-all(f32[16,1,1024]{2,1,0:T(1,128)S(1)} %broadcast_in_dim.18), channel_id=1, replica_groups=mesh['dp'=4,'row'=4,'col'=16] {'dp','row'}, dimensions={0} | all-to-all | bytes 131072 | tf_op jit(solution)/shard_map/all_to_all | solution.py:267
  122.0 13.7 %all_to_all.17 = f32[16,1,128]{2,1,0:T(1,128)S(1)} all-to-all(f32[16,1,128]{2,1,0:T(1,128)S(1)} %broadcast_in_dim.19), channel_id=1, replica_groups=mesh['dp'=4,'row'=4,'col'=16] {'col'}, dimensions={0} | all-to-all | bytes 16384 | tf_op jit(solution)/shard_map/all_to_all | solution.py:267
  135.7 3.2 %shard_map.82 = (f32[512,2048]{1,0:T(8,128)}, f32[1,1]{1,0:T(1,128)}) custom-call(f32[512,2048]{1,0:T(8,128)S(1)} %get-tuple-element.53.g_ref, f32[1,512]{1,0:T(1,128)S(1)} %get-tuple-element.57.row_ref, f32[1,2048]{1,0:T(1,128)S(1)} %get-tuple-element.58.col_ref, f32[16,128]{1,0:T(8,128)S(1)} %bitcast.36), custom_call_target="tpu_custom_call" | custom-call | flops 2097152 | bytes 8388608 | tf_op jit(solution)/shard_map/pallas_call | solution.py:219
  (60 shorter events, 19.2 us)
Async XLA Ops:
  0.6 9.3 %copy-start.8 = (bf16[128,512]{1,0:T(8,128)(2,1)S(1)}, bf16[128,512]{1,0:T(8,128)(2,1)}, u32[]{:S(2)}) copy-start(bf16[128,512]{1,0:T(8,128)(2,1)} %param.4) | copy-start | bytes 393220
  0.6 9.3 %collective-permute-start.3 = (bf16[128,512]{1,0:T(8,128)(2,1)}, bf16[128,512]{1,0:T(8,128)(2,1)S(1)}, u32[]{:S(2)}, u32[]{:S(2)}) collective-permute-start(bf16[128,512]{1,0:T(8,128)(2,1)} %param.4), channel_id=1, source_target_pairs={{0,32},{16,48},{32,0},{48,16},{1,33},{17,49},{33,1},{49,17},{2,34}... | collective-permute-start | bytes 393224 | tf_op jit(solution)/shard_map/ppermute | solution.py:258
  6.0 6.3 %collective-permute-start = (bf16[32,2048]{1,0:T(8,128)(2,1)S(1)}, bf16[32,2048]{1,0:T(8,128)(2,1)S(1)}, u32[]{:S(2)}, u32[]{:S(2)}) collective-permute-start(bf16[32,2048]{1,0:T(8,128)(2,1)S(1)} %get-tuple-element.67), channel_id=1, source_target_pairs={{0,64},{64,0},{128,192},{192,128},{1,65},{65,1},{129,193},{193,129... | collective-permute-start | bytes 393224 | tf_op jit(solution)/shard_map/ppermute | solution.py:250
  7.3 7.5 %collective-permute-start.1 = (bf16[32,2048]{1,0:T(8,128)(2,1)S(1)}, bf16[32,2048]{1,0:T(8,128)(2,1)S(1)}, u32[]{:S(2)}, u32[]{:S(2)}) collective-permute-start(bf16[32,2048]{1,0:T(8,128)(2,1)S(1)} %get-tuple-element.66), channel_id=1, source_target_pairs={{0,128},{64,192},{128,0},{192,64},{1,129},{65,193},{129,1},{193,65... | collective-permute-start | bytes 393224 | tf_op jit(solution)/shard_map/ppermute | solution.py:250
  9.7 7.9 %collective-permute-start.2 = (bf16[32,2048]{1,0:T(8,128)(2,1)S(1)}, bf16[32,2048]{1,0:T(8,128)(2,1)S(1)}, u32[]{:S(2)}, u32[]{:S(2)}) collective-permute-start(bf16[32,2048]{1,0:T(8,128)(2,1)S(1)} %get-tuple-element.65), channel_id=1, source_target_pairs={{0,192},{64,128},{128,64},{192,0},{1,193},{65,129},{129,65},{193,1... | collective-permute-start | bytes 393224 | tf_op jit(solution)/shard_map/ppermute | solution.py:250
  9.9 8.5 %collective-permute-start.4 = (bf16[256,512]{1,0:T(8,128)(2,1)S(1)}, bf16[256,512]{1,0:T(8,128)(2,1)S(1)}, u32[]{:S(2)}, u32[]{:S(2)}) collective-permute-start(bf16[256,512]{1,0:T(8,128)(2,1)S(1)} %pad_maximum_fusion.2), channel_id=1, source_target_pairs={{0,16},{16,0},{32,48},{48,32},{1,17},{17,1},{33,49},{49,33},{2,18}... | collective-permute-start | bytes 786440 | tf_op jit(solution)/shard_map/ppermute | solution.py:258
  18.5 19.4 %collective-permute-start.5 = (bf16[128,2048]{1,0:T(8,128)(2,1)}, bf16[128,2048]{1,0:T(8,128)(2,1)S(1)}, u32[]{:S(2)}, u32[]{:S(2)}) collective-permute-start(bf16[128,2048]{1,0:T(8,128)(2,1)} %pad_maximum_fusion), channel_id=1, source_target_pairs={{0,2},{1,3},{2,0},{3,1},{4,6},{5,7},{6,4},{7,5},{8,10},{9,11},{10,... | collective-permute-start | bytes 1572872 | tf_op jit(solution)/shard_map/ppermute | solution.py:262
  24.4 17.0 %collective-permute-start.7 = (bf16[128,2048]{1,0:T(8,128)(2,1)}, bf16[128,2048]{1,0:T(8,128)(2,1)}, u32[]{:S(2)}, u32[]{:S(2)}) collective-permute-start(bf16[128,2048]{1,0:T(8,128)(2,1)} %pad_maximum_fusion), channel_id=1, source_target_pairs={{0,4},{1,5},{2,6},{3,7},{4,8},{5,9},{6,10},{7,11},{8,12},{9,13},{1... | collective-permute-start | bytes 1572872 | tf_op jit(solution)/shard_map/ppermute | solution.py:254
  25.7 24.0 %collective-permute-start.8 = (bf16[128,2048]{1,0:T(8,128)(2,1)}, bf16[128,2048]{1,0:T(8,128)(2,1)}, u32[]{:S(2)}, u32[]{:S(2)}) collective-permute-start(bf16[128,2048]{1,0:T(8,128)(2,1)} %pad_maximum_fusion), channel_id=1, source_target_pairs={{0,8},{1,9},{2,10},{3,11},{4,12},{5,13},{6,14},{7,15},{8,0},{9,1},... | collective-permute-start | bytes 1572872 | tf_op jit(solution)/shard_map/ppermute | solution.py:254
  28.3 22.3 %collective-permute-start.9 = (bf16[128,2048]{1,0:T(8,128)(2,1)}, bf16[128,2048]{1,0:T(8,128)(2,1)}, u32[]{:S(2)}, u32[]{:S(2)}) collective-permute-start(bf16[128,2048]{1,0:T(8,128)(2,1)} %pad_maximum_fusion), channel_id=1, source_target_pairs={{0,12},{1,13},{2,14},{3,15},{4,0},{5,1},{6,2},{7,3},{8,4},{9,5},{1... | collective-permute-start | bytes 1572872 | tf_op jit(solution)/shard_map/ppermute | solution.py:254
  29.4 12.0 %collective-permute-start.6 = (bf16[512,512]{1,0:T(8,128)(2,1)S(1)}, bf16[512,512]{1,0:T(8,128)(2,1)}, u32[]{:S(2)}, u32[]{:S(2)}) collective-permute-start(bf16[512,512]{1,0:T(8,128)(2,1)S(1)} %pad_maximum_fusion.1.refs_0_), channel_id=1, source_target_pairs={{0,128},{64,192},{128,0},{192,64},{1,129},{65,193},{129,1},{193,65... | collective-permute-start | bytes 1572872 | tf_op jit(solution)/shard_map/ppermute | solution.py:250
  50.6 11.4 %collective-permute-start.13 = (bf16[512,512]{1,0:T(8,128)(2,1)S(1)}, bf16[512,512]{1,0:T(8,128)(2,1)S(1)}, u32[]{:S(2)}, u32[]{:S(2)}) collective-permute-start(bf16[512,512]{1,0:T(8,128)(2,1)S(1)} %pad_maximum_fusion.1.refs_0_), channel_id=1, source_target_pairs={{0,64},{64,0},{128,192},{192,128},{1,65},{65,1},{129,193},{193,129... | collective-permute-start | bytes 1572872 | tf_op jit(solution)/shard_map/ppermute | solution.py:250
  51.9 13.1 %collective-permute-start.14 = (bf16[512,512]{1,0:T(8,128)(2,1)S(1)}, bf16[512,512]{1,0:T(8,128)(2,1)S(1)}, u32[]{:S(2)}, u32[]{:S(2)}) collective-permute-start(bf16[512,512]{1,0:T(8,128)(2,1)S(1)} %pad_maximum_fusion.1.refs_0_), channel_id=1, source_target_pairs={{0,192},{64,128},{128,64},{192,0},{1,193},{65,129},{129,65},{193,1... | collective-permute-start | bytes 1572872 | tf_op jit(solution)/shard_map/ppermute | solution.py:250
  53.7 15.0 %collective-permute-start.10 = (bf16[128,2048]{1,0:T(8,128)(2,1)}, bf16[128,2048]{1,0:T(8,128)(2,1)}, u32[]{:S(2)}, u32[]{:S(2)}) collective-permute-start(bf16[128,2048]{1,0:T(8,128)(2,1)} %copy-done.4), channel_id=1, source_target_pairs={{0,4},{1,5},{2,6},{3,7},{4,8},{5,9},{6,10},{7,11},{8,12},{9,13},{1... | collective-permute-start | bytes 1572872 | tf_op jit(solution)/shard_map/ppermute | solution.py:254
  55.3 25.4 %collective-permute-start.11 = (bf16[128,2048]{1,0:T(8,128)(2,1)}, bf16[128,2048]{1,0:T(8,128)(2,1)}, u32[]{:S(2)}, u32[]{:S(2)}) collective-permute-start(bf16[128,2048]{1,0:T(8,128)(2,1)} %copy-done.4), channel_id=1, source_target_pairs={{0,8},{1,9},{2,10},{3,11},{4,12},{5,13},{6,14},{7,15},{8,0},{9,1},... | collective-permute-start | bytes 1572872 | tf_op jit(solution)/shard_map/ppermute | solution.py:254
  58.3 22.5 %collective-permute-start.12 = (bf16[128,2048]{1,0:T(8,128)(2,1)}, bf16[128,2048]{1,0:T(8,128)(2,1)}, u32[]{:S(2)}, u32[]{:S(2)}) collective-permute-start(bf16[128,2048]{1,0:T(8,128)(2,1)} %copy-done.4), channel_id=1, source_target_pairs={{0,12},{1,13},{2,14},{3,15},{4,0},{5,1},{6,2},{7,3},{8,4},{9,5},{1... | collective-permute-start | bytes 1572872 | tf_op jit(solution)/shard_map/ppermute | solution.py:254
  62.0 21.5 %collective-permute-start.19 = (bf16[512,2048]{1,0:T(8,128)(2,1)S(1)}, bf16[512,2048]{1,0:T(8,128)(2,1)}, u32[]{:S(2)}, u32[]{:S(2)}) collective-permute-start(bf16[512,2048]{1,0:T(8,128)(2,1)S(1)} %constant_dynamic-update-slice_fusion.own_ref), channel_id=1, source_target_pairs={{0,1},{1,0},{2,3},{3,2},{4,5},{5,4},{6,7},{7,6},{8,9},{9,8},{10,11... | collective-permute-start | bytes 6291464 | tf_op jit(solution)/shard_map/ppermute | solution.py:246
  68.7 14.9 %copy-start.3 = (bf16[512,1024]{1,0:T(8,128)(2,1)S(1)}, bf16[512,1024]{1,0:T(8,128)(2,1)}, u32[]{:S(2)}) copy-start(bf16[512,1024]{1,0:T(8,128)(2,1)} %copy-done.2) | copy-start | bytes 3145732
  80.7 7.4 %collective-permute-start.15 = (bf16[128,2048]{1,0:T(8,128)(2,1)}, bf16[128,2048]{1,0:T(8,128)(2,1)S(1)}, u32[]{:S(2)}, u32[]{:S(2)}) collective-permute-start(bf16[128,2048]{1,0:T(8,128)(2,1)} %copy-done.4), channel_id=1, source_target_pairs={{0,1},{1,0},{2,3},{3,2},{4,5},{5,4},{6,7},{7,6},{8,9},{9,8},{10,11... | collective-permute-start | bytes 1572872 | tf_op jit(solution)/shard_map/ppermute | solution.py:246
  82.8 5.4 %collective-permute-start.16 = (bf16[128,2048]{1,0:T(8,128)(2,1)}, bf16[128,2048]{1,0:T(8,128)(2,1)S(1)}, u32[]{:S(2)}, u32[]{:S(2)}) collective-permute-start(bf16[128,2048]{1,0:T(8,128)(2,1)} %collective-permute-done.10.refs_0_.refs_1_), channel_id=1, source_target_pairs={{0,1},{1,0},{2,3},{3,2},{4,5},{5,4},{6,7},{7,6},{8,9},{9,8},{10,11... | collective-permute-start | bytes 1572872 | tf_op jit(solution)/shard_map/ppermute | solution.py:246
  83.1 5.1 %collective-permute-start.17 = (bf16[128,2048]{1,0:T(8,128)(2,1)}, bf16[128,2048]{1,0:T(8,128)(2,1)S(1)}, u32[]{:S(2)}, u32[]{:S(2)}) collective-permute-start(bf16[128,2048]{1,0:T(8,128)(2,1)} %collective-permute-done.11.refs_1_.refs_2_), channel_id=1, source_target_pairs={{0,1},{1,0},{2,3},{3,2},{4,5},{5,4},{6,7},{7,6},{8,9},{9,8},{10,11... | collective-permute-start | bytes 1572872 | tf_op jit(solution)/shard_map/ppermute | solution.py:246
  83.3 4.9 %collective-permute-start.18 = (bf16[128,2048]{1,0:T(8,128)(2,1)}, bf16[128,2048]{1,0:T(8,128)(2,1)S(1)}, u32[]{:S(2)}, u32[]{:S(2)}) collective-permute-start(bf16[128,2048]{1,0:T(8,128)(2,1)} %collective-permute-done.12.refs_2_.refs_3_), channel_id=1, source_target_pairs={{0,1},{1,0},{2,3},{3,2},{4,5},{5,4},{6,7},{7,6},{8,9},{9,8},{10,11... | collective-permute-start | bytes 1572872 | tf_op jit(solution)/shard_map/ppermute | solution.py:246
  88.2 18.6 %copy-start.6 = (f32[2048]{0:T(1024)S(1)}, f32[2048]{0:T(1024)}, u32[]{:S(2)}) copy-start(f32[2048]{0:T(1024)} %param.7) | copy-start | bytes 24580
  106.8 14.6 %copy-start.7 = (f32[512]{0:T(512)S(1)}, f32[512]{0:T(512)}, u32[]{:S(2)}) copy-start(f32[512]{0:T(512)} %param.6) | copy-start | bytes 6148
  (5 other events, 17.8 us)

commit v9 on v8

--- a/solution.py
+++ b/solution.py
@@ -13,24 +13,29 @@
     refs[-1][...] = jnp.zeros_like(refs[-1])
 
 
-def after(*blocks):
+def after(*blocks, scale=34):
     return pl.pallas_call(
         after_kernel,
         in_specs=[pl.BlockSpec(memory_space=pl.ANY)] * len(blocks),
         out_shape=pltpu.VMEM((8, 128), jnp.float32),
-        cost_estimate=pl.CostEstimate(flops=1 << 34, bytes_accessed=0, transcendentals=0),
+        cost_estimate=pl.CostEstimate(flops=1 << scale, bytes_accessed=0, transcendentals=0),
     )(*blocks)
+
+
+NEAR = [(s, t, far) for t in range(4) for s, far in ((0, 0), (1, 0), (2, 0), (3, 0), (0, 1))]
+FAR = [(s, t, 1) for t in range(4) for s in (1, 2, 3)]
 
 
 def arrange_kernel(at_ref, *refs):
     pieces = refs[:4]
-    for far, out_ref in enumerate(refs[4:]):
-        for other in (0, 1):
-            for t in range(4):
+    for order, out_ref in zip((NEAR, FAR), refs[4:]):
+        blocks = [block + (other,) for other in (0, 1) for block in order]
+        for k in range(0, len(blocks), 4):
+            rows = []
+            for s, t, far, other in blocks[k : k + 4]:
                 start = pl.multiple_of(at_ref[t] + at_ref[4 + far] + at_ref[6 + other], 32)
-                rows = [piece[pl.ds(start, 32), :] for piece in pieces]
-                column = other * 512 + t * 128
-                out_ref[:, column : column + 128] = jnp.concatenate(rows, axis=0).T
+                rows.append(pieces[s][pl.ds(start, 32), :])
+            out_ref[:, 32 * k : 32 * k + 128] = jnp.concatenate(rows, axis=0).T
 
 
 def arrange(at, pieces):
@@ -39,7 +44,9 @@
         arrange_kernel,
         in_specs=[pl.BlockSpec(memory_space=pltpu.SMEM)] + [whole] * 4,
         out_specs=[whole] * 2,
-        out_shape=[jax.ShapeDtypeStruct((512, 1024), jnp.bfloat16)] * 2,
+        out_shape=[
+            jax.ShapeDtypeStruct((512, 64 * len(order)), jnp.bfloat16) for order in (NEAR, FAR)
+        ],
         compiler_params=PARAMS,
         cost_estimate=pl.CostEstimate(flops=0, bytes_accessed=4 << 20, transcendentals=0),
     )(at, *pieces)
@@ -48,8 +55,8 @@
 def near_kernel(x_ref, own_ref, other_ref, first_ref, second_ref, out_ref):
     del first_ref, second_ref
     out_ref[...] = jnp.dot(
-        x_ref[:, 0:512], own_ref[...], preferred_element_type=jnp.float32
-    ) + jnp.dot(x_ref[:, 512:1024], other_ref[...], preferred_element_type=jnp.float32)
+        x_ref[:, 0:640], own_ref[...], preferred_element_type=jnp.float32
+    ) + jnp.dot(x_ref[:, 640:1280], other_ref[...], preferred_element_type=jnp.float32)
 
 
 def across(value):
@@ -78,7 +85,7 @@
     value = near_ref[...]
     for half in (0, 1):
         g = jnp.concatenate([ref[...] for ref in blocks[4 * half : 4 * half + 4]], axis=0)
-        x = x_ref[:, 512 * half : 512 * half + 512]
+        x = x_ref[:, 384 * half : 384 * half + 384]
         value += jnp.dot(x, g, preferred_element_type=jnp.float32)
     out_ref[...] = value
     squares = value * value + 1e-30
@@ -109,7 +116,7 @@
     return pl.pallas_call(
         near_kernel,
         grid=(2048 // COLS,),
-        in_specs=[fixed(512, 1024), moving(512), moving(512), fixed(8, 128), fixed(8, 128)],
+        in_specs=[fixed(512, 1280), moving(640), moving(640), fixed(8, 128), fixed(8, 128)],
         out_specs=G_SPEC,
         out_shape=jax.ShapeDtypeStruct((512, 2048), jnp.float32),
         compiler_params=PARAMS,
@@ -121,7 +128,7 @@
     return pl.pallas_call(
         far_kernel,
         grid=(2048 // COLS,),
-        in_specs=[fixed(512, 1024)] + [moving(128)] * 8 + [G_SPEC],
+        in_specs=[fixed(512, 768)] + [moving(96)] * 8 + [G_SPEC],
         out_specs=[G_SPEC, moving(1), fixed(1, 512)],
         out_shape=[
             pltpu.VMEM((512, 2048), jnp.float32),
@@ -283,22 +290,26 @@
     groups = [
         lax.dynamic_index_in_dim(by_group, me ^ s, 0, keepdims=False) for s in range(4)
     ]
-    blocks = [groups[0]] + [swap_x(groups[s], s) for s in (1, 2, 3)]
+    far0 = swap_z(groups[0])
+    blocks = [swap_x(groups[s], s) for s in (1, 2, 3)]
+    near = jnp.concatenate([groups[0]] + blocks + [far0])
+    near, rest, pair, at = stage((near, jnp.concatenate(blocks), pair, at))
+
+    far = swap_z(rest)
+    near1, near3 = move_y(near, 1), move_y(near, -1)
     x0 = jnp.concatenate([pair, swap_row(pair, 1)])
-    near, x0, at = stage((jnp.concatenate(blocks), x0, at))
-
-    far = swap_z(near)
-    nears = [move_y(near, t) for t in (1, 2, 3)]
+    near1, near3, x0 = stage((near1, near3, x0))
+    near2a, near2b = move_y(near1[0:80], 1), move_y(near3[80:160], -1)
+    x1, x3 = swap_x(x0, 1), swap_x(x0, 3)
+    early = after(far)
+    far, early, x0, x1, x3, near2a, near2b = stage((far, early, x0, x1, x3, near2a, near2b))
+
+    own = jnp.concatenate([near, near1, near2a, near2b, near3])
+    other = swap_cores(own)
     x2 = swap_x(x0, 2)
-    early = after(far)
-    far, early, x0, x2, *nears = stage((far, early, x0, x2, *nears))
-
-    own = jnp.concatenate([near, *nears])
-    other = swap_cores(own)
-    x1, x3 = swap_x(x0, 1), swap_x(x0, 3)
     fars = [move_y(far, t) for t in (1, 2, 3)]
     x_near, x_far = arrange(at, (x0, x1, x2, x3))
-    late = after(*fars)
+    late = after(x_far, *fars, scale=35)
     late, x_near, x_far, far, *fars = stage((late, x_near, x_far, far, *fars))
 
     fars = [far, *fars]

time: 140 us -> 155 us (1.11)
  waiting for transfers between devices: 34.5 us -> 44.3 us
  local copies, waits for them, and re-layouts: 8.73 us -> 15.7 us
  starting transfers between devices: 37.2 us -> 34.3 us
  blocking collectives: 39.4 us -> 41.9 us
    ppermute x2, waiting for transfers between devices: 0.01 us -> 30.7 us  [swap_row(): return lax.ppermute(value, 'row', flipped(4, mask))]
    ppermute x6 -> x7, waiting for transfers between devices: 21.2 us -> 5.22 us  [move_y(): return lax.ppermute(value, 'col', cyclic(4, 4, shift % 4))]
    unnamed x24 -> x47, local copies, waits for them, and re-layouts: 7.41 us -> 13.3 us
    ppermute x2, starting transfers between devices: 6.16 us -> 1.2 us  [swap_row(): return lax.ppermute(value, 'row', flipped(4, mask))]
    ppermute x1 -> x2, waiting for transfers between devices: 4.7 us -> 0.01 us  [swap_z(): return lax.ppermute(value, 'col', flipped(16, 2))]
    ppermute x1 -> x2, starting transfers between devices: 5.93 us -> 9 us  [swap_z(): return lax.ppermute(value, 'col', flipped(16, 2))]
    all_to_all x3, blocking collectives: 39.4 us -> 41.9 us  [copies(): return lax.all_to_all(rows, axis, 0, 0).reshape(16, value.shape[1])]
    ppermute x6, starting transfers between devices: 9.72 us -> 7.39 us  [swap_x(): return lax.ppermute(value, 'dp', flipped(4, mask))]
  transfers between devices with their start and end apart: 20 -> 22, of which waited for: 8 -> 7; matrix products, arithmetic and copies ran while one was open for 5% -> 6% of each run, Pallas kernels for 5% -> 5%
where the time goes in v9:
time: 155 us
  waiting for transfers between devices  44.3 us (29%)
  blocking collectives  41.9 us (27%)
  starting transfers between devices  34.3 us (22%)
  Pallas kernels  17.6 us (11%)
  local copies, waits for them, and re-layouts  15.7 us (10%)
    all_to_all x3, blocking collectives, copies(): return lax.all_to_all(rows, axis, 0, 0).reshape(16, value.shape[1])  41.9 us
    ppermute x2, waiting for transfers between devices, swap_row(): return lax.ppermute(value, 'row', flipped(4, mask))  30.7 us
    unnamed x47, local copies, waits for them, and re-layouts  13.3 us
    ppermute x7, starting transfers between devices, move_y(): return lax.ppermute(value, 'col', cyclic(4, 4, shift % 4))  9.13 us
    ppermute x2, starting transfers between devices, swap_z(): return lax.ppermute(value, 'col', flipped(16, 2))  9 us
    ppermute x6, waiting for transfers between devices, swap_x(): return lax.ppermute(value, 'dp', flipped(4, mask))  8.27 us
    ppermute x5, starting transfers between devices, swap_cores(): return lax.ppermute(value, 'col', flipped(16, 1))  7.57 us
    ppermute x6, starting transfers between devices, swap_x(): return lax.ppermute(value, 'dp', flipped(4, mask))  7.39 us
  transfers between devices with their start and end apart: 22, of which 7 were waited for; matrix products, arithmetic and copies ran while one was open for 6% of the time, Pallas kernels for 5%

profile of v9, /device:TPU:1, one launch (start us, length us, event | category | flops | bytes accessed | tf_op | source)
XLA Modules:
  0.0 154.8 jit_solution(15302246741899765111)
XLA Ops:
  0.7 1.4 copy.15
  2.1 2.1 %collective-permute-start = (bf16[32,2048]{1,0:T(8,128)(2,1)S(1)}, bf16[32,2048]{1,0:T(8,128)(2,1)S(1)}, u32[]{:S(2)}, u32[]{:S(2)}) collective-permute-start(bf16[32,2048]{1,0:T(8,128)(2,1)S(1)} %get-tuple-element.76), channel_id=1, source_target_pairs={{0,64},{64,0},{128,192},{192,128},{1,65},{65,1},{129,193},{193,129... | collective-permute-start | bytes 393224 | tf_op jit(solution)/shard_map/ppermute | solution.py:257
  4.2 2.5 %collective-permute-start.1 = (bf16[32,2048]{1,0:T(8,128)(2,1)S(1)}, bf16[32,2048]{1,0:T(8,128)(2,1)S(1)}, u32[]{:S(2)}, u32[]{:S(2)}) collective-permute-start(bf16[32,2048]{1,0:T(8,128)(2,1)S(1)} %get-tuple-element.75), channel_id=1, source_target_pairs={{0,128},{64,192},{128,0},{192,64},{1,129},{65,193},{129,1},{193,65... | collective-permute-start | bytes 393224 | tf_op jit(solution)/shard_map/ppermute | solution.py:257
  7.4 7.1 %collective-permute-start.3 = (bf16[32,2048]{1,0:T(8,128)(2,1)S(1)}, bf16[32,2048]{1,0:T(8,128)(2,1)S(1)}, u32[]{:S(2)}, u32[]{:S(2)}) collective-permute-start(bf16[32,2048]{1,0:T(8,128)(2,1)S(1)} %get-tuple-element.73), channel_id=1, source_target_pairs={{0,2},{1,3},{2,0},{3,1},{4,6},{5,7},{6,4},{7,5},{8,10},{9,11},{10,... | collective-permute-start | bytes 393224 | tf_op jit(solution)/shard_map/ppermute | solution.py:269
  17.8 9.5 %collective-permute-done.4 = bf16[128,512]{1,0:T(8,128)(2,1)S(1)} collective-permute-done((bf16[128,512]{1,0:T(8,128)(2,1)}, bf16[128,512]{1,0:T(8,128)(2,1)S(1)}, u32[]{:S(2)}, u32[]{:S(2)}) %collective-permute-start.4) | collective-permute-done | bytes 131104 | tf_op jit(solution)/shard_map/ppermute | solution.py:265
  29.3 1.4 collective-permute-start.7
  30.7 1.9 %collective-permute-start.5 = (bf16[96,2048]{1,0:T(8,128)(2,1)S(1)}, bf16[96,2048]{1,0:T(8,128)(2,1)S(1)}, u32[]{:S(2)}, u32[]{:S(2)}) collective-permute-start(bf16[96,2048]{1,0:T(8,128)(2,1)S(1)} %pad_maximum_fusion.1), channel_id=1, source_target_pairs={{0,2},{1,3},{2,0},{3,1},{4,6},{5,7},{6,4},{7,5},{8,10},{9,11},{10,... | collective-permute-start | bytes 1179656 | tf_op jit(solution)/shard_map/ppermute | solution.py:269
  33.8 21.2 %collective-permute-done.8 = bf16[256,512]{1,0:T(8,128)(2,1)S(1)} collective-permute-done((bf16[256,512]{1,0:T(8,128)(2,1)S(1)}, bf16[256,512]{1,0:T(8,128)(2,1)S(1)}, u32[]{:S(2)}, u32[]{:S(2)}) %collective-permute-start.8) | collective-permute-done | bytes 262176 | tf_op jit(solution)/shard_map/ppermute | solution.py:265
  55.1 2.6 %collective-permute-start.10 = (bf16[512,512]{1,0:T(8,128)(2,1)S(1)}, bf16[512,512]{1,0:T(8,128)(2,1)}, u32[]{:S(2)}, u32[]{:S(2)}) collective-permute-start(bf16[512,512]{1,0:T(8,128)(2,1)S(1)} %pad_maximum_fusion.refs_0_), channel_id=1, source_target_pairs={{0,192},{64,128},{128,64},{192,0},{1,193},{65,129},{129,65},{193,1... | collective-permute-start | bytes 1572872 | tf_op jit(solution)/shard_map/ppermute | solution.py:257
  59.2 2.7 %collective-permute-start.12 = (bf16[80,2048]{1,0:T(8,128)(2,1)}, bf16[80,2048]{1,0:T(8,128)(2,1)}, u32[]{:S(2)}, u32[]{:S(2)}) collective-permute-start(bf16[80,2048]{1,0:T(8,128)(2,1)} %slice.7), channel_id=1, source_target_pairs={{0,12},{1,13},{2,14},{3,15},{4,0},{5,1},{6,2},{7,3},{8,4},{9,5},{1... | collective-permute-start | bytes 983048 | tf_op jit(solution)/shard_map/ppermute | solution.py:261
  63.9 4.0 %collective-permute-done.11 = bf16[80,2048]{1,0:T(8,128)(2,1)} collective-permute-done((bf16[80,2048]{1,0:T(8,128)(2,1)}, bf16[80,2048]{1,0:T(8,128)(2,1)}, u32[]{:S(2)}, u32[]{:S(2)}) %collective-permute-start.11) | collective-permute-done | bytes 327712 | tf_op jit(solution)/shard_map/ppermute | solution.py:261
  69.9 2.6 %collective-permute-start.15 = (bf16[96,2048]{1,0:T(8,128)(2,1)}, bf16[96,2048]{1,0:T(8,128)(2,1)S(1)}, u32[]{:S(2)}, u32[]{:S(2)}) collective-permute-start(bf16[96,2048]{1,0:T(8,128)(2,1)} %copy-done.4), channel_id=1, source_target_pairs={{0,8},{1,9},{2,10},{3,11},{4,12},{5,13},{6,14},{7,15},{8,0},{9,1},... | collective-permute-start | bytes 1179656 | tf_op jit(solution)/shard_map/ppermute | solution.py:261
  75.9 3.4 %collective-permute-start.21 = (bf16[640,2048]{1,0:T(8,128)(2,1)S(1)}, bf16[640,2048]{1,0:T(8,128)(2,1)}, u32[]{:S(2)}, u32[]{:S(2)}) collective-permute-start(bf16[640,2048]{1,0:T(8,128)(2,1)S(1)} %constant_dynamic-update-slice_fusion.5.own_ref), channel_id=1, source_target_pairs={{0,1},{1,0},{2,3},{3,2},{4,5},{5,4},{6,7},{7,6},{8,9},{9,8},{10,11... | collective-permute-start | bytes 7864328 | tf_op jit(solution)/shard_map/ppermute | solution.py:253
  79.3 6.2 %collective-permute-done.13.refs_2_ = bf16[512,512]{1,0:T(8,128)(2,1)S(1)} collective-permute-done((bf16[512,512]{1,0:T(8,128)(2,1)S(1)}, bf16[512,512]{1,0:T(8,128)(2,1)S(1)}, u32[]{:S(2)}, u32[]{:S(2)}) %collective-permute-start.13) | collective-permute-done | bytes 524320 | tf_op jit(solution)/shard_map/ppermute | solution.py:257
  85.5 1.8 %shard_map.76 = (bf16[512,1280]{1,0:T(8,128)(2,1)S(1)}, bf16[512,768]{1,0:T(8,128)(2,1)S(1)}) custom-call(s32[8]{0:T(128)S(1)} %stack.35.at_ref, bf16[512,512]{1,0:T(8,128)(2,1)S(1)} %pad_maximum_fusion.refs_0_, bf16[512,512]{1,0:T(8,128)(2,1)} %collective-permute-done.9.refs_1_, bf16[512,512]{1,0:T(8,128)(2,1)S(1)} %collective-permute-done.13.refs_2_, ...), custom_call_target="tpu_custom_call" | custom-call | bytes 4194304 | tf_op jit(solution)/shard_map/pallas_call | solution.py:43
  91.2 3.7 %collective-permute-start.17 = (bf16[96,2048]{1,0:T(8,128)(2,1)}, bf16[96,2048]{1,0:T(8,128)(2,1)S(1)}, u32[]{:S(2)}, u32[]{:S(2)}) collective-permute-start(bf16[96,2048]{1,0:T(8,128)(2,1)} %copy-done.4), channel_id=1, source_target_pairs={{0,1},{1,0},{2,3},{3,2},{4,5},{5,4},{6,7},{7,6},{8,9},{9,8},{10,11... | collective-permute-start | bytes 1179656 | tf_op jit(solution)/shard_map/ppermute | solution.py:253
  95.5 1.3 copy-done.1
  96.8 5.6 %shard_map.78.refs_8_ = f32[512,2048]{1,0:T(8,128)S(1)} custom-call(bf16[512,1280]{1,0:T(8,128)(2,1)S(1)} %copy-done.1, bf16[640,2048]{1,0:T(8,128)(2,1)S(1)} %constant_dynamic-update-slice_fusion.5.own_ref, bf16[640,2048]{1,0:T(8,128)(2,1)} %collective-permute-done.21.other_ref, f32[8,128]{1,0:T(8,128)S(1)} %shard_map.75.first_ref, ...), custom_call_target="tpu_custom_call" | custom-call | flops 2147483648 | bytes 9437184 | tf_op jit(solution)/shard_map/pallas_call | solution.py:116
  102.5 4.1 %shard_map.79 = (f32[512,2048]{1,0:T(8,128)S(1)}, f32[1,2048]{1,0:T(1,128)S(1)}, f32[1,512]{1,0:T(1,128)S(1)}) custom-call(bf16[512,768]{1,0:T(8,128)(2,1)S(1)} %copy-done.3, bf16[96,2048]{1,0:T(8,128)(2,1)S(1)} %copy-done.5, bf16[96,2048]{1,0:T(8,128)(2,1)S(1)} %copy-done.7, bf16[96,2048]{1,0:T(8,128)(2,1)S(1)} %copy-done.9, ...), custom_call_target="tpu_custom_call" | custom-call | flops 2147483648 | bytes 9437184 | tf_op jit(solution)/shard_map/pallas_call | solution.py:128
  106.7 15.2 %all_to_all.15 = f32[16,1,2048]{2,1,0:T(1,128)S(1)} all-to-all(f32[16,1,2048]{2,1,0:T(1,128)S(1)} %broadcast_in_dim.17), channel_id=1, replica_groups=mesh['dp'=4,'row'=4,'col'=16] {'col'}, dimensions={0} | all-to-all | bytes 262144 | tf_op jit(solution)/shard_map/all_to_all | solution.py:274
  122.0 2.3 %shard_map.80 = (f32[1,2048]{1,0:T(1,128)}, f32[1,2048]{1,0:T(1,128)S(1)}, f32[1,1024]{1,0:T(1,128)S(1)}) custom-call(f32[512,2048]{1,0:T(8,128)S(1)} %get-tuple-element.61.g_ref, f32[1,2048]{1,0:T(1,128)S(1)} %bitcast.38, f32[16,2048]{1,0:T(8,128)S(1)} %bitcast.35, f32[1,512]{1,0:T(1,128)S(1)} %get-tuple-element.63.row_ref), custom_call_target="tpu_custom_call" | custom-call | flops 4194304 | bytes 4194304 | tf_op jit(solution)/shard_map/pallas_call | solution.py:162
  124.3 12.9 %all_to_all.16 = f32[16,1,1024]{2,1,0:T(1,128)S(1)} all-to-all(f32[16,1,1024]{2,1,0:T(1,128)S(1)} %broadcast_in_dim.18), channel_id=1, replica_groups=mesh['dp'=4,'row'=4,'col'=16] {'dp','row'}, dimensions={0} | all-to-all | bytes 131072 | tf_op jit(solution)/shard_map/all_to_all | solution.py:274
  137.8 13.8 %all_to_all.17 = f32[16,1,128]{2,1,0:T(1,128)S(1)} all-to-all(f32[16,1,128]{2,1,0:T(1,128)S(1)} %broadcast_in_dim.19), channel_id=1, replica_groups=mesh['dp'=4,'row'=4,'col'=16] {'col'}, dimensions={0} | all-to-all | bytes 16384 | tf_op jit(solution)/shard_map/all_to_all | solution.py:274
  151.6 3.2 %shard_map.82 = (f32[512,2048]{1,0:T(8,128)}, f32[1,1]{1,0:T(1,128)}) custom-call(f32[512,2048]{1,0:T(8,128)S(1)} %get-tuple-element.61.g_ref, f32[1,512]{1,0:T(1,128)S(1)} %get-tuple-element.65.row_ref, f32[1,2048]{1,0:T(1,128)S(1)} %get-tuple-element.66.col_ref, f32[16,128]{1,0:T(8,128)S(1)} %bitcast.37), custom_call_target="tpu_custom_call" | custom-call | flops 2097152 | bytes 8388608 | tf_op jit(solution)/shard_map/pallas_call | solution.py:226
  (90 shorter events, 21.3 us)
Async XLA Ops:
  0.6 26.7 %copy-start.17 = (bf16[128,512]{1,0:T(8,128)(2,1)S(1)}, bf16[128,512]{1,0:T(8,128)(2,1)}, u32[]{:S(2)}) copy-start(bf16[128,512]{1,0:T(8,128)(2,1)} %param.4) | copy-start | bytes 393220
  2.1 13.6 %collective-permute-start = (bf16[32,2048]{1,0:T(8,128)(2,1)S(1)}, bf16[32,2048]{1,0:T(8,128)(2,1)S(1)}, u32[]{:S(2)}, u32[]{:S(2)}) collective-permute-start(bf16[32,2048]{1,0:T(8,128)(2,1)S(1)} %get-tuple-element.76), channel_id=1, source_target_pairs={{0,64},{64,0},{128,192},{192,128},{1,65},{65,1},{129,193},{193,129... | collective-permute-start | bytes 393224 | tf_op jit(solution)/shard_map/ppermute | solution.py:257
  4.2 12.2 %collective-permute-start.1 = (bf16[32,2048]{1,0:T(8,128)(2,1)S(1)}, bf16[32,2048]{1,0:T(8,128)(2,1)S(1)}, u32[]{:S(2)}, u32[]{:S(2)}) collective-permute-start(bf16[32,2048]{1,0:T(8,128)(2,1)S(1)} %get-tuple-element.75), channel_id=1, source_target_pairs={{0,128},{64,192},{128,0},{192,64},{1,129},{65,193},{129,1},{193,65... | collective-permute-start | bytes 393224 | tf_op jit(solution)/shard_map/ppermute | solution.py:257
  6.7 10.4 %collective-permute-start.2 = (bf16[32,2048]{1,0:T(8,128)(2,1)S(1)}, bf16[32,2048]{1,0:T(8,128)(2,1)S(1)}, u32[]{:S(2)}, u32[]{:S(2)}) collective-permute-start(bf16[32,2048]{1,0:T(8,128)(2,1)S(1)} %get-tuple-element.74), channel_id=1, source_target_pairs={{0,192},{64,128},{128,64},{192,0},{1,193},{65,129},{129,65},{193,1... | collective-permute-start | bytes 393224 | tf_op jit(solution)/shard_map/ppermute | solution.py:257
  7.4 19.9 %collective-permute-start.3 = (bf16[32,2048]{1,0:T(8,128)(2,1)S(1)}, bf16[32,2048]{1,0:T(8,128)(2,1)S(1)}, u32[]{:S(2)}, u32[]{:S(2)}) collective-permute-start(bf16[32,2048]{1,0:T(8,128)(2,1)S(1)} %get-tuple-element.73), channel_id=1, source_target_pairs={{0,2},{1,3},{2,0},{3,1},{4,6},{5,7},{6,4},{7,5},{8,10},{9,11},{10,... | collective-permute-start | bytes 393224 | tf_op jit(solution)/shard_map/ppermute | solution.py:269
  14.4 12.8 %collective-permute-start.4 = (bf16[128,512]{1,0:T(8,128)(2,1)}, bf16[128,512]{1,0:T(8,128)(2,1)S(1)}, u32[]{:S(2)}, u32[]{:S(2)}) collective-permute-start(bf16[128,512]{1,0:T(8,128)(2,1)} %param.4), channel_id=1, source_target_pairs={{0,32},{16,48},{32,0},{48,16},{1,33},{17,49},{33,1},{49,17},{2,34}... | collective-permute-start | bytes 393224 | tf_op jit(solution)/shard_map/ppermute | solution.py:265
  28.0 27.1 %collective-permute-start.6 = (bf16[160,2048]{1,0:T(8,128)(2,1)}, bf16[160,2048]{1,0:T(8,128)(2,1)S(1)}, u32[]{:S(2)}, u32[]{:S(2)}) collective-permute-start(bf16[160,2048]{1,0:T(8,128)(2,1)} %constant_dynamic-update-slice_fusion), channel_id=1, source_target_pairs={{0,4},{1,5},{2,6},{3,7},{4,8},{5,9},{6,10},{7,11},{8,12},{9,13},{1... | collective-permute-start | bytes 1966088 | tf_op jit(solution)/shard_map/ppermute | solution.py:261
  29.3 25.8 %collective-permute-start.7 = (bf16[160,2048]{1,0:T(8,128)(2,1)}, bf16[160,2048]{1,0:T(8,128)(2,1)S(1)}, u32[]{:S(2)}, u32[]{:S(2)}) collective-permute-start(bf16[160,2048]{1,0:T(8,128)(2,1)} %constant_dynamic-update-slice_fusion), channel_id=1, source_target_pairs={{0,12},{1,13},{2,14},{3,15},{4,0},{5,1},{6,2},{7,3},{8,4},{9,5},{1... | collective-permute-start | bytes 1966088 | tf_op jit(solution)/shard_map/ppermute | solution.py:261
  30.7 31.2 %collective-permute-start.5 = (bf16[96,2048]{1,0:T(8,128)(2,1)S(1)}, bf16[96,2048]{1,0:T(8,128)(2,1)S(1)}, u32[]{:S(2)}, u32[]{:S(2)}) collective-permute-start(bf16[96,2048]{1,0:T(8,128)(2,1)S(1)} %pad_maximum_fusion.1), channel_id=1, source_target_pairs={{0,2},{1,3},{2,0},{3,1},{4,6},{5,7},{6,4},{7,5},{8,10},{9,11},{10,... | collective-permute-start | bytes 1179656 | tf_op jit(solution)/shard_map/ppermute | solution.py:269
  32.7 22.4 %collective-permute-start.8 = (bf16[256,512]{1,0:T(8,128)(2,1)S(1)}, bf16[256,512]{1,0:T(8,128)(2,1)S(1)}, u32[]{:S(2)}, u32[]{:S(2)}) collective-permute-start(bf16[256,512]{1,0:T(8,128)(2,1)S(1)} %pad_maximum_fusion.2), channel_id=1, source_target_pairs={{0,16},{16,0},{32,48},{48,32},{1,17},{17,1},{33,49},{49,33},{2,18}... | collective-permute-start | bytes 786440 | tf_op jit(solution)/shard_map/ppermute | solution.py:265
  55.1 13.8 %collective-permute-start.10 = (bf16[512,512]{1,0:T(8,128)(2,1)S(1)}, bf16[512,512]{1,0:T(8,128)(2,1)}, u32[]{:S(2)}, u32[]{:S(2)}) collective-permute-start(bf16[512,512]{1,0:T(8,128)(2,1)S(1)} %pad_maximum_fusion.refs_0_), channel_id=1, source_target_pairs={{0,192},{64,128},{128,64},{192,0},{1,193},{65,129},{129,65},{193,1... | collective-permute-start | bytes 1572872 | tf_op jit(solution)/shard_map/ppermute | solution.py:257
  57.7 12.2 %collective-permute-start.9 = (bf16[512,512]{1,0:T(8,128)(2,1)S(1)}, bf16[512,512]{1,0:T(8,128)(2,1)}, u32[]{:S(2)}, u32[]{:S(2)}) collective-permute-start(bf16[512,512]{1,0:T(8,128)(2,1)S(1)} %pad_maximum_fusion.refs_0_), channel_id=1, source_target_pairs={{0,64},{64,0},{128,192},{192,128},{1,65},{65,1},{129,193},{193,129... | collective-permute-start | bytes 1572872 | tf_op jit(solution)/shard_map/ppermute | solution.py:257
  58.4 9.4 %collective-permute-start.11 = (bf16[80,2048]{1,0:T(8,128)(2,1)}, bf16[80,2048]{1,0:T(8,128)(2,1)}, u32[]{:S(2)}, u32[]{:S(2)}) collective-permute-start(bf16[80,2048]{1,0:T(8,128)(2,1)} %slice.6), channel_id=1, source_target_pairs={{0,4},{1,5},{2,6},{3,7},{4,8},{5,9},{6,10},{7,11},{8,12},{9,13},{1... | collective-permute-start | bytes 983048 | tf_op jit(solution)/shard_map/ppermute | solution.py:261
  59.2 8.7 %collective-permute-start.12 = (bf16[80,2048]{1,0:T(8,128)(2,1)}, bf16[80,2048]{1,0:T(8,128)(2,1)}, u32[]{:S(2)}, u32[]{:S(2)}) collective-permute-start(bf16[80,2048]{1,0:T(8,128)(2,1)} %slice.7), channel_id=1, source_target_pairs={{0,12},{1,13},{2,14},{3,15},{4,0},{5,1},{6,2},{7,3},{8,4},{9,5},{1... | collective-permute-start | bytes 983048 | tf_op jit(solution)/shard_map/ppermute | solution.py:261
  69.9 19.4 %collective-permute-start.14 = (bf16[96,2048]{1,0:T(8,128)(2,1)}, bf16[96,2048]{1,0:T(8,128)(2,1)S(1)}, u32[]{:S(2)}, u32[]{:S(2)}) collective-permute-start(bf16[96,2048]{1,0:T(8,128)(2,1)} %copy-done.4), channel_id=1, source_target_pairs={{0,4},{1,5},{2,6},{3,7},{4,8},{5,9},{6,10},{7,11},{8,12},{9,13},{1... | collective-permute-start | bytes 1179656 | tf_op jit(solution)/shard_map/ppermute | solution.py:261
  69.9 19.3 %collective-permute-start.15 = (bf16[96,2048]{1,0:T(8,128)(2,1)}, bf16[96,2048]{1,0:T(8,128)(2,1)S(1)}, u32[]{:S(2)}, u32[]{:S(2)}) collective-permute-start(bf16[96,2048]{1,0:T(8,128)(2,1)} %copy-done.4), channel_id=1, source_target_pairs={{0,8},{1,9},{2,10},{3,11},{4,12},{5,13},{6,14},{7,15},{8,0},{9,1},... | collective-permute-start | bytes 1179656 | tf_op jit(solution)/shard_map/ppermute | solution.py:261
  72.6 17.9 %collective-permute-start.16 = (bf16[96,2048]{1,0:T(8,128)(2,1)}, bf16[96,2048]{1,0:T(8,128)(2,1)S(1)}, u32[]{:S(2)}, u32[]{:S(2)}) collective-permute-start(bf16[96,2048]{1,0:T(8,128)(2,1)} %copy-done.4), channel_id=1, source_target_pairs={{0,12},{1,13},{2,14},{3,15},{4,0},{5,1},{6,2},{7,3},{8,4},{9,5},{1... | collective-permute-start | bytes 1179656 | tf_op jit(solution)/shard_map/ppermute | solution.py:261
  73.6 11.9 %collective-permute-start.13 = (bf16[512,512]{1,0:T(8,128)(2,1)S(1)}, bf16[512,512]{1,0:T(8,128)(2,1)S(1)}, u32[]{:S(2)}, u32[]{:S(2)}) collective-permute-start(bf16[512,512]{1,0:T(8,128)(2,1)S(1)} %pad_maximum_fusion.refs_0_), channel_id=1, source_target_pairs={{0,128},{64,192},{128,0},{192,64},{1,129},{65,193},{129,1},{193,65... | collective-permute-start | bytes 1572872 | tf_op jit(solution)/shard_map/ppermute | solution.py:257
  75.9 19.6 %collective-permute-start.21 = (bf16[640,2048]{1,0:T(8,128)(2,1)S(1)}, bf16[640,2048]{1,0:T(8,128)(2,1)}, u32[]{:S(2)}, u32[]{:S(2)}) collective-permute-start(bf16[640,2048]{1,0:T(8,128)(2,1)S(1)} %constant_dynamic-update-slice_fusion.5.own_ref), channel_id=1, source_target_pairs={{0,1},{1,0},{2,3},{3,2},{4,5},{5,4},{6,7},{7,6},{8,9},{9,8},{10,11... | collective-permute-start | bytes 7864328 | tf_op jit(solution)/shard_map/ppermute | solution.py:253
  91.2 11.1 %collective-permute-start.17 = (bf16[96,2048]{1,0:T(8,128)(2,1)}, bf16[96,2048]{1,0:T(8,128)(2,1)S(1)}, u32[]{:S(2)}, u32[]{:S(2)}) collective-permute-start(bf16[96,2048]{1,0:T(8,128)(2,1)} %copy-done.4), channel_id=1, source_target_pairs={{0,1},{1,0},{2,3},{3,2},{4,5},{5,4},{6,7},{7,6},{8,9},{9,8},{10,11... | collective-permute-start | bytes 1179656 | tf_op jit(solution)/shard_map/ppermute | solution.py:253
  94.9 7.4 %collective-permute-start.18 = (bf16[96,2048]{1,0:T(8,128)(2,1)}, bf16[96,2048]{1,0:T(8,128)(2,1)S(1)}, u32[]{:S(2)}, u32[]{:S(2)}) collective-permute-start(bf16[96,2048]{1,0:T(8,128)(2,1)} %copy-done.6), channel_id=1, source_target_pairs={{0,1},{1,0},{2,3},{3,2},{4,5},{5,4},{6,7},{7,6},{8,9},{9,8},{10,11... | collective-permute-start | bytes 1179656 | tf_op jit(solution)/shard_map/ppermute | solution.py:253
  94.9 7.5 %collective-permute-start.19 = (bf16[96,2048]{1,0:T(8,128)(2,1)}, bf16[96,2048]{1,0:T(8,128)(2,1)S(1)}, u32[]{:S(2)}, u32[]{:S(2)}) collective-permute-start(bf16[96,2048]{1,0:T(8,128)(2,1)} %copy-done.8), channel_id=1, source_target_pairs={{0,1},{1,0},{2,3},{3,2},{4,5},{5,4},{6,7},{7,6},{8,9},{9,8},{10,11... | collective-permute-start | bytes 1179656 | tf_op jit(solution)/shard_map/ppermute | solution.py:253
  95.4 7.0 %collective-permute-start.20 = (bf16[96,2048]{1,0:T(8,128)(2,1)}, bf16[96,2048]{1,0:T(8,128)(2,1)S(1)}, u32[]{:S(2)}, u32[]{:S(2)}) collective-permute-start(bf16[96,2048]{1,0:T(8,128)(2,1)} %copy-done.10), channel_id=1, source_target_pairs={{0,1},{1,0},{2,3},{3,2},{4,5},{5,4},{6,7},{7,6},{8,9},{9,8},{10,11... | collective-permute-start | bytes 1179656 | tf_op jit(solution)/shard_map/ppermute | solution.py:253
  106.7 30.5 %copy-start.13 = (f32[512]{0:T(512)S(1)}, f32[512]{0:T(512)}, u32[]{:S(2)}) copy-start(f32[512]{0:T(512)} %param.6) | copy-start | bytes 6148
  (16 other events, 87.4 us)

commit v10 on v8

--- a/solution.py
+++ b/solution.py
@@ -13,12 +13,12 @@
     refs[-1][...] = jnp.zeros_like(refs[-1])
 
 
-def after(*blocks):
+def after(*blocks, scale=34):
     return pl.pallas_call(
         after_kernel,
         in_specs=[pl.BlockSpec(memory_space=pl.ANY)] * len(blocks),
         out_shape=pltpu.VMEM((8, 128), jnp.float32),
-        cost_estimate=pl.CostEstimate(flops=1 << 34, bytes_accessed=0, transcendentals=0),
+        cost_estimate=pl.CostEstimate(flops=1 << scale, bytes_accessed=0, transcendentals=0),
     )(*blocks)
 
 
@@ -39,7 +39,7 @@
         arrange_kernel,
         in_specs=[pl.BlockSpec(memory_space=pltpu.SMEM)] + [whole] * 4,
         out_specs=[whole] * 2,
-        out_shape=[jax.ShapeDtypeStruct((512, 1024), jnp.bfloat16)] * 2,
+        out_shape=[pltpu.VMEM((512, 1024), jnp.bfloat16)] * 2,
         compiler_params=PARAMS,
         cost_estimate=pl.CostEstimate(flops=0, bytes_accessed=4 << 20, transcendentals=0),
     )(at, *pieces)
@@ -114,7 +114,7 @@
         out_shape=jax.ShapeDtypeStruct((512, 2048), jnp.float32),
         compiler_params=PARAMS,
         cost_estimate=COST,
-    )(x, own, other, *tokens)
+    )(in_vmem(x), own, other, *tokens)
 
 
 def far_product(x, blocks, near):
@@ -131,7 +131,7 @@
         scratch_shapes=[pltpu.VMEM((512, 128), jnp.float32)],
         compiler_params=PARAMS,
         cost_estimate=COST,
-    )(x, *blocks, near)
+    )(in_vmem(x), *blocks, near)
 
 
 def weigh_kernel(
@@ -289,16 +289,17 @@
 
     far = swap_z(near)
     nears = [move_y(near, t) for t in (1, 2, 3)]
+    x0, x1 = stage((x0, swap_x(x0, 1)))
     x2 = swap_x(x0, 2)
-    early = after(far)
+    early = after(far, scale=35)
     far, early, x0, x2, *nears = stage((far, early, x0, x2, *nears))
 
     own = jnp.concatenate([near, *nears])
     other = swap_cores(own)
-    x1, x3 = swap_x(x0, 1), swap_x(x0, 3)
+    x3 = swap_x(x0, 3)
     fars = [move_y(far, t) for t in (1, 2, 3)]
     x_near, x_far = arrange(at, (x0, x1, x2, x3))
-    late = after(*fars)
+    late = after(x_far, *fars, scale=35)
     late, x_near, x_far, far, *fars = stage((late, x_near, x_far, far, *fars))
 
     fars = [far, *fars]

time: 140 us -> 139 us (level)
  waiting for transfers between devices: 34.5 us -> 30.2 us
  blocking collectives: 39.4 us -> 43.1 us
  local copies, waits for them, and re-layouts: 8.73 us -> 10.4 us
    all_to_all x3, blocking collectives: 39.4 us -> 43.1 us  [copies(): return lax.all_to_all(rows, axis, 0, 0).reshape(16, value.shape[1])]
    ppermute x6, waiting for transfers between devices: 8.59 us -> 6.15 us  [swap_x(): return lax.ppermute(value, 'dp', flipped(4, mask))]
    ppermute x6, waiting for transfers between devices: 21.2 us -> 19.5 us  [move_y(): return lax.ppermute(value, 'col', cyclic(4, 4, shift % 4))]
    unnamed x24 -> x40, local copies, waits for them, and re-layouts: 7.41 us -> 9.08 us
    ppermute x6, starting transfers between devices: 9.58 us -> 8.04 us  [move_y(): return lax.ppermute(value, 'col', cyclic(4, 4, shift % 4))]
    ppermute x5, starting transfers between devices: 5.79 us -> 7.23 us  [swap_cores(): return lax.ppermute(value, 'col', flipped(16, 1))]
where the time goes in v10:
time: 139 us
  blocking collectives  43.1 us (31%)
  starting transfers between devices  36.8 us (26%)
  waiting for transfers between devices  30.2 us (22%)
  Pallas kernels  16.6 us (12%)
  local copies, waits for them, and re-layouts  10.4 us (7%)
    all_to_all x3, blocking collectives, copies(): return lax.all_to_all(rows, axis, 0, 0).reshape(16, value.shape[1])  43.1 us
    ppermute x6, waiting for transfers between devices, move_y(): return lax.ppermute(value, 'col', cyclic(4, 4, shift % 4))  19.5 us
    unnamed x40, local copies, waits for them, and re-layouts  9.08 us
    ppermute x6, starting transfers between devices, swap_x(): return lax.ppermute(value, 'dp', flipped(4, mask))  8.52 us
    ppermute x6, starting transfers between devices, move_y(): return lax.ppermute(value, 'col', cyclic(4, 4, shift % 4))  8.04 us
    ppermute x5, starting transfers between devices, swap_cores(): return lax.ppermute(value, 'col', flipped(16, 1))  7.23 us
    ppermute x1, starting transfers between devices, swap_z(): return lax.ppermute(value, 'col', flipped(16, 2))  6.82 us
    ppermute x2, starting transfers between devices, swap_row(): return lax.ppermute(value, 'row', flipped(4, mask))  6.16 us
  transfers between devices with their start and end apart: 20, of which 8 were waited for; matrix products, arithmetic and copies ran while one was open for 5% of the time, Pallas kernels for 5%

profile of v10, /device:TPU:1, one launch (start us, length us, event | category | flops | bytes accessed | tf_op | source)
XLA Modules:
  0.0 138.9 jit_solution(15041839626686601086)
XLA Ops:
  0.6 3.9 %collective-permute-start.3 = (bf16[128,512]{1,0:T(8,128)(2,1)}, bf16[128,512]{1,0:T(8,128)(2,1)S(1)}, u32[]{:S(2)}, u32[]{:S(2)}) collective-permute-start(bf16[128,512]{1,0:T(8,128)(2,1)} %param.4), channel_id=1, source_target_pairs={{0,32},{16,48},{32,0},{48,16},{1,33},{17,49},{33,1},{49,17},{2,34}... | collective-permute-start | bytes 393224 | tf_op jit(solution)/shard_map/ppermute | solution.py:258
  7.3 2.5 %collective-permute-start.1 = (bf16[32,2048]{1,0:T(8,128)(2,1)S(1)}, bf16[32,2048]{1,0:T(8,128)(2,1)S(1)}, u32[]{:S(2)}, u32[]{:S(2)}) collective-permute-start(bf16[32,2048]{1,0:T(8,128)(2,1)S(1)} %get-tuple-element.70), channel_id=1, source_target_pairs={{0,128},{64,192},{128,0},{192,64},{1,129},{65,193},{129,1},{193,65... | collective-permute-start | bytes 393224 | tf_op jit(solution)/shard_map/ppermute | solution.py:250
  9.9 2.2 %collective-permute-start.4 = (bf16[256,512]{1,0:T(8,128)(2,1)S(1)}, bf16[256,512]{1,0:T(8,128)(2,1)S(1)}, u32[]{:S(2)}, u32[]{:S(2)}) collective-permute-start(bf16[256,512]{1,0:T(8,128)(2,1)S(1)} %pad_maximum_fusion.2), channel_id=1, source_target_pairs={{0,16},{16,0},{32,48},{48,32},{1,17},{17,1},{33,49},{49,33},{2,18}... | collective-permute-start | bytes 786440 | tf_op jit(solution)/shard_map/ppermute | solution.py:258
  12.3 2.5 %collective-permute-done.1 = bf16[32,2048]{1,0:T(8,128)(2,1)S(1)} collective-permute-done((bf16[32,2048]{1,0:T(8,128)(2,1)S(1)}, bf16[32,2048]{1,0:T(8,128)(2,1)S(1)}, u32[]{:S(2)}, u32[]{:S(2)}) %collective-permute-start.1) | collective-permute-done | bytes 131104 | tf_op jit(solution)/shard_map/ppermute | solution.py:250
  14.8 2.8 %collective-permute-done.2 = bf16[32,2048]{1,0:T(8,128)(2,1)S(1)} collective-permute-done((bf16[32,2048]{1,0:T(8,128)(2,1)S(1)}, bf16[32,2048]{1,0:T(8,128)(2,1)S(1)}, u32[]{:S(2)}, u32[]{:S(2)}) %collective-permute-start.2) | collective-permute-done | bytes 131104 | tf_op jit(solution)/shard_map/ppermute | solution.py:250
  18.8 6.8 %collective-permute-start.5 = (bf16[128,2048]{1,0:T(8,128)(2,1)}, bf16[128,2048]{1,0:T(8,128)(2,1)S(1)}, u32[]{:S(2)}, u32[]{:S(2)}) collective-permute-start(bf16[128,2048]{1,0:T(8,128)(2,1)} %pad_maximum_fusion), channel_id=1, source_target_pairs={{0,2},{1,3},{2,0},{3,1},{4,6},{5,7},{6,4},{7,5},{8,10},{9,11},{10,... | collective-permute-start | bytes 1572872 | tf_op jit(solution)/shard_map/ppermute | solution.py:262
  25.6 2.7 %collective-permute-start.10 = (bf16[128,2048]{1,0:T(8,128)(2,1)}, bf16[128,2048]{1,0:T(8,128)(2,1)}, u32[]{:S(2)}, u32[]{:S(2)}) collective-permute-start(bf16[128,2048]{1,0:T(8,128)(2,1)} %pad_maximum_fusion), channel_id=1, source_target_pairs={{0,12},{1,13},{2,14},{3,15},{4,0},{5,1},{6,2},{7,3},{8,4},{9,5},{1... | collective-permute-start | bytes 1572872 | tf_op jit(solution)/shard_map/ppermute | solution.py:254
  31.9 2.5 %collective-permute-start.7 = (bf16[512,512]{1,0:T(8,128)(2,1)S(1)}, bf16[512,512]{1,0:T(8,128)(2,1)}, u32[]{:S(2)}, u32[]{:S(2)}) collective-permute-start(bf16[512,512]{1,0:T(8,128)(2,1)S(1)} %pad_maximum_fusion.1.refs_0_), channel_id=1, source_target_pairs={{0,128},{64,192},{128,0},{192,64},{1,129},{65,193},{129,1},{193,65... | collective-permute-start | bytes 1572872 | tf_op jit(solution)/shard_map/ppermute | solution.py:250
  34.4 4.5 %collective-permute-done.5.refs_0_ = bf16[128,2048]{1,0:T(8,128)(2,1)S(1)} collective-permute-done((bf16[128,2048]{1,0:T(8,128)(2,1)}, bf16[128,2048]{1,0:T(8,128)(2,1)S(1)}, u32[]{:S(2)}, u32[]{:S(2)}) %collective-permute-start.5) | collective-permute-done | bytes 524320 | tf_op jit(solution)/shard_map/ppermute | solution.py:262
  39.6 2.0 %collective-permute-done.8 = bf16[128,2048]{1,0:T(8,128)(2,1)} collective-permute-done((bf16[128,2048]{1,0:T(8,128)(2,1)}, bf16[128,2048]{1,0:T(8,128)(2,1)}, u32[]{:S(2)}, u32[]{:S(2)}) %collective-permute-start.8) | collective-permute-done | bytes 524320 | tf_op jit(solution)/shard_map/ppermute | solution.py:254
  41.6 9.2 %collective-permute-done.9 = bf16[128,2048]{1,0:T(8,128)(2,1)} collective-permute-done((bf16[128,2048]{1,0:T(8,128)(2,1)}, bf16[128,2048]{1,0:T(8,128)(2,1)}, u32[]{:S(2)}, u32[]{:S(2)}) %collective-permute-start.9) | collective-permute-done | bytes 524320 | tf_op jit(solution)/shard_map/ppermute | solution.py:254
  52.4 2.1 %collective-permute-start.14 = (bf16[128,2048]{1,0:T(8,128)(2,1)}, bf16[128,2048]{1,0:T(8,128)(2,1)S(1)}, u32[]{:S(2)}, u32[]{:S(2)}) collective-permute-start(bf16[128,2048]{1,0:T(8,128)(2,1)} %copy-done.4), channel_id=1, source_target_pairs={{0,12},{1,13},{2,14},{3,15},{4,0},{5,1},{6,2},{7,3},{8,4},{9,5},{1... | collective-permute-start | bytes 1572872 | tf_op jit(solution)/shard_map/ppermute | solution.py:254
  54.5 1.8 %collective-permute-start.11 = (bf16[512,512]{1,0:T(8,128)(2,1)S(1)}, bf16[512,512]{1,0:T(8,128)(2,1)S(1)}, u32[]{:S(2)}, u32[]{:S(2)}) collective-permute-start(bf16[512,512]{1,0:T(8,128)(2,1)S(1)} %pad_maximum_fusion.1.refs_0_), channel_id=1, source_target_pairs={{0,192},{64,128},{128,64},{192,0},{1,193},{65,129},{129,65},{193,1... | collective-permute-start | bytes 1572872 | tf_op jit(solution)/shard_map/ppermute | solution.py:250
  59.6 4.6 %collective-permute-start.19 = (bf16[512,2048]{1,0:T(8,128)(2,1)S(1)}, bf16[512,2048]{1,0:T(8,128)(2,1)}, u32[]{:S(2)}, u32[]{:S(2)}) collective-permute-start(bf16[512,2048]{1,0:T(8,128)(2,1)S(1)} %constant_dynamic-update-slice_fusion.own_ref), channel_id=1, source_target_pairs={{0,1},{1,0},{2,3},{3,2},{4,5},{5,4},{6,7},{7,6},{8,9},{9,8},{10,11... | collective-permute-start | bytes 6291464 | tf_op jit(solution)/shard_map/ppermute | solution.py:246
  68.7 3.1 %collective-permute-done.13.refs_2_ = bf16[128,2048]{1,0:T(8,128)(2,1)S(1)} collective-permute-done((bf16[128,2048]{1,0:T(8,128)(2,1)}, bf16[128,2048]{1,0:T(8,128)(2,1)S(1)}, u32[]{:S(2)}, u32[]{:S(2)}) %collective-permute-start.13) | collective-permute-done | bytes 524320 | tf_op jit(solution)/shard_map/ppermute | solution.py:254
  71.8 5.3 %collective-permute-done.14.refs_3_ = bf16[128,2048]{1,0:T(8,128)(2,1)S(1)} collective-permute-done((bf16[128,2048]{1,0:T(8,128)(2,1)}, bf16[128,2048]{1,0:T(8,128)(2,1)S(1)}, u32[]{:S(2)}, u32[]{:S(2)}) %collective-permute-start.14) | collective-permute-done | bytes 524320 | tf_op jit(solution)/shard_map/ppermute | solution.py:254
  77.9 1.9 %collective-permute-start.15 = (bf16[128,2048]{1,0:T(8,128)(2,1)}, bf16[128,2048]{1,0:T(8,128)(2,1)S(1)}, u32[]{:S(2)}, u32[]{:S(2)}) collective-permute-start(bf16[128,2048]{1,0:T(8,128)(2,1)} %copy-done.4), channel_id=1, source_target_pairs={{0,1},{1,0},{2,3},{3,2},{4,5},{5,4},{6,7},{7,6},{8,9},{9,8},{10,11... | collective-permute-start | bytes 1572872 | tf_op jit(solution)/shard_map/ppermute | solution.py:246
  80.6 4.6 %shard_map.78.refs_8_ = f32[512,2048]{1,0:T(8,128)S(1)} custom-call(bf16[512,1024]{1,0:T(8,128)(2,1)S(1)} %copy-done.3, bf16[512,2048]{1,0:T(8,128)(2,1)S(1)} %constant_dynamic-update-slice_fusion.own_ref, bf16[512,2048]{1,0:T(8,128)(2,1)} %collective-permute-done.19.other_ref, f32[8,128]{1,0:T(8,128)S(1)} %shard_map.75.first_ref, ...), custom_call_target="tpu_custom_call" | custom-call | flops 2147483648 | bytes 9437184 | tf_op jit(solution)/shard_map/pallas_call | solution.py:109
  85.2 4.2 %shard_map.79 = (f32[512,2048]{1,0:T(8,128)S(1)}, f32[1,2048]{1,0:T(1,128)S(1)}, f32[1,512]{1,0:T(1,128)S(1)}) custom-call(bf16[512,1024]{1,0:T(8,128)(2,1)S(1)} %copy-done.1, bf16[128,2048]{1,0:T(8,128)(2,1)S(1)} %copy-done.5, bf16[128,2048]{1,0:T(8,128)(2,1)S(1)} %copy-done.7, bf16[128,2048]{1,0:T(8,128)(2,1)S(1)} %copy-done.9, ...), custom_call_target="tpu_custom_call" | custom-call | flops 2147483648 | bytes 9437184 | tf_op jit(solution)/shard_map/pallas_call | solution.py:121
  89.6 13.7 %all_to_all.15 = f32[16,1,2048]{2,1,0:T(1,128)S(1)} all-to-all(f32[16,1,2048]{2,1,0:T(1,128)S(1)} %broadcast_in_dim.17), channel_id=1, replica_groups=mesh['dp'=4,'row'=4,'col'=16] {'col'}, dimensions={0} | all-to-all | bytes 262144 | tf_op jit(solution)/shard_map/all_to_all | solution.py:267
  103.3 2.3 %shard_map.80 = (f32[1,2048]{1,0:T(1,128)}, f32[1,2048]{1,0:T(1,128)S(1)}, f32[1,1024]{1,0:T(1,128)S(1)}) custom-call(f32[512,2048]{1,0:T(8,128)S(1)} %get-tuple-element.57.g_ref, f32[1,2048]{1,0:T(1,128)S(1)} %bitcast.37, f32[16,2048]{1,0:T(8,128)S(1)} %bitcast.34, f32[1,512]{1,0:T(1,128)S(1)} %get-tuple-element.59.row_ref), custom_call_target="tpu_custom_call" | custom-call | flops 4194304 | bytes 4194304 | tf_op jit(solution)/shard_map/pallas_call | solution.py:155
  105.6 14.6 %all_to_all.16 = f32[16,1,1024]{2,1,0:T(1,128)S(1)} all-to-all(f32[16,1,1024]{2,1,0:T(1,128)S(1)} %broadcast_in_dim.18), channel_id=1, replica_groups=mesh['dp'=4,'row'=4,'col'=16] {'dp','row'}, dimensions={0} | all-to-all | bytes 131072 | tf_op jit(solution)/shard_map/all_to_all | solution.py:267
  120.9 14.7 %all_to_all.17 = f32[16,1,128]{2,1,0:T(1,128)S(1)} all-to-all(f32[16,1,128]{2,1,0:T(1,128)S(1)} %broadcast_in_dim.19), channel_id=1, replica_groups=mesh['dp'=4,'row'=4,'col'=16] {'col'}, dimensions={0} | all-to-all | bytes 16384 | tf_op jit(solution)/shard_map/all_to_all | solution.py:267
  135.7 3.2 %shard_map.82 = (f32[512,2048]{1,0:T(8,128)}, f32[1,1]{1,0:T(1,128)}) custom-call(f32[512,2048]{1,0:T(8,128)S(1)} %get-tuple-element.57.g_ref, f32[1,512]{1,0:T(1,128)S(1)} %get-tuple-element.61.row_ref, f32[1,2048]{1,0:T(1,128)S(1)} %get-tuple-element.62.col_ref, f32[16,128]{1,0:T(8,128)S(1)} %bitcast.36), custom_call_target="tpu_custom_call" | custom-call | flops 2097152 | bytes 8388608 | tf_op jit(solution)/shard_map/pallas_call | solution.py:219
  (76 shorter events, 20.3 us)
Async XLA Ops:
  0.6 9.3 %copy-start.16 = (bf16[128,512]{1,0:T(8,128)(2,1)S(1)}, bf16[128,512]{1,0:T(8,128)(2,1)}, u32[]{:S(2)}) copy-start(bf16[128,512]{1,0:T(8,128)(2,1)} %param.4) | copy-start | bytes 393220
  0.6 9.3 %collective-permute-start.3 = (bf16[128,512]{1,0:T(8,128)(2,1)}, bf16[128,512]{1,0:T(8,128)(2,1)S(1)}, u32[]{:S(2)}, u32[]{:S(2)}) collective-permute-start(bf16[128,512]{1,0:T(8,128)(2,1)} %param.4), channel_id=1, source_target_pairs={{0,32},{16,48},{32,0},{48,16},{1,33},{17,49},{33,1},{49,17},{2,34}... | collective-permute-start | bytes 393224 | tf_op jit(solution)/shard_map/ppermute | solution.py:258
  6.0 6.3 %collective-permute-start = (bf16[32,2048]{1,0:T(8,128)(2,1)S(1)}, bf16[32,2048]{1,0:T(8,128)(2,1)S(1)}, u32[]{:S(2)}, u32[]{:S(2)}) collective-permute-start(bf16[32,2048]{1,0:T(8,128)(2,1)S(1)} %get-tuple-element.71), channel_id=1, source_target_pairs={{0,64},{64,0},{128,192},{192,128},{1,65},{65,1},{129,193},{193,129... | collective-permute-start | bytes 393224 | tf_op jit(solution)/shard_map/ppermute | solution.py:250
  7.3 7.5 %collective-permute-start.1 = (bf16[32,2048]{1,0:T(8,128)(2,1)S(1)}, bf16[32,2048]{1,0:T(8,128)(2,1)S(1)}, u32[]{:S(2)}, u32[]{:S(2)}) collective-permute-start(bf16[32,2048]{1,0:T(8,128)(2,1)S(1)} %get-tuple-element.70), channel_id=1, source_target_pairs={{0,128},{64,192},{128,0},{192,64},{1,129},{65,193},{129,1},{193,65... | collective-permute-start | bytes 393224 | tf_op jit(solution)/shard_map/ppermute | solution.py:250
  9.7 7.9 %collective-permute-start.2 = (bf16[32,2048]{1,0:T(8,128)(2,1)S(1)}, bf16[32,2048]{1,0:T(8,128)(2,1)S(1)}, u32[]{:S(2)}, u32[]{:S(2)}) collective-permute-start(bf16[32,2048]{1,0:T(8,128)(2,1)S(1)} %get-tuple-element.69), channel_id=1, source_target_pairs={{0,192},{64,128},{128,64},{192,0},{1,193},{65,129},{129,65},{193,1... | collective-permute-start | bytes 393224 | tf_op jit(solution)/shard_map/ppermute | solution.py:250
  9.9 8.5 %collective-permute-start.4 = (bf16[256,512]{1,0:T(8,128)(2,1)S(1)}, bf16[256,512]{1,0:T(8,128)(2,1)S(1)}, u32[]{:S(2)}, u32[]{:S(2)}) collective-permute-start(bf16[256,512]{1,0:T(8,128)(2,1)S(1)} %pad_maximum_fusion.2), channel_id=1, source_target_pairs={{0,16},{16,0},{32,48},{48,32},{1,17},{17,1},{33,49},{49,33},{2,18}... | collective-permute-start | bytes 786440 | tf_op jit(solution)/shard_map/ppermute | solution.py:258
  18.5 12.6 %collective-permute-start.6 = (bf16[512,512]{1,0:T(8,128)(2,1)S(1)}, bf16[512,512]{1,0:T(8,128)(2,1)S(1)}, u32[]{:S(2)}, u32[]{:S(2)}) collective-permute-start(bf16[512,512]{1,0:T(8,128)(2,1)S(1)} %pad_maximum_fusion.1.refs_0_), channel_id=1, source_target_pairs={{0,64},{64,0},{128,192},{192,128},{1,65},{65,1},{129,193},{193,129... | collective-permute-start | bytes 1572872 | tf_op jit(solution)/shard_map/ppermute | solution.py:250
  18.8 20.0 %collective-permute-start.5 = (bf16[128,2048]{1,0:T(8,128)(2,1)}, bf16[128,2048]{1,0:T(8,128)(2,1)S(1)}, u32[]{:S(2)}, u32[]{:S(2)}) collective-permute-start(bf16[128,2048]{1,0:T(8,128)(2,1)} %pad_maximum_fusion), channel_id=1, source_target_pairs={{0,2},{1,3},{2,0},{3,1},{4,6},{5,7},{6,4},{7,5},{8,10},{9,11},{10,... | collective-permute-start | bytes 1572872 | tf_op jit(solution)/shard_map/ppermute | solution.py:262
  25.6 14.0 %collective-permute-start.10 = (bf16[128,2048]{1,0:T(8,128)(2,1)}, bf16[128,2048]{1,0:T(8,128)(2,1)}, u32[]{:S(2)}, u32[]{:S(2)}) collective-permute-start(bf16[128,2048]{1,0:T(8,128)(2,1)} %pad_maximum_fusion), channel_id=1, source_target_pairs={{0,12},{1,13},{2,14},{3,15},{4,0},{5,1},{6,2},{7,3},{8,4},{9,5},{1... | collective-permute-start | bytes 1572872 | tf_op jit(solution)/shard_map/ppermute | solution.py:254
  28.4 13.2 %collective-permute-start.8 = (bf16[128,2048]{1,0:T(8,128)(2,1)}, bf16[128,2048]{1,0:T(8,128)(2,1)}, u32[]{:S(2)}, u32[]{:S(2)}) collective-permute-start(bf16[128,2048]{1,0:T(8,128)(2,1)} %pad_maximum_fusion), channel_id=1, source_target_pairs={{0,4},{1,5},{2,6},{3,7},{4,8},{5,9},{6,10},{7,11},{8,12},{9,13},{1... | collective-permute-start | bytes 1572872 | tf_op jit(solution)/shard_map/ppermute | solution.py:254
  28.4 22.5 %collective-permute-start.9 = (bf16[128,2048]{1,0:T(8,128)(2,1)}, bf16[128,2048]{1,0:T(8,128)(2,1)}, u32[]{:S(2)}, u32[]{:S(2)}) collective-permute-start(bf16[128,2048]{1,0:T(8,128)(2,1)} %pad_maximum_fusion), channel_id=1, source_target_pairs={{0,8},{1,9},{2,10},{3,11},{4,12},{5,13},{6,14},{7,15},{8,0},{9,1},... | collective-permute-start | bytes 1572872 | tf_op jit(solution)/shard_map/ppermute | solution.py:254
  31.9 18.9 %collective-permute-start.7 = (bf16[512,512]{1,0:T(8,128)(2,1)S(1)}, bf16[512,512]{1,0:T(8,128)(2,1)}, u32[]{:S(2)}, u32[]{:S(2)}) collective-permute-start(bf16[512,512]{1,0:T(8,128)(2,1)S(1)} %pad_maximum_fusion.1.refs_0_), channel_id=1, source_target_pairs={{0,128},{64,192},{128,0},{192,64},{1,129},{65,193},{129,1},{193,65... | collective-permute-start | bytes 1572872 | tf_op jit(solution)/shard_map/ppermute | solution.py:250
  39.6 25.3 %copy-start.13 = (bf16[512,512]{1,0:T(8,128)(2,1)S(1)}, bf16[512,512]{1,0:T(8,128)(2,1)}, u32[]{:S(2)}) copy-start(bf16[512,512]{1,0:T(8,128)(2,1)} %copy-done.12) | copy-start | bytes 1572868
  50.8 17.8 %collective-permute-start.12 = (bf16[128,2048]{1,0:T(8,128)(2,1)}, bf16[128,2048]{1,0:T(8,128)(2,1)S(1)}, u32[]{:S(2)}, u32[]{:S(2)}) collective-permute-start(bf16[128,2048]{1,0:T(8,128)(2,1)} %copy-done.4), channel_id=1, source_target_pairs={{0,4},{1,5},{2,6},{3,7},{4,8},{5,9},{6,10},{7,11},{8,12},{9,13},{1... | collective-permute-start | bytes 1572872 | tf_op jit(solution)/shard_map/ppermute | solution.py:254
  50.8 20.9 %collective-permute-start.13 = (bf16[128,2048]{1,0:T(8,128)(2,1)}, bf16[128,2048]{1,0:T(8,128)(2,1)S(1)}, u32[]{:S(2)}, u32[]{:S(2)}) collective-permute-start(bf16[128,2048]{1,0:T(8,128)(2,1)} %copy-done.4), channel_id=1, source_target_pairs={{0,8},{1,9},{2,10},{3,11},{4,12},{5,13},{6,14},{7,15},{8,0},{9,1},... | collective-permute-start | bytes 1572872 | tf_op jit(solution)/shard_map/ppermute | solution.py:254
  52.4 24.6 %collective-permute-start.14 = (bf16[128,2048]{1,0:T(8,128)(2,1)}, bf16[128,2048]{1,0:T(8,128)(2,1)S(1)}, u32[]{:S(2)}, u32[]{:S(2)}) collective-permute-start(bf16[128,2048]{1,0:T(8,128)(2,1)} %copy-done.4), channel_id=1, source_target_pairs={{0,12},{1,13},{2,14},{3,15},{4,0},{5,1},{6,2},{7,3},{8,4},{9,5},{1... | collective-permute-start | bytes 1572872 | tf_op jit(solution)/shard_map/ppermute | solution.py:254
  54.5 10.4 %collective-permute-start.11 = (bf16[512,512]{1,0:T(8,128)(2,1)S(1)}, bf16[512,512]{1,0:T(8,128)(2,1)S(1)}, u32[]{:S(2)}, u32[]{:S(2)}) collective-permute-start(bf16[512,512]{1,0:T(8,128)(2,1)S(1)} %pad_maximum_fusion.1.refs_0_), channel_id=1, source_target_pairs={{0,192},{64,128},{128,64},{192,0},{1,193},{65,129},{129,65},{193,1... | collective-permute-start | bytes 1572872 | tf_op jit(solution)/shard_map/ppermute | solution.py:250
  59.6 21.0 %collective-permute-start.19 = (bf16[512,2048]{1,0:T(8,128)(2,1)S(1)}, bf16[512,2048]{1,0:T(8,128)(2,1)}, u32[]{:S(2)}, u32[]{:S(2)}) collective-permute-start(bf16[512,2048]{1,0:T(8,128)(2,1)S(1)} %constant_dynamic-update-slice_fusion.own_ref), channel_id=1, source_target_pairs={{0,1},{1,0},{2,3},{3,2},{4,5},{5,4},{6,7},{7,6},{8,9},{9,8},{10,11... | collective-permute-start | bytes 6291464 | tf_op jit(solution)/shard_map/ppermute | solution.py:246
  77.9 7.2 %collective-permute-start.15 = (bf16[128,2048]{1,0:T(8,128)(2,1)}, bf16[128,2048]{1,0:T(8,128)(2,1)S(1)}, u32[]{:S(2)}, u32[]{:S(2)}) collective-permute-start(bf16[128,2048]{1,0:T(8,128)(2,1)} %copy-done.4), channel_id=1, source_target_pairs={{0,1},{1,0},{2,3},{3,2},{4,5},{5,4},{6,7},{7,6},{8,9},{9,8},{10,11... | collective-permute-start | bytes 1572872 | tf_op jit(solution)/shard_map/ppermute | solution.py:246
  79.8 5.4 %collective-permute-start.16 = (bf16[128,2048]{1,0:T(8,128)(2,1)}, bf16[128,2048]{1,0:T(8,128)(2,1)S(1)}, u32[]{:S(2)}, u32[]{:S(2)}) collective-permute-start(bf16[128,2048]{1,0:T(8,128)(2,1)} %copy-done.6), channel_id=1, source_target_pairs={{0,1},{1,0},{2,3},{3,2},{4,5},{5,4},{6,7},{7,6},{8,9},{9,8},{10,11... | collective-permute-start | bytes 1572872 | tf_op jit(solution)/shard_map/ppermute | solution.py:246
  80.0 5.1 %collective-permute-start.17 = (bf16[128,2048]{1,0:T(8,128)(2,1)}, bf16[128,2048]{1,0:T(8,128)(2,1)S(1)}, u32[]{:S(2)}, u32[]{:S(2)}) collective-permute-start(bf16[128,2048]{1,0:T(8,128)(2,1)} %copy-done.8), channel_id=1, source_target_pairs={{0,1},{1,0},{2,3},{3,2},{4,5},{5,4},{6,7},{7,6},{8,9},{9,8},{10,11... | collective-permute-start | bytes 1572872 | tf_op jit(solution)/shard_map/ppermute | solution.py:246
  80.3 4.9 %collective-permute-start.18 = (bf16[128,2048]{1,0:T(8,128)(2,1)}, bf16[128,2048]{1,0:T(8,128)(2,1)S(1)}, u32[]{:S(2)}, u32[]{:S(2)}) collective-permute-start(bf16[128,2048]{1,0:T(8,128)(2,1)} %copy-done.10), channel_id=1, source_target_pairs={{0,1},{1,0},{2,3},{3,2},{4,5},{5,4},{6,7},{7,6},{8,9},{9,8},{10,11... | collective-permute-start | bytes 1572872 | tf_op jit(solution)/shard_map/ppermute | solution.py:246
  85.1 18.2 %copy-start.14 = (f32[2048]{0:T(1024)S(1)}, f32[2048]{0:T(1024)}, u32[]{:S(2)}) copy-start(f32[2048]{0:T(1024)} %param.7) | copy-start | bytes 24580
  103.3 17.0 %copy-start.15 = (f32[512]{0:T(512)S(1)}, f32[512]{0:T(512)}, u32[]{:S(2)}) copy-start(f32[512]{0:T(512)} %param.6) | copy-start | bytes 6148
  (13 other events, 57.4 us)
